TPU v7x, 32 devices: a whole 2x2x4 slice. The times are simulated.
32 devices in a mesh: pipe: 8 (over z, core), expert: 4 (over y, x).
Axes of the slice: x: 2, y: 2, z: 4, core: 2. Of those that a mesh axis runs over, the one named last changes fastest.
Arguments:
- fwd_in: bfloat16 [8, 256, 3584], P('pipe', 'expert'), may hold values from -6 to 6
- bwd_in: bfloat16 [8, 256, 3584], P('pipe', 'expert'), may hold values from -6 to 6
- bwd_grad_in: bfloat16 [8, 256, 3584], P('pipe', 'expert'), may hold values from -6 to 6
- w_gate: bfloat16 [8, 7168, 1024], P('pipe', 'expert'), may hold values from -0.09375 to 0.09375
- w_up: bfloat16 [8, 7168, 1024], P('pipe', 'expert'), may hold values from -0.09375 to 0.09375
- w_down: bfloat16 [8, 1024, 7168], P('pipe', None, 'expert'), may hold values from -0.1875 to 0.1875
- fwd_ids: int32 [8, 256, 1], P('pipe', 'expert'), may hold values from 0 to 1; in each aligned block of 64 rows (0 to 63, 64 to 127, ..., all dimensions but the last counted through in order) at most 40 rows name the same one
- fwd_gates: float32 [8, 256, 1], P('pipe', 'expert'), may hold values from 0.25 to 1
- bwd_ids: int32 [8, 256, 1], P('pipe', 'expert'), may hold values from 0 to 1; in each aligned block of 64 rows (0 to 63, 64 to 127, ..., all dimensions but the last counted through in order) at most 40 rows name the same one
- bwd_gates: float32 [8, 256, 1], P('pipe', 'expert'), may hold values from 0.25 to 1
Outputs:
- fwd_out: bfloat16 [8, 256, 3584], P('pipe', 'expert')
- bwd_out: bfloat16 [8, 256, 3584], P('pipe', 'expert')
Inputs may be any that keep to these rules, and one draw needn't show every extreme that they name: `fwd_ids`: each row names 1 different experts; among the 64 tokens of one device (aligned blocks of rows) no expert is named more than 40 times. `bwd_ids`: each row names 1 different experts; among the 64 tokens of one device (aligned blocks of rows) no expert is named more than 40 times.
All inputs are finite; a program needn't handle non-finite values.
Results may differ from a plain program's by a relative error of at most 0.01.
Values may be sent and summed in bfloat16 or wider, within the bound.
No kernel may reach another device: no remote copies, remote signals or barrier semaphores. Data moves between devices by JAX's collectives and lax.ppermute only.
A program may use at most 128 MiB of HBM per device.

v0:
```python
import jax
import jax.numpy as jnp
from jax import lax
from jax.sharding import PartitionSpec as P

EXPERTS = 2
TOP = 1
CAP = 40


def partner(value, axis, bit):
    mask = 2**bit
    pairs = [(source, source ^ mask) for source in range(lax.axis_size(axis))]
    return lax.ppermute(value, axis, pairs)


def shifted(x, axis, by):
    length = lax.axis_size(axis)
    pairs = [(i, i + by) for i in range(length) if 0 <= i + by < length]
    return lax.ppermute(x, axis, pairs)


def slot_positions(expert_ids):
    flat_ids = expert_ids.reshape(-1)
    onehot = (flat_ids[:, None] == jnp.arange(EXPERTS, dtype=jnp.int32)[None, :]).astype(jnp.int32)
    before = jnp.cumsum(onehot, axis=0) - onehot
    slot_pos = jnp.sum(before * onehot, axis=1)
    return flat_ids * CAP + slot_pos


def dispatch_rows(inputs, position, group):
    token_count, model_width = inputs.shape
    slots_total = EXPERTS * CAP
    match = (jnp.arange(slots_total, dtype=jnp.int32)[:, None] == position[None, :]).astype(
        jnp.int32
    )
    table = jnp.sum(match.reshape(slots_total, token_count, TOP), axis=2).astype(jnp.bfloat16)
    table = table.reshape(EXPERTS, CAP, token_count)
    pieces = inputs.reshape(token_count, group, model_width // group)
    filled = jnp.einsum("ect,tgk->egck", table, pieces, preferred_element_type=jnp.float32).astype(
        jnp.bfloat16
    )
    return filled.reshape(EXPERTS * group, CAP, model_width // group)


def combine_rows(residual, returned, expert_ids, position, gate_values, group):
    token_count, model_width = residual.shape
    blocks = returned.reshape(EXPERTS, group, CAP, model_width // group)
    flat_ids = expert_ids.reshape(-1)
    slot_pos = position - flat_ids * CAP
    picked = blocks[flat_ids, :, slot_pos, :].reshape(token_count, TOP, model_width)
    summed = jnp.sum(gate_values[:, :, None] * picked.astype(jnp.float32), axis=1)
    return (residual.astype(jnp.float32) + summed).astype(jnp.bfloat16)


def group_reduce(partial_value, bits, my_index):
    current = partial_value
    for bit in range(bits):
        half = current.shape[0] // 2
        my_bit = my_index >> bit & 1
        keep = jnp.where(my_bit == 0, current[:half], current[half:])
        given = jnp.where(my_bit == 0, current[half:], current[:half])
        got = partner(given.astype(jnp.bfloat16), "expert", bit)
        current = keep + got.astype(jnp.float32)
    return current


def group_collect(block, bits, my_index):
    current = block
    for bit in reversed(range(bits)):
        got = partner(current, "expert", bit)
        my_bit = my_index >> bit & 1
        current = jnp.where(
            my_bit == 0,
            jnp.concatenate([current, got], axis=0),
            jnp.concatenate([got, current], axis=0),
        )
    return current


def hidden_of(summed, hidden_units):
    return (jax.nn.silu(summed[:, :hidden_units]) * summed[:, hidden_units:]).astype(jnp.bfloat16)


def grads_of(summed, hidden_units):
    back_gate = summed[:, :hidden_units]
    back_up = summed[:, hidden_units : 2 * hidden_units]
    grad_hidden = summed[:, 2 * hidden_units :]
    sig_gate = jax.nn.sigmoid(back_gate)
    grad_gate = (grad_hidden * back_up * sig_gate * (1.0 + back_gate * (1.0 - sig_gate))).astype(
        jnp.bfloat16
    )
    grad_up = (grad_hidden * (back_gate * sig_gate)).astype(jnp.bfloat16)
    return jnp.concatenate([grad_gate, grad_up], axis=1)


def body(fwd_in, bwd_in, bwd_grad_in, w_gate, w_up, w_down, fwd_ids, fwd_gates, bwd_ids, bwd_gates):
    section_index = lax.axis_index("pipe")
    final_section = lax.axis_size("pipe") - 1
    group = lax.axis_size("expert") // EXPERTS
    bits = group.bit_length() - 1
    my_index = lax.axis_index("expert")
    arrived = shifted(fwd_in, "pipe", 1)
    section_x = jnp.where(section_index == 0, fwd_in, arrived)[0]
    came_back = shifted(bwd_grad_in, "pipe", -1)
    section_g = jnp.where(section_index == final_section, bwd_grad_in, came_back)[0]
    saved_x = bwd_in[0]
    in_mats = jnp.concatenate([w_gate[0], w_up[0]], axis=1)
    down_mats = w_down[0]
    hidden_units = down_mats.shape[0]
    fwd_position = slot_positions(fwd_ids[0])
    bwd_position = slot_positions(bwd_ids[0])
    send_fwd = dispatch_rows(section_x, fwd_position, group)
    send_saved = dispatch_rows(saved_x, bwd_position, group)
    send_grad = dispatch_rows(section_g, bwd_position, group)
    received = lax.all_to_all(send_fwd, "expert", split_axis=0, concat_axis=0, tiled=True)
    source_count, slot_count, width = received.shape
    rows = received.reshape(source_count * slot_count, width)
    partial_value = jnp.dot(rows, in_mats, preferred_element_type=jnp.float32)
    block = group_reduce(partial_value, bits, my_index)
    hidden = group_collect(hidden_of(block, hidden_units), bits, my_index)
    produced = jnp.dot(hidden, down_mats, preferred_element_type=jnp.float32).astype(jnp.bfloat16)
    back_fwd = lax.all_to_all(
        produced.reshape(source_count, slot_count, width),
        "expert",
        split_axis=0,
        concat_axis=0,
        tiled=True,
    )
    received = lax.all_to_all(send_saved, "expert", split_axis=0, concat_axis=0, tiled=True)
    source_count, slot_count, width = received.shape
    rows = received.reshape(source_count * slot_count, width)
    grad_rows = lax.all_to_all(
        send_grad, "expert", split_axis=0, concat_axis=0, tiled=True
    ).reshape(source_count * slot_count, width)
    partial_value = jnp.concatenate(
        [
            jnp.dot(rows, in_mats, preferred_element_type=jnp.float32),
            jnp.dot(grad_rows, down_mats.T, preferred_element_type=jnp.float32),
        ],
        axis=1,
    )
    block = group_reduce(partial_value, bits, my_index)
    joined = group_collect(grads_of(block, hidden_units), bits, my_index)
    produced = jnp.dot(joined, in_mats.T, preferred_element_type=jnp.float32).astype(jnp.bfloat16)
    back_bwd = lax.all_to_all(
        produced.reshape(source_count, slot_count, width),
        "expert",
        split_axis=0,
        concat_axis=0,
        tiled=True,
    )
    fwd_out = combine_rows(section_x, back_fwd, fwd_ids[0], fwd_position, fwd_gates[0], group)
    bwd_out = combine_rows(section_g, back_bwd, bwd_ids[0], bwd_position, bwd_gates[0], group)
    return (fwd_out[None], bwd_out[None])


def solution(mesh):
    return jax.shard_map(
        body,
        mesh=mesh,
        in_specs=(
            P("pipe", "expert", None),
            P("pipe", "expert", None),
            P("pipe", "expert", None),
            P("pipe", "expert", None),
            P("pipe", "expert", None),
            P("pipe", None, "expert"),
            P("pipe", "expert", None),
            P("pipe", "expert", None),
            P("pipe", "expert", None),
            P("pipe", "expert", None),
        ),
        out_specs=(P("pipe", "expert", None), P("pipe", "expert", None)),
        check_vma=False,
    )
```

profile of v0, /device:TPU:0, one launch (start us, length us, event | category | flops | bytes accessed | tf_op | source)
XLA Modules:
  0.0 100.8 jit_solution(10589013348806652622)
XLA Ops:
  3.0 1.1 %reshape_squeeze.25 = bf16[64,2,1792]{2,1,0:T(2,128)(2,1)S(1)} reshape(bf16[1,64,3584]{2,1,0:T(8,128)(2,1)} %param.11) | data formatting | bytes 917504 | tf_op jit(solution)/shard_map/reshape;squeeze | solution.py:39
  4.1 1.2 %convolution_convert_fusion.2 = bf16[2,40,2,1792]{3,1,2,0:T(8,128)(2,1)} fusion(bf16[64,2,1792]{2,1,0:T(2,128)(2,1)S(1)} %reshape_squeeze.25, s32[64]{0:T(128)S(1)} %multiply_add_fusion.1, s32[2,40]{1,0:T(2,128)S(1)} %multiply_add_fusion), kind=kOutput, calls=%fused_computation.10 | convolution fusion | flops 37002240 | bytes 1032768 | tf_op jit(solution)/shard_map/ect,tgk->egck/dot_general | solution.py:40
  5.3 5.2 %all-to-all-start.2 = ((bf16[4,40,1792]{2,1,0:T(8,128)(2,1)}), bf16[4,40,1792]{2,1,0:T(8,128)(2,1)S(1)}, u32[]{:S(2)}, u32[]{:S(2)}) async-start(bf16[4,40,1792]{2,1,0:T(8,128)(2,1)} %bitcast.21), calls=%async_computation.2 | async-start | bytes 1146880 | tf_op jit(solution)/shard_map/all_to_all | solution.py:130
  10.4 1.3 %collective-permute-start.3 = (bf16[1,64,3584]{2,1,0:T(8,128)(2,1)}, bf16[1,64,3584]{2,1,0:T(8,128)(2,1)}, u32[]{:S(2)}, u32[]{:S(2)}) collective-permute-start(bf16[1,64,3584]{2,1,0:T(8,128)(2,1)} %param.12), channel_id=1, source_target_pairs={{4,0},{8,4},{12,8},{16,12},{20,16},{24,20},{28,24},{5,1},{9,5},{13... | collective-permute-start | bytes 1376264 | tf_op jit(solution)/shard_map/ppermute | solution.py:20
  11.7 3.1 %collective-permute-start = (bf16[1,64,3584]{2,1,0:T(8,128)(2,1)}, bf16[1,64,3584]{2,1,0:T(8,128)(2,1)S(1)}, u32[]{:S(2)}, u32[]{:S(2)}) collective-permute-start(bf16[1,64,3584]{2,1,0:T(8,128)(2,1)} %param.10), channel_id=1, source_target_pairs={{0,4},{4,8},{8,12},{12,16},{16,20},{20,24},{24,28},{1,5},{5,9},{9,... | collective-permute-start | bytes 1376264 | tf_op jit(solution)/shard_map/ppermute | solution.py:20
  19.0 4.6 %fusion.9 = f32[160,2048]{1,0:T(8,128)S(1)} fusion(bf16[160,1792]{1,0:T(8,128)(2,1)S(1)} %bitcast.73, bf16[1792,1024]{1,0:T(8,128)(2,1)} %bitcast.81, bf16[1792,1024]{1,0:T(8,128)(2,1)} %bitcast.84), kind=kOutput, calls=%fused_computation.14 | convolution fusion | flops 1189085184 | bytes 9224192 | tf_op jit(solution)/shard_map/dot_general | solution.py:138
  25.0 3.7 %all-to-all-start = ((bf16[4,40,1792]{2,1,0:T(8,128)(2,1)}), bf16[4,40,1792]{2,1,0:T(8,128)(2,1)S(1)}, u32[]{:S(2)}, u32[]{:S(2)}) async-start(bf16[4,40,1792]{2,1,0:T(8,128)(2,1)} %bitcast.5), calls=%async_computation | async-start | bytes 1146880 | tf_op jit(solution)/shard_map/all_to_all | solution.py:116
  31.1 7.5 %all-to-all-done = bf16[4,40,1792]{2,1,0:T(8,128)(2,1)S(1)} async-done(((bf16[4,40,1792]{2,1,0:T(8,128)(2,1)}), bf16[4,40,1792]{2,1,0:T(8,128)(2,1)S(1)}, u32[]{:S(2)}, u32[]{:S(2)}) %all-to-all-start) | async-done | bytes 573472 | tf_op jit(solution)/shard_map/all_to_all | solution.py:116
  38.6 4.1 %all-to-all-start.3 = ((bf16[4,40,1792]{2,1,0:T(8,128)(2,1)}), bf16[4,40,1792]{2,1,0:T(8,128)(2,1)}, u32[]{:S(2)}, u32[]{:S(2)}) async-start(bf16[4,40,1792]{2,1,0:T(8,128)(2,1)} %bitcast.25), calls=%async_computation.3 | async-start | bytes 1146880 | tf_op jit(solution)/shard_map/all_to_all | solution.py:133
  42.8 4.7 %fusion.10 = f32[160,2048]{1,0:T(8,128)S(1)} fusion(bf16[160,1792]{1,0:T(8,128)(2,1)} %bitcast.74, bf16[1792,1024]{1,0:T(8,128)(2,1)} %bitcast.82, bf16[1792,1024]{1,0:T(8,128)(2,1)} %bitcast.85), kind=kOutput, calls=%fused_computation.15 | convolution fusion | flops 1189085184 | bytes 9224192 | tf_op jit(solution)/shard_map/dot_general | solution.py:119
  48.3 2.0 %collective-permute-start.1 = (bf16[80,2048]{1,0:T(8,128)(2,1)}, bf16[80,2048]{1,0:T(8,128)(2,1)}, u32[]{:S(2)}, u32[]{:S(2)}) collective-permute-start(bf16[80,2048]{1,0:T(8,128)(2,1)} %select_convert_fusion.1), channel_id=1, source_target_pairs={{0,1},{1,0},{2,3},{3,2},{4,5},{5,4},{6,7},{7,6},{8,9},{9,8},{10,11... | collective-permute-start | bytes 983048 | tf_op jit(solution)/shard_map/ppermute | solution.py:14
  50.2 2.2 %all-to-all-done.3 = bf16[4,40,1792]{2,1,0:T(8,128)(2,1)} async-done(((bf16[4,40,1792]{2,1,0:T(8,128)(2,1)}), bf16[4,40,1792]{2,1,0:T(8,128)(2,1)}, u32[]{:S(2)}, u32[]{:S(2)}) %all-to-all-start.3) | async-done | bytes 573472 | tf_op jit(solution)/shard_map/all_to_all | solution.py:133
  52.4 3.6 %fusion = f32[160,1024]{1,0:T(8,128)S(1)} fusion(bf16[160,1792]{1,0:T(8,128)(2,1)} %bitcast.26, bf16[1,1024,1792]{2,1,0:T(8,128)(2,1)} %param.15), kind=kOutput, calls=%fused_computation.3 | convolution fusion | flops 587202560 | bytes 4898816 | tf_op jit(solution)/shard_map/dot_general | solution.py:139
  57.0 2.4 %collective-permute-done.1 = bf16[80,2048]{1,0:T(8,128)(2,1)} collective-permute-done((bf16[80,2048]{1,0:T(8,128)(2,1)}, bf16[80,2048]{1,0:T(8,128)(2,1)}, u32[]{:S(2)}, u32[]{:S(2)}) %collective-permute-start.1) | collective-permute-done | bytes 327712 | tf_op jit(solution)/shard_map/ppermute | solution.py:14
  60.6 1.5 %collective-permute-start.2 = (bf16[80,1024]{1,0:T(8,128)(2,1)S(1)}, bf16[80,1024]{1,0:T(8,128)(2,1)S(1)}, u32[]{:S(2)}, u32[]{:S(2)}) collective-permute-start(bf16[80,1024]{1,0:T(8,128)(2,1)S(1)} %fusion.29), channel_id=1, source_target_pairs={{0,1},{1,0},{2,3},{3,2},{4,5},{5,4},{6,7},{7,6},{8,9},{9,8},{10,11... | collective-permute-start | bytes 491528 | tf_op jit(solution)/shard_map/ppermute | solution.py:14
  62.1 8.2 %collective-permute-done.4 = bf16[80,3072]{1,0:T(8,128)(2,1)S(1)} collective-permute-done((bf16[80,3072]{1,0:T(8,128)(2,1)S(1)}, bf16[80,3072]{1,0:T(8,128)(2,1)S(1)}, u32[]{:S(2)}, u32[]{:S(2)}) %collective-permute-start.4) | collective-permute-done | bytes 491552 | tf_op jit(solution)/shard_map/ppermute | solution.py:14
  71.7 2.1 %collective-permute-done.2 = bf16[80,1024]{1,0:T(8,128)(2,1)S(1)} collective-permute-done((bf16[80,1024]{1,0:T(8,128)(2,1)S(1)}, bf16[80,1024]{1,0:T(8,128)(2,1)S(1)}, u32[]{:S(2)}, u32[]{:S(2)}) %collective-permute-start.2) | collective-permute-done | bytes 163872 | tf_op jit(solution)/shard_map/ppermute | solution.py:14
  73.8 1.6 %fusion.4 = bf16[160,1792]{1,0:T(8,128)(2,1)} fusion(bf16[1,1024,1792]{2,1,0:T(8,128)(2,1)S(1)} %copy-done, bf16[80,1024]{1,0:T(8,128)(2,1)S(1)} %collective-permute-done.2, bf16[80,1024]{1,0:T(8,128)(2,1)S(1)} %fusion.29, pred[]{:T(512)S(6)} %eq.112), kind=kOutput, calls=%fused_computation.7 | convolution fusion | flops 588963840 | bytes 4571137 | tf_op jit(solution)/shard_map/dot_general | solution.py:122
  75.4 3.5 %all-to-all-start.1 = ((bf16[4,40,1792]{2,1,0:T(8,128)(2,1)}), bf16[4,40,1792]{2,1,0:T(8,128)(2,1)S(1)}, u32[]{:S(2)}, u32[]{:S(2)}) async-start(bf16[4,40,1792]{2,1,0:T(8,128)(2,1)} %bitcast.10), calls=%async_computation.1 | async-start | bytes 1146880 | tf_op jit(solution)/shard_map/all_to_all | solution.py:123
  79.8 6.6 %convolution_convert_fusion = bf16[160,1792]{1,0:T(8,128)(2,1)} fusion(bf16[1792,1024]{1,0:T(8,128)(2,1)} %bitcast.83, bf16[1792,1024]{1,0:T(8,128)(2,1)} %bitcast.86, bf16[80,2048]{1,0:T(8,128)(2,1)S(1)} %collective-permute-done.5, bf16[80,1024]{1,0:T(8,128)(2,1)S(1)} %get-tuple-element.3, bf16[80,1024]{1,0:T(8,128)(2,1)S(1)} %get-tuple-element.2, pred[]{:T(512)S(6)} %eq.112), kind=kOutput, calls=%fused_computation.8 | convolution fusion | flops 1193631744 | bytes 8568833 | tf_op jit(solution)/shard_map/dot_general | solution.py:145
  86.4 3.8 %all-to-all-start.4 = ((bf16[4,40,1792]{2,1,0:T(8,128)(2,1)}), bf16[4,40,1792]{2,1,0:T(8,128)(2,1)S(1)}, u32[]{:S(2)}, u32[]{:S(2)}) async-start(bf16[4,40,1792]{2,1,0:T(8,128)(2,1)} %bitcast.27), calls=%async_computation.4 | async-start | bytes 1146880 | tf_op jit(solution)/shard_map/all_to_all | solution.py:146
  90.7 1.5 %gather_fusion = bf16[64,2,1792]{2,1,0:T(2,128)(2,1)S(1)} fusion(bf16[2,2,40,1792]{3,1,2,0:T(2,128)(2,1)S(1)} %copy.22, s32[64]{0:T(128)S(1)} %fusion.61), kind=kCustom, calls=%fused_computation | custom fusion | bytes 918016 | tf_op jit(solution)/shard_map/gather | solution.py:51
  93.5 4.1 %all-to-all-done.4 = bf16[4,40,1792]{2,1,0:T(8,128)(2,1)S(1)} async-done(((bf16[4,40,1792]{2,1,0:T(8,128)(2,1)}), bf16[4,40,1792]{2,1,0:T(8,128)(2,1)S(1)}, u32[]{:S(2)}, u32[]{:S(2)}) %all-to-all-start.4) | async-done | bytes 573472 | tf_op jit(solution)/shard_map/all_to_all | solution.py:146
  98.0 1.5 %gather_fusion.1 = bf16[64,2,1792]{2,1,0:T(2,128)(2,1)S(1)} fusion(bf16[2,2,40,1792]{3,1,2,0:T(2,128)(2,1)S(1)} %copy.26, s32[64]{0:T(128)S(1)} %fusion.60), kind=kCustom, calls=%fused_computation.1 | custom fusion | bytes 918016 | tf_op jit(solution)/shard_map/gather | solution.py:51
  (51 shorter events, 18.9 us)
Async XLA Ops:
  5.3 13.7 %all-to-all-start.2 = ((bf16[4,40,1792]{2,1,0:T(8,128)(2,1)}), bf16[4,40,1792]{2,1,0:T(8,128)(2,1)S(1)}, u32[]{:S(2)}, u32[]{:S(2)}) async-start(bf16[4,40,1792]{2,1,0:T(8,128)(2,1)} %bitcast.21), calls=%async_computation.2 | async-start | bytes 1146880 | tf_op jit(solution)/shard_map/all_to_all | solution.py:130
  10.4 18.3 %collective-permute-start.3 = (bf16[1,64,3584]{2,1,0:T(8,128)(2,1)}, bf16[1,64,3584]{2,1,0:T(8,128)(2,1)}, u32[]{:S(2)}, u32[]{:S(2)}) collective-permute-start(bf16[1,64,3584]{2,1,0:T(8,128)(2,1)} %param.12), channel_id=1, source_target_pairs={{4,0},{8,4},{12,8},{16,12},{20,16},{24,20},{28,24},{5,1},{9,5},{13... | collective-permute-start | bytes 1376264 | tf_op jit(solution)/shard_map/ppermute | solution.py:20
  11.7 11.9 %collective-permute-start = (bf16[1,64,3584]{2,1,0:T(8,128)(2,1)}, bf16[1,64,3584]{2,1,0:T(8,128)(2,1)S(1)}, u32[]{:S(2)}, u32[]{:S(2)}) collective-permute-start(bf16[1,64,3584]{2,1,0:T(8,128)(2,1)} %param.10), channel_id=1, source_target_pairs={{0,4},{4,8},{8,12},{12,16},{16,20},{20,24},{24,28},{1,5},{5,9},{9,... | collective-permute-start | bytes 1376264 | tf_op jit(solution)/shard_map/ppermute | solution.py:20
  19.0 4.7 %copy-start.2 = (bf16[1,64,3584]{2,1,0:T(8,128)(2,1)S(1)}, bf16[1,64,3584]{2,1,0:T(8,128)(2,1)}, u32[]{:S(2)}) copy-start(bf16[1,64,3584]{2,1,0:T(8,128)(2,1)} %param.10) | copy-start | bytes 1376260
  23.6 5.1 %copy-start.3 = (bf16[1,64,3584]{2,1,0:T(8,128)(2,1)S(1)}, bf16[1,64,3584]{2,1,0:T(8,128)(2,1)}, u32[]{:S(2)}) copy-start(bf16[1,64,3584]{2,1,0:T(8,128)(2,1)} %param.12) | copy-start | bytes 1376260
  25.0 13.6 %all-to-all-start = ((bf16[4,40,1792]{2,1,0:T(8,128)(2,1)}), bf16[4,40,1792]{2,1,0:T(8,128)(2,1)S(1)}, u32[]{:S(2)}, u32[]{:S(2)}) async-start(bf16[4,40,1792]{2,1,0:T(8,128)(2,1)} %bitcast.5), calls=%async_computation | async-start | bytes 1146880 | tf_op jit(solution)/shard_map/all_to_all | solution.py:116
  38.6 4.2 %copy-start.1 = (bf16[4,40,1792]{2,1,0:T(8,128)(2,1)}, bf16[4,40,1792]{2,1,0:T(8,128)(2,1)S(1)}, u32[]{:S(2)}) copy-start(bf16[4,40,1792]{2,1,0:T(8,128)(2,1)S(1)} %all-to-all-done) | copy-start | bytes 1720324
  38.6 13.8 %all-to-all-start.3 = ((bf16[4,40,1792]{2,1,0:T(8,128)(2,1)}), bf16[4,40,1792]{2,1,0:T(8,128)(2,1)}, u32[]{:S(2)}, u32[]{:S(2)}) async-start(bf16[4,40,1792]{2,1,0:T(8,128)(2,1)} %bitcast.25), calls=%async_computation.3 | async-start | bytes 1146880 | tf_op jit(solution)/shard_map/all_to_all | solution.py:133
  48.3 11.2 %collective-permute-start.1 = (bf16[80,2048]{1,0:T(8,128)(2,1)}, bf16[80,2048]{1,0:T(8,128)(2,1)}, u32[]{:S(2)}, u32[]{:S(2)}) collective-permute-start(bf16[80,2048]{1,0:T(8,128)(2,1)} %select_convert_fusion.1), channel_id=1, source_target_pairs={{0,1},{1,0},{2,3},{3,2},{4,5},{5,4},{6,7},{7,6},{8,9},{9,8},{10,11... | collective-permute-start | bytes 983048 | tf_op jit(solution)/shard_map/ppermute | solution.py:14
  56.1 14.2 %collective-permute-start.4 = (bf16[80,3072]{1,0:T(8,128)(2,1)S(1)}, bf16[80,3072]{1,0:T(8,128)(2,1)S(1)}, u32[]{:S(2)}, u32[]{:S(2)}) collective-permute-start(bf16[80,3072]{1,0:T(8,128)(2,1)S(1)} %select_convert_fusion), channel_id=1, source_target_pairs={{0,1},{1,0},{2,3},{3,2},{4,5},{5,4},{6,7},{7,6},{8,9},{9,8},{10,11... | collective-permute-start | bytes 1474568 | tf_op jit(solution)/shard_map/ppermute | solution.py:14
  60.5 13.3 %copy-start = (bf16[1,1024,1792]{2,1,0:T(8,128)(2,1)S(1)}, bf16[1,1024,1792]{2,1,0:T(8,128)(2,1)}, u32[]{:S(2)}) copy-start(bf16[1,1024,1792]{2,1,0:T(8,128)(2,1)} %param.15) | copy-start | bytes 11010052
  60.6 13.2 %collective-permute-start.2 = (bf16[80,1024]{1,0:T(8,128)(2,1)S(1)}, bf16[80,1024]{1,0:T(8,128)(2,1)S(1)}, u32[]{:S(2)}, u32[]{:S(2)}) collective-permute-start(bf16[80,1024]{1,0:T(8,128)(2,1)S(1)} %fusion.29), channel_id=1, source_target_pairs={{0,1},{1,0},{2,3},{3,2},{4,5},{5,4},{6,7},{7,6},{8,9},{9,8},{10,11... | collective-permute-start | bytes 491528 | tf_op jit(solution)/shard_map/ppermute | solution.py:14
  70.7 9.2 %collective-permute-start.5 = (bf16[80,2048]{1,0:T(8,128)(2,1)S(1)}, bf16[80,2048]{1,0:T(8,128)(2,1)S(1)}, u32[]{:S(2)}, u32[]{:S(2)}) collective-permute-start(bf16[80,2048]{1,0:T(8,128)(2,1)S(1)} %pad_maximum_fusion.5), channel_id=1, source_target_pairs={{0,1},{1,0},{2,3},{3,2},{4,5},{5,4},{6,7},{7,6},{8,9},{9,8},{10,11... | collective-permute-start | bytes 983048 | tf_op jit(solution)/shard_map/ppermute | solution.py:14
  75.4 11.0 %all-to-all-start.1 = ((bf16[4,40,1792]{2,1,0:T(8,128)(2,1)}), bf16[4,40,1792]{2,1,0:T(8,128)(2,1)S(1)}, u32[]{:S(2)}, u32[]{:S(2)}) async-start(bf16[4,40,1792]{2,1,0:T(8,128)(2,1)} %bitcast.10), calls=%async_computation.1 | async-start | bytes 1146880 | tf_op jit(solution)/shard_map/all_to_all | solution.py:123
  86.4 6.1 %copy-start.4 = (f32[1,64,1]{1,2,0:T(1,128)S(1)}, f32[1,64,1]{1,2,0:T(1,128)}, u32[]{:S(2)}) copy-start(f32[1,64,1]{1,2,0:T(1,128)} %param.17) | copy-start | bytes 772
  86.4 11.2 %all-to-all-start.4 = ((bf16[4,40,1792]{2,1,0:T(8,128)(2,1)}), bf16[4,40,1792]{2,1,0:T(8,128)(2,1)S(1)}, u32[]{:S(2)}, u32[]{:S(2)}) async-start(bf16[4,40,1792]{2,1,0:T(8,128)(2,1)} %bitcast.27), calls=%async_computation.4 | async-start | bytes 1146880 | tf_op jit(solution)/shard_map/all_to_all | solution.py:146
  90.7 9.1 %copy-start.5 = (f32[1,64,1]{1,2,0:T(1,128)S(1)}, f32[1,64,1]{1,2,0:T(1,128)}, u32[]{:S(2)}) copy-start(f32[1,64,1]{1,2,0:T(1,128)} %param.19) | copy-start | bytes 772
where the time goes:
time: 101 us
  starting transfers between devices  30.1 us (30%)
  waiting for transfers between devices  28 us (28%)
  matrix products  22.9 us (23%)
  other arithmetic  11.4 us (11%)
  local copies, waits for them, and re-layouts  7.52 us (7%)
    ppermute x4, waiting for transfers between devices, partner(): return lax.ppermute(value, axis, pairs)  13.7 us
    all_to_all x1, waiting for transfers between devices, body(): lax.all_to_all(send_fwd, 'expert', split_axis=0, concat_axis=0, tiled=True)  7.49 us
    all_to_all x2, starting transfers between devices, body(): lax.all_to_all(produced.reshape(source_count, slot_count, width), 'expert...  7.31 us
    dot_general x1, matrix products, body(): jnp.dot(joined, in_mats.T, preferred_element_type=jnp.float32)  6.57 us
    ppermute x4, starting transfers between devices, partner(): return lax.ppermute(value, axis, pairs)  5.46 us
    all_to_all x1, starting transfers between devices, body(): lax.all_to_all(send_saved, 'expert', split_axis=0, concat_axis=0, tiled=T...  5.16 us
    dot_general x1, matrix products, body(): partial_value = jnp.dot(rows, in_mats, preferred_element_type=jnp.float32)  4.7 us
    dot_general x1, matrix products, body(): jnp.dot(rows, in_mats, preferred_element_type=jnp.float32)  4.63 us
  transfers between devices with their start and end apart: 11, of which 8 were waited for; matrix products, arithmetic and copies ran while one was open for 34% of the time, Pallas kernels for 0%

commit v1 on v0

v1 whole, which is shorter than its diff:
```python
import functools

import jax
import jax.numpy as jnp
from jax import lax
from jax.experimental import pallas as pl
from jax.experimental.pallas import tpu as pltpu
from jax.sharding import PartitionSpec as P

EXPERTS = 2
CAP = 40
BF16 = jnp.bfloat16
F32 = jnp.float32
VMEM_LIMIT = 40 * 1024 * 1024


def kernel_call(kernel, out_shape, grid, in_specs, out_specs, flops, moved):
    return pl.pallas_call(
        kernel,
        out_shape=out_shape,
        grid=grid,
        in_specs=in_specs,
        out_specs=out_specs,
        compiler_params=pltpu.CompilerParams(vmem_limit_bytes=VMEM_LIMIT),
        cost_estimate=pl.CostEstimate(flops=flops, bytes_accessed=moved, transcendentals=0),
    )


def full(shape):
    return pl.BlockSpec(shape, lambda j: (0,) * len(shape))


def tables(ids_row, expert, dtype):
    tokens = ids_row.shape[1]
    row = lax.broadcasted_iota(jnp.int32, (tokens, tokens), 0)
    col = lax.broadcasted_iota(jnp.int32, (tokens, tokens), 1)
    earlier = (row < col).astype(BF16)
    mine = jnp.broadcast_to(ids_row == expert, (8, tokens))
    before = jnp.dot(mine.astype(BF16), earlier, preferred_element_type=F32)[:1].astype(jnp.int32)
    place = lax.broadcasted_iota(jnp.int32, (1, tokens), 1)
    slot = lax.broadcasted_iota(jnp.int32, (CAP, tokens), 0)
    same = ids_row == expert
    table_same = ((slot == before) & same).astype(dtype)
    table_other = ((slot == place - before) & jnp.logical_not(same)).astype(dtype)
    return table_same, table_other


def slot_kernel(group, *refs):
    ids_ref, *rest = refs
    xs, (same_ref, other_ref) = rest[:group], rest[group:]
    expert = lax.axis_index("expert") // group
    same_rows, other_rows = [], []
    for r in range(group):
        t_same, t_other = tables(ids_ref[r : r + 1, :], expert, BF16)
        both = jnp.concatenate([t_same, t_other], axis=0)
        rows = jnp.dot(both, xs[r][...], preferred_element_type=F32)
        same_rows.append(rows[:CAP])
        other_rows.append(rows[CAP:])
    same_ref[...] = jnp.concatenate(same_rows, axis=0).astype(BF16)
    other_ref[...] = jnp.concatenate(other_rows, axis=0).astype(BF16)


def slot_rows(ids, xs):
    group = len(xs)
    tokens, width = xs[0].shape
    out = jax.ShapeDtypeStruct((group * CAP, width), BF16)
    return kernel_call(
        functools.partial(slot_kernel, group),
        (out, out),
        (1,),
        [full(ids.shape)] + [full(x.shape) for x in xs],
        (full(out.shape), full(out.shape)),
        2 * group * 2 * CAP * tokens * width,
        2 * group * (tokens + 2 * CAP) * width,
    )(ids, *xs)


def split_rows(acc, parts, group, outs, put):
    for r in range(group):
        rows = [acc[(p * group + r) * CAP : (p * group + r + 1) * CAP] for p in range(parts)]
        put(outs[r], jnp.concatenate(rows, axis=0).astype(BF16))


def dot_nt(a, b):
    return lax.dot_general(a, b, (((1,), (1,)), ((), ())), preferred_element_type=F32)


def in_kernel(parts, group, *refs):
    rows = jnp.concatenate([refs[p][...] for p in range(parts)], axis=0)
    gate, up, *outs = refs[parts:]
    for k, mat in enumerate((gate, up)):

        def put(ref, value, k=k):
            ref[k] = value

        split_rows(
            jnp.dot(rows, mat[...], preferred_element_type=F32), parts, group, outs, put
        )


def in_partials(parts, gate, up, group):
    width, hidden = gate.shape
    tile = 256
    rows = len(parts) * CAP
    out = jax.ShapeDtypeStruct((2, rows, hidden), BF16)
    column = pl.BlockSpec((width, tile), lambda j: (0, j))
    return kernel_call(
        functools.partial(in_kernel, len(parts), group),
        (out,) * group,
        (hidden // tile,),
        [full(p.shape) for p in parts] + [column, column],
        (pl.BlockSpec((2, rows, tile), lambda j: (0, 0, j)),) * group,
        2 * rows * group * width * 2 * hidden,
        2 * 2 * width * hidden,
    )(*parts, gate, up)


def grad_kernel(parts, group, *refs):
    rows = jnp.concatenate([refs[p][...] for p in range(parts)], axis=0)
    down, *outs = refs[parts:]

    def put(ref, value):
        ref[...] = value

    split_rows(dot_nt(rows, down[...]), parts, group, outs, put)


def grad_partials(parts, down, group):
    hidden, width = down.shape
    tile = 256
    rows = len(parts) * CAP
    out = jax.ShapeDtypeStruct((rows, hidden), BF16)
    return kernel_call(
        functools.partial(grad_kernel, len(parts), group),
        (out,) * group,
        (hidden // tile,),
        [full(p.shape) for p in parts] + [pl.BlockSpec((tile, width), lambda j: (j, 0))],
        (pl.BlockSpec((rows, tile), lambda j: (0, j)),) * group,
        2 * rows * group * width * hidden,
        2 * width * hidden,
    )(*parts, down)


def width_tile(width):
    return 256 if width % 256 == 0 else width


def down_kernel(group, *refs):
    hs, (down, *outs) = refs[:group], refs[group:]
    rows = jnp.concatenate([h[...] for h in hs], axis=0)
    acc = jnp.dot(rows, down[...], preferred_element_type=F32).astype(BF16)
    for p in range(2):
        for r in range(group):
            at = (r * 2 + p) * CAP
            outs[p * group + r][...] = acc[at : at + CAP]


def down_rows(hs, down):
    group = len(hs)
    hidden, width = down.shape
    tile = width_tile(width)
    out = jax.ShapeDtypeStruct((CAP, width), BF16)
    return kernel_call(
        functools.partial(down_kernel, group),
        (out,) * (2 * group),
        (width // tile,),
        [full(h.shape) for h in hs] + [pl.BlockSpec((hidden, tile), lambda j: (0, j))],
        (pl.BlockSpec((CAP, tile), lambda j: (0, j)),) * (2 * group),
        2 * group * 2 * CAP * hidden * width,
        2 * hidden * width,
    )(*hs, down)


def back_kernel(group, *refs):
    gs, (gate, up, *outs) = refs[:group], refs[group:]
    grads_gate = jnp.concatenate([g[0] for g in gs], axis=0)
    grads_up = jnp.concatenate([g[1] for g in gs], axis=0)
    acc = (dot_nt(grads_gate, gate[...]) + dot_nt(grads_up, up[...])).astype(BF16)
    for p in range(2):
        for r in range(group):
            at = (r * 2 + p) * CAP
            outs[p * group + r][...] = acc[at : at + CAP]


def back_rows(gs, gate, up):
    group = len(gs)
    width, hidden = gate.shape
    tile = width_tile(width)
    out = jax.ShapeDtypeStruct((CAP, width), BF16)
    row = pl.BlockSpec((tile, hidden), lambda j: (j, 0))
    return kernel_call(
        functools.partial(back_kernel, group),
        (out,) * (2 * group),
        (width // tile,),
        [full(g.shape) for g in gs] + [row, row],
        (pl.BlockSpec((CAP, tile), lambda j: (0, j)),) * (2 * group),
        2 * group * 2 * CAP * hidden * 2 * width,
        2 * 2 * hidden * width,
    )(*gs, gate, up)


def combine_kernel(group, *refs):
    ids, gates, base, *rest = refs
    same, other, out = rest[:group], rest[group : 2 * group], rest[2 * group]
    index = lax.axis_index("expert")
    t_same, t_other = tables(ids[...], index // group, BF16)
    tokens = base.shape[0]
    width = same[0].shape[1]
    row = lax.broadcasted_iota(jnp.int32, (tokens, tokens), 0)
    col = lax.broadcasted_iota(jnp.int32, (tokens, tokens), 1)
    weight = jnp.sum(jnp.where(row == col, gates[...], 0.0), axis=1, keepdims=True)
    contract = (((0,), (0,)), ((), ()))
    table = jnp.concatenate([t_same, t_other], axis=0)
    for r in range(group):
        blocks = jnp.concatenate([same[r][...], other[r][...]], axis=0)
        picked = lax.dot_general(table, blocks, contract, preferred_element_type=F32)
        for own in range(group):

            @pl.when(lax.rem(index, group) == own)
            def _(own=own, r=r, picked=picked):
                at = (own ^ r) * width
                out[:, at : at + width] = (
                    base[:, at : at + width].astype(F32) + weight * picked
                ).astype(BF16)


def combine(ids, gates, base, same, other):
    group = len(same)
    return kernel_call(
        functools.partial(combine_kernel, group),
        jax.ShapeDtypeStruct(base.shape, BF16),
        (1,),
        [full(v.shape) for v in (ids, gates, base, *same, *other)],
        full(base.shape),
        4 * CAP * base.shape[0] * base.shape[1],
        8 * base.shape[0] * base.shape[1],
    )(ids, gates, base, *same, *other)


def body(fwd_in, bwd_in, bwd_grad_in, w_gate, w_up, w_down, fwd_ids, fwd_gates, bwd_ids, bwd_gates):
    sections = lax.axis_size("pipe")
    devices = lax.axis_size("expert")
    group = devices // EXPERTS
    partners = range(1, group)
    section = lax.axis_index("pipe")
    slice_index = lax.rem(lax.axis_index("expert"), group)
    tokens, model = fwd_in.shape[1:]
    width = model // group
    gate, up, down = w_gate[0], w_up[0], w_down[0]

    def to_partner(value, mask):
        return lax.ppermute(value, "expert", [(i, i ^ mask) for i in range(devices)])

    def along(value, pairs):
        flat = [(a * devices + i, b * devices + j) for (a, i), (b, j) in pairs]
        return lax.ppermute(value, ("pipe", "expert"), flat)

    def piece(value, r):
        return lax.dynamic_slice_in_dim(value, (slice_index ^ r) * width, width, axis=1)

    first, last = 0, sections - 1
    fwd_in, bwd_in, bwd_grad_in = fwd_in[0], bwd_in[0], bwd_grad_in[0]
    own_ids = jnp.concatenate([fwd_ids.reshape(1, tokens), bwd_ids.reshape(1, tokens)], axis=0)
    all_ids = [own_ids] + [to_partner(own_ids, r) for r in partners]
    ids_fwd = jnp.concatenate([v[:1] for v in all_ids], axis=0)
    ids_bwd = jnp.concatenate([v[1:] for v in all_ids], axis=0)

    saved = [piece(bwd_in, 0)] + [to_partner(piece(bwd_in, r), r) for r in partners]
    steps = [(p, p + 1) for p in range(last)]
    x_here = lax.ppermute(fwd_in, "pipe", steps)
    g_here = lax.ppermute(bwd_grad_in, "pipe", [(b, a) for a, b in steps])
    section_x = jnp.where(section == first, fwd_in, x_here)
    section_g = jnp.where(section == last, bwd_grad_in, g_here)
    xs, gs = [piece(section_x, 0)], [piece(section_g, 0)]
    for r in partners:
        x_piece, g_piece = piece(fwd_in, r), piece(bwd_grad_in, r)
        x_far = along(
            x_piece, [((a, i), (b, i ^ r)) for a, b in steps for i in range(devices)]
        )
        g_far = along(
            g_piece, [((b, i), (a, i ^ r)) for a, b in steps for i in range(devices)]
        )
        kept = along(
            jnp.where(section == first, x_piece, g_piece),
            [((p, i), (p, i ^ r)) for p in (first, last) for i in range(devices)],
        )
        xs.append(jnp.where(section == first, kept, x_far))
        gs.append(jnp.where(section == last, kept, g_far))

    def dispatch(ids, pieces):
        same, other = slot_rows(ids, pieces)
        return same, to_partner(other, group)

    saved_same, saved_other = dispatch(ids_bwd, saved)
    x_same, x_other = dispatch(ids_fwd, xs)
    g_same, g_other = dispatch(ids_bwd, gs)

    def summed(partials):
        total = partials[0].astype(F32)
        for r in partners:
            total = total + to_partner(partials[r], r).astype(F32)
        return total

    back = summed(in_partials([saved_same, saved_other], gate, up, group))
    ahead = summed(in_partials([x_same, x_other], gate, up, group))
    grad_hidden = summed(grad_partials([g_same, g_other], down, group))

    hidden = (jax.nn.silu(ahead[0]) * ahead[1]).astype(BF16)
    hiddens = [hidden] + [to_partner(hidden, r) for r in partners]
    sig = jax.nn.sigmoid(back[0])
    grad_gate = grad_hidden * back[1] * sig * (1.0 + back[0] * (1.0 - sig))
    grad_up = grad_hidden * (back[0] * sig)
    grads = jnp.stack([grad_gate.astype(BF16), grad_up.astype(BF16)])
    all_grads = [grads] + [to_partner(grads, r) for r in partners]

    def returned(blocks):
        same = [blocks[0]] + [to_partner(blocks[r], r) for r in partners]
        other = [to_partner(blocks[group + r], group + r) for r in range(group)]
        return same, other

    fwd_same, fwd_other = returned(down_rows(hiddens, down))
    bwd_same, bwd_other = returned(back_rows(all_grads, gate, up))
    fwd_out = combine(
        ids_fwd[:1], fwd_gates.reshape(1, tokens), section_x, fwd_same, fwd_other
    )
    bwd_out = combine(
        ids_bwd[:1], bwd_gates.reshape(1, tokens), section_g, bwd_same, bwd_other
    )
    return (fwd_out[None], bwd_out[None])


def solution(mesh):
    spec = P("pipe", "expert", None)
    return jax.shard_map(
        body,
        mesh=mesh,
        in_specs=(spec,) * 5 + (P("pipe", None, "expert"),) + (spec,) * 4,
        out_specs=(spec, spec),
        check_vma=False,
    )
```

time: 101 us -> 98.5 us (0.975)
  matrix products: 22.9 us -> 0 us
  Pallas kernels: 0 us -> 18.3 us
  waiting for transfers between devices: 28 us -> 40.2 us
  other arithmetic: 11.4 us -> 3.74 us
  local copies, waits for them, and re-layouts: 7.52 us -> 3.21 us
  starting transfers between devices: 30.1 us -> 31.8 us
    ppermute x6 -> x21, waiting for transfers between devices: 13.7 us -> 40.2 us  [the longest x16 39.9 us: to_partner(): lax.ppermute(value, 'expert', [(i, i ^ mask) for i in range(devices)])]
    dot_general x8 -> x0, matrix products: 22.9 us -> none  [the longest x1 6.57 us: body(): jnp.dot(joined, in_mats.T, preferred_element_type=jnp.float32)]
    ppermute x6 -> x21, starting transfers between devices: 9.8 us -> 31.8 us  [the longest x16 20.5 us: to_partner(): lax.ppermute(value, 'expert', [(i, i ^ mask) for i in range(devices)])]
    all_to_all x5 -> x0, starting transfers between devices: 20.3 us -> none  [the longest x2 7.31 us: body(): lax.all_to_all(produced.reshape(source_count, slot_count, width), 'expert...]
    pallas_call x0 -> x10, Pallas kernels: none -> 18.3 us  [the longest x2 5.95 us: in_partials(): kernel_call(functools.partial(in_kernel, len(parts), group), (out,) * gro...]
    all_to_all x5 -> x0, waiting for transfers between devices: 14.3 us -> none  [the longest x1 7.49 us: body(): lax.all_to_all(send_fwd, 'expert', split_axis=0, concat_axis=0, tiled=True)]
    convert_element_type x8 -> x1, other arithmetic: 4.5 us -> 0.1 us  [body(): hidden = (jax.nn.silu(ahead[0]) * ahead[1]).astype(BF16)]
    gather x2 -> x0, local copies, waits for them, and re-layouts: 3.08 us -> none  [combine_rows(): blocks[flat_ids, :, slot_pos, :].reshape(token_count, TOP, model_width)]
  transfers between devices with their start and end apart: 11 -> 21, of which waited for: 8 -> 9; matrix products, arithmetic and copies ran while one was open for 34% -> 5% of each run, Pallas kernels for 0% -> 17%
where the time goes in v1:
time: 98.5 us; the launch traced here: 98.1 us
  waiting for transfers between devices  40.2 us (41%)
  starting transfers between devices  31.8 us (32%)
  Pallas kernels  18.3 us (19%)
  other arithmetic  3.74 us (4%)
  local copies, waits for them, and re-layouts  3.21 us (3%)
    ppermute x16, waiting for transfers between devices, to_partner(): lax.ppermute(value, 'expert', [(i, i ^ mask) for i in range(devices)])  39.9 us
    ppermute x16, starting transfers between devices, to_partner(): lax.ppermute(value, 'expert', [(i, i ^ mask) for i in range(devices)])  20.5 us
    ppermute x3, starting transfers between devices, along(): return lax.ppermute(value, ('pipe', 'expert'), flat)  7.51 us
    pallas_call x2, Pallas kernels, in_partials(): kernel_call(functools.partial(in_kernel, len(parts), group), (out,) * gro...  5.95 us
    pallas_call x1, Pallas kernels, back_rows(): kernel_call(functools.partial(back_kernel, group), (out,) * (2 * group),...  3.66 us
    pallas_call x2, Pallas kernels, combine(): kernel_call(functools.partial(combine_kernel, group), jax.ShapeDtypeStruc...  2.94 us
    ppermute x1, starting transfers between devices, body(): x_here = lax.ppermute(fwd_in, 'pipe', steps)  2.52 us
    pallas_call x1, Pallas kernels, down_rows(): kernel_call(functools.partial(down_kernel, group), (out,) * (2 * group),...  2.17 us
  transfers between devices with their start and end apart: 21, of which 9 were waited for; matrix products, arithmetic and copies ran while one was open for 5% of the time, Pallas kernels for 17%

profile of v1, /device:TPU:0, one launch (start us, length us, event | category | flops | bytes accessed | tf_op | source)
XLA Modules:
  0.0 98.1 jit_solution(1823291845270815964)
XLA Ops:
  0.7 2.5 %collective-permute-start = (bf16[64,3584]{1,0:T(8,128)(2,1)}, bf16[64,3584]{1,0:T(8,128)(2,1)S(1)}, u32[]{:S(2)}, u32[]{:S(2)}) collective-permute-start(bf16[64,3584]{1,0:T(8,128)(2,1)} %bitcast.75), channel_id=1, source_target_pairs={{0,4},{4,8},{8,12},{12,16},{16,20},{20,24},{24,28},{1,5},{5,9},{9,... | collective-permute-start | bytes 1376264 | tf_op jit(solution)/shard_map/ppermute | solution.py:270
  3.9 2.3 %collective-permute-start.1 = (s32[2,64]{1,0:T(2,128)S(1)}, s32[2,64]{1,0:T(2,128)S(1)}, u32[]{:S(2)}, u32[]{:S(2)}) collective-permute-start(s32[2,64]{1,0:T(2,128)S(1)} %pad_add_fusion), channel_id=1, source_target_pairs={{0,1},{1,0},{2,3},{3,2},{4,5},{5,4},{6,7},{7,6},{8,9},{9,8},{10,11... | collective-permute-start | bytes 1544 | tf_op jit(solution)/shard_map/ppermute | solution.py:252
  7.3 1.9 %collective-permute-start.2 = (bf16[64,1792]{1,0:T(8,128)(2,1)S(1)}, bf16[64,1792]{1,0:T(8,128)(2,1)S(1)}, u32[]{:S(2)}, u32[]{:S(2)}) collective-permute-start(bf16[64,1792]{1,0:T(8,128)(2,1)S(1)} %get-tuple-element.42), channel_id=1, source_target_pairs={{0,1},{1,0},{2,3},{3,2},{28,29},{29,28},{30,31},{31,30}} | collective-permute-start | bytes 688136 | tf_op jit(solution)/shard_map/ppermute | solution.py:256
  10.5 4.3 %collective-permute-start.3 = (bf16[64,1792]{1,0:T(8,128)(2,1)S(1)}, bf16[64,1792]{1,0:T(8,128)(2,1)S(1)}, u32[]{:S(2)}, u32[]{:S(2)}) collective-permute-start(bf16[64,1792]{1,0:T(8,128)(2,1)S(1)} %get-tuple-element.44), channel_id=1, source_target_pairs={{0,5},{1,4},{2,7},{3,6},{4,9},{5,8},{6,11},{7,10},{8,13},{9,12},{1... | collective-permute-start | bytes 688136 | tf_op jit(solution)/shard_map/ppermute | solution.py:256
  16.0 2.1 %collective-permute-start.14 = (bf16[64,1792]{1,0:T(8,128)(2,1)S(1)}, bf16[64,1792]{1,0:T(8,128)(2,1)S(1)}, u32[]{:S(2)}, u32[]{:S(2)}) collective-permute-start(bf16[64,1792]{1,0:T(8,128)(2,1)S(1)} %get-tuple-element.47), channel_id=1, source_target_pairs={{0,1},{1,0},{2,3},{3,2},{4,5},{5,4},{6,7},{7,6},{8,9},{9,8},{10,11... | collective-permute-start | bytes 688136 | tf_op jit(solution)/shard_map/ppermute | solution.py:252
  19.3 8.1 %collective-permute-done.14.refs_2_ = bf16[64,1792]{1,0:T(8,128)(2,1)S(1)} collective-permute-done((bf16[64,1792]{1,0:T(8,128)(2,1)S(1)}, bf16[64,1792]{1,0:T(8,128)(2,1)S(1)}, u32[]{:S(2)}, u32[]{:S(2)}) %collective-permute-start.14) | collective-permute-done | bytes 229408 | tf_op jit(solution)/shard_map/ppermute | solution.py:252
  29.3 1.6 %collective-permute-start.15 = (bf16[80,1792]{1,0:T(8,128)(2,1)S(1)}, bf16[80,1792]{1,0:T(8,128)(2,1)S(1)}, u32[]{:S(2)}, u32[]{:S(2)}) collective-permute-start(bf16[80,1792]{1,0:T(8,128)(2,1)S(1)} %get-tuple-element.35), channel_id=1, source_target_pairs={{0,2},{1,3},{2,0},{3,1},{4,6},{5,7},{6,4},{7,5},{8,10},{9,11},{10,... | collective-permute-start | bytes 860168 | tf_op jit(solution)/shard_map/ppermute | solution.py:252
  32.1 1.6 %collective-permute-start.4 = (bf16[80,1792]{1,0:T(8,128)(2,1)S(1)}, bf16[80,1792]{1,0:T(8,128)(2,1)S(1)}, u32[]{:S(2)}, u32[]{:S(2)}) collective-permute-start(bf16[80,1792]{1,0:T(8,128)(2,1)S(1)} %get-tuple-element.23), channel_id=1, source_target_pairs={{0,2},{1,3},{2,0},{3,1},{4,6},{5,7},{6,4},{7,5},{8,10},{9,11},{10,... | collective-permute-start | bytes 860168 | tf_op jit(solution)/shard_map/ppermute | solution.py:252
  34.8 4.2 %collective-permute-done.15.refs_1_ = bf16[80,1792]{1,0:T(8,128)(2,1)S(1)} collective-permute-done((bf16[80,1792]{1,0:T(8,128)(2,1)S(1)}, bf16[80,1792]{1,0:T(8,128)(2,1)S(1)}, u32[]{:S(2)}, u32[]{:S(2)}) %collective-permute-start.15) | collective-permute-done | bytes 286752 | tf_op jit(solution)/shard_map/ppermute | solution.py:252
  39.0 2.0 %copy-done.1 = bf16[1,1792,1024]{2,1,0:T(8,128)(2,1)S(1)} copy-done((bf16[1,1792,1024]{2,1,0:T(8,128)(2,1)S(1)}, bf16[1,1792,1024]{2,1,0:T(8,128)(2,1)}, u32[]{:S(2)}) %copy-start.1) | copy-done | bytes 3670040
  41.0 3.0 %shard_map.120 = (bf16[2,80,1024]{2,1,0:T(8,128)(2,1)S(1)}, bf16[2,80,1024]{2,1,0:T(8,128)(2,1)S(1)}) custom-call(bf16[80,1792]{1,0:T(8,128)(2,1)S(1)} %get-tuple-element.34.refs_0_, bf16[80,1792]{1,0:T(8,128)(2,1)S(1)} %collective-permute-done.15.refs_1_, bf16[1792,1024]{1,0:T(8,128)(2,1)S(1)} %bitcast.59, bf16[1792,1024]{1,0:T(8,128)(2,1)S(1)} %bitcast.62), custom_call_target="tpu_custom_call" | custom-call | flops 1174405120 | bytes 7340032 | tf_op jit(solution)/shard_map/pallas_call | solution.py:107
  44.9 3.0 %shard_map.114 = (bf16[2,80,1024]{2,1,0:T(8,128)(2,1)S(1)}, bf16[2,80,1024]{2,1,0:T(8,128)(2,1)S(1)}) custom-call(bf16[80,1792]{1,0:T(8,128)(2,1)S(1)} %get-tuple-element.22.refs_0_, bf16[80,1792]{1,0:T(8,128)(2,1)S(1)} %collective-permute-done.4.refs_1_, bf16[1792,1024]{1,0:T(8,128)(2,1)S(1)} %bitcast.60, bf16[1792,1024]{1,0:T(8,128)(2,1)S(1)} %bitcast.63), custom_call_target="tpu_custom_call" | custom-call | flops 1174405120 | bytes 7340032 | tf_op jit(solution)/shard_map/pallas_call | solution.py:107
  49.1 1.9 %shard_map.118 = (bf16[80,1024]{1,0:T(8,128)(2,1)S(1)}, bf16[80,1024]{1,0:T(8,128)(2,1)S(1)}) custom-call(bf16[80,1792]{1,0:T(8,128)(2,1)S(1)} %get-tuple-element.30.refs_0_, bf16[80,1792]{1,0:T(8,128)(2,1)S(1)} %collective-permute-done.12.refs_1_, bf16[1024,1792]{1,0:T(8,128)(2,1)S(1)} %bitcast.65), custom_call_target="tpu_custom_call" | custom-call | flops 587202560 | bytes 3670016 | tf_op jit(solution)/shard_map/pallas_call | solution.py:133
  52.0 1.8 %collective-permute-done.16 = bf16[2,80,1024]{2,1,0:T(8,128)(2,1)S(1)} collective-permute-done((bf16[2,80,1024]{2,1,0:T(8,128)(2,1)S(1)}, bf16[2,80,1024]{2,1,0:T(8,128)(2,1)S(1)}, u32[]{:S(2)}, u32[]{:S(2)}) %collective-permute-start.16) | collective-permute-done | bytes 327712 | tf_op jit(solution)/shard_map/ppermute | solution.py:252
  53.8 10.4 %collective-permute-done.13 = bf16[80,1024]{1,0:T(8,128)(2,1)S(1)} collective-permute-done((bf16[80,1024]{1,0:T(8,128)(2,1)S(1)}, bf16[80,1024]{1,0:T(8,128)(2,1)S(1)}, u32[]{:S(2)}, u32[]{:S(2)}) %collective-permute-start.13) | collective-permute-done | bytes 163872 | tf_op jit(solution)/shard_map/ppermute | solution.py:252
  65.1 1.8 %collective-permute-start.6 = (bf16[80,1024]{1,0:T(8,128)(2,1)S(1)}, bf16[80,1024]{1,0:T(8,128)(2,1)S(1)}, u32[]{:S(2)}, u32[]{:S(2)}) collective-permute-start(bf16[80,1024]{1,0:T(8,128)(2,1)S(1)} %fusion.5.refs_0_), channel_id=1, source_target_pairs={{0,1},{1,0},{2,3},{3,2},{4,5},{5,4},{6,7},{7,6},{8,9},{9,8},{10,11... | collective-permute-start | bytes 491528 | tf_op jit(solution)/shard_map/ppermute | solution.py:252
  66.9 11.5 %collective-permute-done.6.refs_1_ = bf16[80,1024]{1,0:T(8,128)(2,1)S(1)} collective-permute-done((bf16[80,1024]{1,0:T(8,128)(2,1)S(1)}, bf16[80,1024]{1,0:T(8,128)(2,1)S(1)}, u32[]{:S(2)}, u32[]{:S(2)}) %collective-permute-start.6) | collective-permute-done | bytes 163872 | tf_op jit(solution)/shard_map/ppermute | solution.py:252
  78.4 2.2 %shard_map.115 = (bf16[40,1792]{1,0:T(8,128)(2,1)S(1)}, bf16[40,1792]{1,0:T(8,128)(2,1)S(1)}, bf16[40,1792]{1,0:T(8,128)(2,1)S(1)}, bf16[40,1792]{1,0:T(8,128)(2,1)S(1)}) custom-call(bf16[80,1024]{1,0:T(8,128)(2,1)S(1)} %fusion.5.refs_0_, bf16[80,1024]{1,0:T(8,128)(2,1)S(1)} %collective-permute-done.6.refs_1_, bf16[1024,1792]{1,0:T(8,128)(2,1)S(1)} %bitcast.66), custom_call_target="tpu_custom_call" | custom-call | flops 587202560 | bytes 3670016 | tf_op jit(solution)/shard_map/pallas_call | solution.py:163
  80.9 1.5 %collective-permute-start.8 = (bf16[40,1792]{1,0:T(8,128)(2,1)S(1)}, bf16[40,1792]{1,0:T(8,128)(2,1)S(1)}, u32[]{:S(2)}, u32[]{:S(2)}) collective-permute-start(bf16[40,1792]{1,0:T(8,128)(2,1)S(1)} %get-tuple-element.28), channel_id=1, source_target_pairs={{0,2},{1,3},{2,0},{3,1},{4,6},{5,7},{6,4},{7,5},{8,10},{9,11},{10,... | collective-permute-start | bytes 430088 | tf_op jit(solution)/shard_map/ppermute | solution.py:252
  82.5 1.8 %collective-permute-start.9 = (bf16[40,1792]{1,0:T(8,128)(2,1)S(1)}, bf16[40,1792]{1,0:T(8,128)(2,1)S(1)}, u32[]{:S(2)}, u32[]{:S(2)}) collective-permute-start(bf16[40,1792]{1,0:T(8,128)(2,1)S(1)} %get-tuple-element.29), channel_id=1, source_target_pairs={{0,3},{1,2},{2,1},{3,0},{4,7},{5,6},{6,5},{7,4},{8,11},{9,10},{10,... | collective-permute-start | bytes 430088 | tf_op jit(solution)/shard_map/ppermute | solution.py:252
  84.2 3.7 %shard_map.121 = (bf16[40,1792]{1,0:T(8,128)(2,1)S(1)}, bf16[40,1792]{1,0:T(8,128)(2,1)S(1)}, bf16[40,1792]{1,0:T(8,128)(2,1)S(1)}, bf16[40,1792]{1,0:T(8,128)(2,1)S(1)}) custom-call(bf16[2,80,1024]{2,1,0:T(8,128)(2,1)S(1)} %pad_maximum_fusion.refs_0_, bf16[2,80,1024]{2,1,0:T(8,128)(2,1)S(1)} %collective-permute-done.17.refs_1_, ...), custom_call_target="tpu_custom_call" | custom-call | flops 1174405120 | bytes 7340032 | tf_op jit(solution)/shard_map/pallas_call | solution.py:191
  88.3 1.5 %collective-permute-start.19 = (bf16[40,1792]{1,0:T(8,128)(2,1)S(1)}, bf16[40,1792]{1,0:T(8,128)(2,1)S(1)}, u32[]{:S(2)}, u32[]{:S(2)}) collective-permute-start(bf16[40,1792]{1,0:T(8,128)(2,1)S(1)} %get-tuple-element.40), channel_id=1, source_target_pairs={{0,2},{1,3},{2,0},{3,1},{4,6},{5,7},{6,4},{7,5},{8,10},{9,11},{10,... | collective-permute-start | bytes 430088 | tf_op jit(solution)/shard_map/ppermute | solution.py:252
  89.8 1.7 %collective-permute-start.20 = (bf16[40,1792]{1,0:T(8,128)(2,1)S(1)}, bf16[40,1792]{1,0:T(8,128)(2,1)S(1)}, u32[]{:S(2)}, u32[]{:S(2)}) collective-permute-start(bf16[40,1792]{1,0:T(8,128)(2,1)S(1)} %get-tuple-element.41), channel_id=1, source_target_pairs={{0,3},{1,2},{2,1},{3,0},{4,7},{5,6},{6,5},{7,4},{8,11},{9,10},{10,... | collective-permute-start | bytes 430088 | tf_op jit(solution)/shard_map/ppermute | solution.py:252
  95.0 1.6 %collective-permute-done.20.refs_6_ = bf16[40,1792]{1,0:T(8,128)(2,1)S(1)} collective-permute-done((bf16[40,1792]{1,0:T(8,128)(2,1)S(1)}, bf16[40,1792]{1,0:T(8,128)(2,1)S(1)}, u32[]{:S(2)}, u32[]{:S(2)}) %collective-permute-start.20) | collective-permute-done | bytes 143392 | tf_op jit(solution)/shard_map/ppermute | solution.py:252
  (63 shorter events, 19.1 us)
Async XLA Ops:
  0.6 30.4 %copy-start.8 = (bf16[1,64,3584]{2,1,0:T(8,128)(2,1)S(1)}, bf16[1,64,3584]{2,1,0:T(8,128)(2,1)}, u32[]{:S(2)}) copy-start(bf16[1,64,3584]{2,1,0:T(8,128)(2,1)} %param.10) | copy-start | bytes 1376260
  0.6 30.8 %copy-start.9 = (bf16[1,64,3584]{2,1,0:T(8,128)(2,1)S(1)}, bf16[1,64,3584]{2,1,0:T(8,128)(2,1)}, u32[]{:S(2)}) copy-start(bf16[1,64,3584]{2,1,0:T(8,128)(2,1)} %param.12) | copy-start | bytes 1376260
  0.7 30.3 %collective-permute-start = (bf16[64,3584]{1,0:T(8,128)(2,1)}, bf16[64,3584]{1,0:T(8,128)(2,1)S(1)}, u32[]{:S(2)}, u32[]{:S(2)}) collective-permute-start(bf16[64,3584]{1,0:T(8,128)(2,1)} %bitcast.75), channel_id=1, source_target_pairs={{0,4},{4,8},{8,12},{12,16},{16,20},{20,24},{24,28},{1,5},{5,9},{9,... | collective-permute-start | bytes 1376264 | tf_op jit(solution)/shard_map/ppermute | solution.py:270
  3.9 12.1 %collective-permute-start.1 = (s32[2,64]{1,0:T(2,128)S(1)}, s32[2,64]{1,0:T(2,128)S(1)}, u32[]{:S(2)}, u32[]{:S(2)}) collective-permute-start(s32[2,64]{1,0:T(2,128)S(1)} %pad_add_fusion), channel_id=1, source_target_pairs={{0,1},{1,0},{2,3},{3,2},{4,5},{5,4},{6,7},{7,6},{8,9},{9,8},{10,11... | collective-permute-start | bytes 1544 | tf_op jit(solution)/shard_map/ppermute | solution.py:252
  7.3 22.0 %collective-permute-start.2 = (bf16[64,1792]{1,0:T(8,128)(2,1)S(1)}, bf16[64,1792]{1,0:T(8,128)(2,1)S(1)}, u32[]{:S(2)}, u32[]{:S(2)}) collective-permute-start(bf16[64,1792]{1,0:T(8,128)(2,1)S(1)} %get-tuple-element.42), channel_id=1, source_target_pairs={{0,1},{1,0},{2,3},{3,2},{28,29},{29,28},{30,31},{31,30}} | collective-permute-start | bytes 688136 | tf_op jit(solution)/shard_map/ppermute | solution.py:256
  9.2 21.7 %collective-permute-start.11 = (bf16[64,1792]{1,0:T(8,128)(2,1)S(1)}, bf16[64,1792]{1,0:T(8,128)(2,1)S(1)}, u32[]{:S(2)}, u32[]{:S(2)}) collective-permute-start(bf16[64,1792]{1,0:T(8,128)(2,1)S(1)} %get-tuple-element.43), channel_id=1, source_target_pairs={{4,1},{5,0},{6,3},{7,2},{8,5},{9,4},{10,7},{11,6},{12,9},{13,8},{1... | collective-permute-start | bytes 688136 | tf_op jit(solution)/shard_map/ppermute | solution.py:256
  10.5 20.4 %collective-permute-start.3 = (bf16[64,1792]{1,0:T(8,128)(2,1)S(1)}, bf16[64,1792]{1,0:T(8,128)(2,1)S(1)}, u32[]{:S(2)}, u32[]{:S(2)}) collective-permute-start(bf16[64,1792]{1,0:T(8,128)(2,1)S(1)} %get-tuple-element.44), channel_id=1, source_target_pairs={{0,5},{1,4},{2,7},{3,6},{4,9},{5,8},{6,11},{7,10},{8,13},{9,12},{1... | collective-permute-start | bytes 688136 | tf_op jit(solution)/shard_map/ppermute | solution.py:256
  15.9 23.0 %copy-start = (bf16[1,1792,1024]{2,1,0:T(8,128)(2,1)S(1)}, bf16[1,1792,1024]{2,1,0:T(8,128)(2,1)}, u32[]{:S(2)}) copy-start(bf16[1,1792,1024]{2,1,0:T(8,128)(2,1)} %param.13) | copy-start | bytes 11010052
  16.0 11.5 %collective-permute-start.14 = (bf16[64,1792]{1,0:T(8,128)(2,1)S(1)}, bf16[64,1792]{1,0:T(8,128)(2,1)S(1)}, u32[]{:S(2)}, u32[]{:S(2)}) collective-permute-start(bf16[64,1792]{1,0:T(8,128)(2,1)S(1)} %get-tuple-element.47), channel_id=1, source_target_pairs={{0,1},{1,0},{2,3},{3,2},{4,5},{5,4},{6,7},{7,6},{8,9},{9,8},{10,11... | collective-permute-start | bytes 688136 | tf_op jit(solution)/shard_map/ppermute | solution.py:252
  27.5 3.9 %collective-permute-start.10 = (bf16[64,3584]{1,0:T(8,128)(2,1)}, bf16[64,3584]{1,0:T(8,128)(2,1)S(1)}, u32[]{:S(2)}, u32[]{:S(2)}) collective-permute-start(bf16[64,3584]{1,0:T(8,128)(2,1)} %bitcast.76), channel_id=1, source_target_pairs={{4,0},{8,4},{12,8},{16,12},{20,16},{24,20},{28,24},{5,1},{9,5},{13... | collective-permute-start | bytes 1376264 | tf_op jit(solution)/shard_map/ppermute | solution.py:271
  29.3 9.6 %collective-permute-start.15 = (bf16[80,1792]{1,0:T(8,128)(2,1)S(1)}, bf16[80,1792]{1,0:T(8,128)(2,1)S(1)}, u32[]{:S(2)}, u32[]{:S(2)}) collective-permute-start(bf16[80,1792]{1,0:T(8,128)(2,1)S(1)} %get-tuple-element.35), channel_id=1, source_target_pairs={{0,2},{1,3},{2,0},{3,1},{4,6},{5,7},{6,4},{7,5},{8,10},{9,11},{10,... | collective-permute-start | bytes 860168 | tf_op jit(solution)/shard_map/ppermute | solution.py:252
  32.1 12.8 %collective-permute-start.4 = (bf16[80,1792]{1,0:T(8,128)(2,1)S(1)}, bf16[80,1792]{1,0:T(8,128)(2,1)S(1)}, u32[]{:S(2)}, u32[]{:S(2)}) collective-permute-start(bf16[80,1792]{1,0:T(8,128)(2,1)S(1)} %get-tuple-element.23), channel_id=1, source_target_pairs={{0,2},{1,3},{2,0},{3,1},{4,6},{5,7},{6,4},{7,5},{8,10},{9,11},{10,... | collective-permute-start | bytes 860168 | tf_op jit(solution)/shard_map/ppermute | solution.py:252
  34.2 15.0 %collective-permute-start.12 = (bf16[80,1792]{1,0:T(8,128)(2,1)S(1)}, bf16[80,1792]{1,0:T(8,128)(2,1)S(1)}, u32[]{:S(2)}, u32[]{:S(2)}) collective-permute-start(bf16[80,1792]{1,0:T(8,128)(2,1)S(1)} %get-tuple-element.31), channel_id=1, source_target_pairs={{0,2},{1,3},{2,0},{3,1},{4,6},{5,7},{6,4},{7,5},{8,10},{9,11},{10,... | collective-permute-start | bytes 860168 | tf_op jit(solution)/shard_map/ppermute | solution.py:252
  44.0 9.8 %collective-permute-start.16 = (bf16[2,80,1024]{2,1,0:T(8,128)(2,1)S(1)}, bf16[2,80,1024]{2,1,0:T(8,128)(2,1)S(1)}, u32[]{:S(2)}, u32[]{:S(2)}) collective-permute-start(bf16[2,80,1024]{2,1,0:T(8,128)(2,1)S(1)} %get-tuple-element.37), channel_id=1, source_target_pairs={{0,1},{1,0},{2,3},{3,2},{4,5},{5,4},{6,7},{7,6},{8,9},{9,8},{10,11... | collective-permute-start | bytes 983048 | tf_op jit(solution)/shard_map/ppermute | solution.py:252
  47.9 17.0 %collective-permute-start.5 = (bf16[2,80,1024]{2,1,0:T(8,128)(2,1)S(1)}, bf16[2,80,1024]{2,1,0:T(8,128)(2,1)S(1)}, u32[]{:S(2)}, u32[]{:S(2)}) collective-permute-start(bf16[2,80,1024]{2,1,0:T(8,128)(2,1)S(1)} %get-tuple-element.25), channel_id=1, source_target_pairs={{0,1},{1,0},{2,3},{3,2},{4,5},{5,4},{6,7},{7,6},{8,9},{9,8},{10,11... | collective-permute-start | bytes 983048 | tf_op jit(solution)/shard_map/ppermute | solution.py:252
  51.1 13.2 %collective-permute-start.13 = (bf16[80,1024]{1,0:T(8,128)(2,1)S(1)}, bf16[80,1024]{1,0:T(8,128)(2,1)S(1)}, u32[]{:S(2)}, u32[]{:S(2)}) collective-permute-start(bf16[80,1024]{1,0:T(8,128)(2,1)S(1)} %get-tuple-element.33), channel_id=1, source_target_pairs={{0,1},{1,0},{2,3},{3,2},{4,5},{5,4},{6,7},{7,6},{8,9},{9,8},{10,11... | collective-permute-start | bytes 491528 | tf_op jit(solution)/shard_map/ppermute | solution.py:252
  64.5 19.7 %collective-permute-start.17 = (bf16[2,80,1024]{2,1,0:T(8,128)(2,1)S(1)}, bf16[2,80,1024]{2,1,0:T(8,128)(2,1)S(1)}, u32[]{:S(2)}, u32[]{:S(2)}) collective-permute-start(bf16[2,80,1024]{2,1,0:T(8,128)(2,1)S(1)} %pad_maximum_fusion.refs_0_), channel_id=1, source_target_pairs={{0,1},{1,0},{2,3},{3,2},{4,5},{5,4},{6,7},{7,6},{8,9},{9,8},{10,11... | collective-permute-start | bytes 983048 | tf_op jit(solution)/shard_map/ppermute | solution.py:252
  65.1 13.4 %collective-permute-start.6 = (bf16[80,1024]{1,0:T(8,128)(2,1)S(1)}, bf16[80,1024]{1,0:T(8,128)(2,1)S(1)}, u32[]{:S(2)}, u32[]{:S(2)}) collective-permute-start(bf16[80,1024]{1,0:T(8,128)(2,1)S(1)} %fusion.5.refs_0_), channel_id=1, source_target_pairs={{0,1},{1,0},{2,3},{3,2},{4,5},{5,4},{6,7},{7,6},{8,9},{9,8},{10,11... | collective-permute-start | bytes 491528 | tf_op jit(solution)/shard_map/ppermute | solution.py:252
  80.6 9.2 %collective-permute-start.7 = (bf16[40,1792]{1,0:T(8,128)(2,1)S(1)}, bf16[40,1792]{1,0:T(8,128)(2,1)S(1)}, u32[]{:S(2)}, u32[]{:S(2)}) collective-permute-start(bf16[40,1792]{1,0:T(8,128)(2,1)S(1)} %get-tuple-element.27), channel_id=1, source_target_pairs={{0,1},{1,0},{2,3},{3,2},{4,5},{5,4},{6,7},{7,6},{8,9},{9,8},{10,11... | collective-permute-start | bytes 430088 | tf_op jit(solution)/shard_map/ppermute | solution.py:252
  80.9 10.5 %collective-permute-start.8 = (bf16[40,1792]{1,0:T(8,128)(2,1)S(1)}, bf16[40,1792]{1,0:T(8,128)(2,1)S(1)}, u32[]{:S(2)}, u32[]{:S(2)}) collective-permute-start(bf16[40,1792]{1,0:T(8,128)(2,1)S(1)} %get-tuple-element.28), channel_id=1, source_target_pairs={{0,2},{1,3},{2,0},{3,1},{4,6},{5,7},{6,4},{7,5},{8,10},{9,11},{10,... | collective-permute-start | bytes 430088 | tf_op jit(solution)/shard_map/ppermute | solution.py:252
  82.5 9.0 %collective-permute-start.9 = (bf16[40,1792]{1,0:T(8,128)(2,1)S(1)}, bf16[40,1792]{1,0:T(8,128)(2,1)S(1)}, u32[]{:S(2)}, u32[]{:S(2)}) collective-permute-start(bf16[40,1792]{1,0:T(8,128)(2,1)S(1)} %get-tuple-element.29), channel_id=1, source_target_pairs={{0,3},{1,2},{2,1},{3,0},{4,7},{5,6},{6,5},{7,4},{8,11},{9,10},{10,... | collective-permute-start | bytes 430088 | tf_op jit(solution)/shard_map/ppermute | solution.py:252
  87.9 6.3 %collective-permute-start.18 = (bf16[40,1792]{1,0:T(8,128)(2,1)S(1)}, bf16[40,1792]{1,0:T(8,128)(2,1)S(1)}, u32[]{:S(2)}, u32[]{:S(2)}) collective-permute-start(bf16[40,1792]{1,0:T(8,128)(2,1)S(1)} %get-tuple-element.39), channel_id=1, source_target_pairs={{0,1},{1,0},{2,3},{3,2},{4,5},{5,4},{6,7},{7,6},{8,9},{9,8},{10,11... | collective-permute-start | bytes 430088 | tf_op jit(solution)/shard_map/ppermute | solution.py:252
  88.3 6.8 %collective-permute-start.19 = (bf16[40,1792]{1,0:T(8,128)(2,1)S(1)}, bf16[40,1792]{1,0:T(8,128)(2,1)S(1)}, u32[]{:S(2)}, u32[]{:S(2)}) collective-permute-start(bf16[40,1792]{1,0:T(8,128)(2,1)S(1)} %get-tuple-element.40), channel_id=1, source_target_pairs={{0,2},{1,3},{2,0},{3,1},{4,6},{5,7},{6,4},{7,5},{8,10},{9,11},{10,... | collective-permute-start | bytes 430088 | tf_op jit(solution)/shard_map/ppermute | solution.py:252
  89.8 6.9 %collective-permute-start.20 = (bf16[40,1792]{1,0:T(8,128)(2,1)S(1)}, bf16[40,1792]{1,0:T(8,128)(2,1)S(1)}, u32[]{:S(2)}, u32[]{:S(2)}) collective-permute-start(bf16[40,1792]{1,0:T(8,128)(2,1)S(1)} %get-tuple-element.41), channel_id=1, source_target_pairs={{0,3},{1,2},{2,1},{3,0},{4,7},{5,6},{6,5},{7,4},{8,11},{9,10},{10,... | collective-permute-start | bytes 430088 | tf_op jit(solution)/shard_map/ppermute | solution.py:252
  (7 other events, 56.7 us)

commit v2 on v1

v2 whole, which is shorter than its diff:
```python
import functools

import jax
import jax.numpy as jnp
from jax import lax
from jax.experimental import pallas as pl
from jax.experimental.pallas import tpu as pltpu
from jax.sharding import PartitionSpec as P

EXPERTS = 2
CAP = 40
BF16 = jnp.bfloat16
F32 = jnp.float32
VMEM_LIMIT = 40 * 1024 * 1024
FWD_IDS, BWD_IDS, FWD_GATES, BWD_GATES = (slice(i, i + 1) for i in range(4))


def kernel_call(kernel, out_shape, inputs, flops, left=0, copies=0):
    whole = pl.BlockSpec(memory_space=pltpu.VMEM)
    outside = pl.BlockSpec(memory_space=pltpu.HBM)
    outs = jax.tree.leaves(out_shape)
    moved = sum(v.size * v.dtype.itemsize for v in (*inputs, *outs))
    return pl.pallas_call(
        kernel,
        out_shape=out_shape,
        in_specs=[outside] * left + [whole] * (len(inputs) - left),
        out_specs=jax.tree.map(lambda _: whole, out_shape),
        scratch_shapes=[pltpu.SemaphoreType.DMA((copies,))] * (copies > 0),
        compiler_params=pltpu.CompilerParams(vmem_limit_bytes=VMEM_LIMIT),
        cost_estimate=pl.CostEstimate(flops=flops, bytes_accessed=moved, transcendentals=0),
    )(*inputs)


def like(shape):
    return jax.ShapeDtypeStruct(shape, BF16)


def tables(ids_row, expert):
    tokens = ids_row.shape[1]
    row = lax.broadcasted_iota(jnp.int32, (tokens, tokens), 0)
    col = lax.broadcasted_iota(jnp.int32, (tokens, tokens), 1)
    earlier = (row < col).astype(BF16)
    mine = jnp.broadcast_to(ids_row == expert, (8, tokens))
    before = jnp.dot(mine.astype(BF16), earlier, preferred_element_type=F32)[:1].astype(jnp.int32)
    place = lax.broadcasted_iota(jnp.int32, (1, tokens), 1)
    slot = lax.broadcasted_iota(jnp.int32, (CAP, tokens), 0)
    same = ids_row == expert
    table_same = ((slot == before) & same).astype(BF16)
    table_other = ((slot == place - before) & jnp.logical_not(same)).astype(BF16)
    return jnp.concatenate([table_same, table_other], axis=0)


def position(group):
    index = lax.axis_index("expert")
    return index // group, lax.rem(index, group)


def fetch(sources, targets, sems):
    copies = [
        pltpu.make_async_copy(source, target, sems.at[i])
        for i, (source, target) in enumerate(zip(sources, targets))
    ]
    for copy in copies:
        copy.start()
    for copy in copies:
        copy.wait()


def home_slots_kernel(group, x, ids, *outs):
    expert, own_slice = position(group)
    table = tables(ids[...][BWD_IDS], expert)
    width = x.shape[1] // group
    for own in range(group):

        @pl.when(own_slice == own)
        def _(own=own):
            for r in range(group):
                at = (own ^ r) * width
                rows = jnp.dot(table, x[:, at : at + width], preferred_element_type=F32)
                outs[r][...] = rows[:CAP].astype(BF16)
                outs[group + r][...] = rows[CAP:].astype(BF16)


def home_slots(x, routing, group):
    tokens, model = x.shape
    out = like((CAP, model // group))
    return kernel_call(
        functools.partial(home_slots_kernel, group),
        (out,) * (2 * group),
        (x, routing),
        4 * CAP * tokens * model * 80,
    )


def stage_kernel(count, *refs):
    fetch(refs[:count], refs[count : 2 * count], refs[-1])


def staged(arrays):
    count = len(arrays)
    return kernel_call(
        functools.partial(stage_kernel, count),
        tuple(like(v.shape) for v in arrays),
        arrays,
        0,
        left=count,
        copies=count,
    )


def stream_slots_kernel(group, last, *refs):
    routing, x_kept, g_kept, x_here, g_here, *outs = refs
    section_x, section_g, x_own, g_own, *sent = outs
    section = lax.axis_index("pipe")
    expert, own_slice = position(group)
    width = x_here.shape[1] // group
    section_x[...] = jnp.where(section == 0, x_kept[...], x_here[...])
    section_g[...] = jnp.where(section == last, g_kept[...], g_here[...])
    small = routing[...]
    streams = (
        (tables(small[FWD_IDS], expert), section_x, x_own),
        (tables(small[BWD_IDS], expert), section_g, g_own),
    )
    for own in range(group):

        @pl.when(own_slice == own)
        def _(own=own):
            for k, (table, value, kept) in enumerate(streams):
                for r in range(group):
                    at = (own ^ r) * width
                    rows = jnp.dot(table, value[:, at : at + width], preferred_element_type=F32)
                    same, other = rows[:CAP].astype(BF16), rows[CAP:].astype(BF16)
                    if r == 0:
                        kept[...] = same
                    else:
                        sent[r - 1][k] = same
                    sent[group - 1 + r][k] = other


def stream_slots(routing, x_kept, g_kept, x_here, g_here, group, last):
    tokens, model = x_here.shape
    width = model // group
    whole, one, two = like(x_here.shape), like((CAP, width)), like((2, CAP, width))
    return kernel_call(
        functools.partial(stream_slots_kernel, group, last),
        (whole, whole, one, one) + (two,) * (2 * group - 1),
        (routing, x_kept, g_kept, x_here, g_here),
        8 * CAP * tokens * model,
    )


def split_rows(acc, group, outs, put):
    parts = acc.shape[0] // (group * CAP)
    for r in range(group):
        rows = [acc[(p * group + r) * CAP : (p * group + r + 1) * CAP] for p in range(parts)]
        put(outs[r], jnp.concatenate(rows, axis=0).astype(BF16))


def dot_nt(a, b):
    return lax.dot_general(a, b, (((1,), (1,)), ((), ())), preferred_element_type=F32)


def tile_of(extent):
    return next(t for t in (512, 256, extent) if extent % t == 0)


def gathered(refs, stream):
    return jnp.concatenate([ref[...] if len(ref.shape) == 2 else ref[stream] for ref in refs], axis=0)


def in_kernel(count, group, stream, *refs):
    rows = gathered(refs[:count], stream)
    gate, up, *outs = refs[count:]
    hidden = gate.shape[1]
    tile = tile_of(hidden)
    for k, mat in enumerate((gate, up)):
        for at in range(0, hidden, tile):

            def put(ref, value, k=k, at=at):
                ref[k, :, at : at + tile] = value

            acc = jnp.dot(rows, mat[:, at : at + tile], preferred_element_type=F32)
            split_rows(acc, group, outs, put)


def in_partials(parts, gate, up, group, stream=0):
    width, hidden = gate.shape
    rows = len(parts) * CAP
    return kernel_call(
        functools.partial(in_kernel, len(parts), group, stream),
        (like((2, rows // group, hidden)),) * group,
        (*parts, gate, up),
        4 * rows * width * hidden,
    )


def grad_kernel(count, group, stream, *refs):
    rows = gathered(refs[:count], stream)
    down, *outs = refs[count:]
    hidden = down.shape[0]
    tile = tile_of(hidden)
    for at in range(0, hidden, tile):

        def put(ref, value, at=at):
            ref[:, at : at + tile] = value

        split_rows(dot_nt(rows, down[at : at + tile, :]), group, outs, put)


def grad_partials(parts, down, group, stream=0):
    hidden, width = down.shape
    rows = len(parts) * CAP
    return kernel_call(
        functools.partial(grad_kernel, len(parts), group, stream),
        (like((rows // group, hidden)),) * group,
        (*parts, down),
        2 * rows * width * hidden,
    )


def put_blocks(acc, group, outs, at, tile):
    for p in range(2):
        for r in range(group):
            block = (r * 2 + p) * CAP
            outs[p * group + r][:, at : at + tile] = acc[block : block + CAP]


def down_kernel(group, *refs):
    hs, (down, *outs) = refs[:group], refs[group:]
    rows = jnp.concatenate([h[...] for h in hs], axis=0)
    width = down.shape[1]
    tile = tile_of(width)
    for at in range(0, width, tile):
        acc = jnp.dot(rows, down[:, at : at + tile], preferred_element_type=F32).astype(BF16)
        put_blocks(acc, group, outs, at, tile)


def down_rows(hs, down):
    group = len(hs)
    hidden, width = down.shape
    return kernel_call(
        functools.partial(down_kernel, group),
        (like((CAP, width)),) * (2 * group),
        (*hs, down),
        4 * group * CAP * hidden * width,
    )


def back_kernel(group, *refs):
    gs, (gate, up, *outs) = refs[:group], refs[group:]
    grads_gate = jnp.concatenate([g[0] for g in gs], axis=0)
    grads_up = jnp.concatenate([g[1] for g in gs], axis=0)
    width = gate.shape[0]
    tile = tile_of(width)
    for at in range(0, width, tile):
        acc = dot_nt(grads_gate, gate[at : at + tile, :]) + dot_nt(grads_up, up[at : at + tile, :])
        put_blocks(acc.astype(BF16), group, outs, at, tile)


def back_rows(gs, gate, up):
    group = len(gs)
    width, hidden = gate.shape
    return kernel_call(
        functools.partial(back_kernel, group),
        (like((CAP, width)),) * (2 * group),
        (*gs, gate, up),
        8 * group * CAP * hidden * width,
    )


def combine_kernel(group, ids, gates, *refs):
    routing, base, *rest = refs
    small = routing[...]
    same, other, out = rest[:group], rest[group : 2 * group], rest[2 * group]
    expert, own_slice = position(group)
    table = tables(small[ids], expert)
    tokens = base.shape[0]
    width = same[0].shape[1]
    row = lax.broadcasted_iota(jnp.int32, (tokens, tokens), 0)
    col = lax.broadcasted_iota(jnp.int32, (tokens, tokens), 1)
    weight = jnp.sum(jnp.where(row == col, small[gates], 0.0), axis=1, keepdims=True)
    contract = (((0,), (0,)), ((), ()))
    for r in range(group):
        blocks = jnp.concatenate([same[r][...], other[r][...]], axis=0)
        picked = lax.dot_general(table, blocks, contract, preferred_element_type=F32)
        for own in range(group):

            @pl.when(own_slice == own)
            def _(own=own, r=r, picked=picked):
                at = (own ^ r) * width
                out[:, at : at + width] = (
                    base[:, at : at + width].astype(F32) + weight * picked
                ).astype(BF16)


def combine(routing, ids, gates, base, same, other):
    group = len(same)
    return kernel_call(
        functools.partial(combine_kernel, group, ids, gates),
        like(base.shape),
        (routing, base, *same, *other),
        4 * CAP * base.shape[0] * base.shape[1],
    )


def after(value, *earlier):
    return lax.optimization_barrier((value, *earlier))[0]


def body(fwd_in, bwd_in, bwd_grad_in, w_gate, w_up, w_down, fwd_ids, fwd_gates, bwd_ids, bwd_gates):
    sections = lax.axis_size("pipe")
    devices = lax.axis_size("expert")
    group = devices // EXPERTS
    partners = range(1, group)
    section = lax.axis_index("pipe")
    tokens, model = fwd_in.shape[1:]
    gate, up, down = w_gate[0], w_up[0], w_down[0]

    def to_partner(value, mask):
        return lax.ppermute(value, "expert", [(i, i ^ mask) for i in range(devices)])

    first, last = 0, sections - 1
    fwd_in, bwd_in, bwd_grad_in = fwd_in[0], bwd_in[0], bwd_grad_in[0]
    small = (fwd_ids, bwd_ids, fwd_gates, bwd_gates)
    routing = jnp.concatenate([v.reshape(1, tokens).astype(F32) for v in small], axis=0)

    def sent(rows):
        return [to_partner(v, r) for r, v in enumerate(rows, 1)]

    steps = [(p, p + 1) for p in range(last)]
    x_here = lax.ppermute(fwd_in, "pipe", steps)
    g_here = lax.ppermute(bwd_grad_in, "pipe", [(b, a) for a, b in steps])
    saved_own, *saved = home_slots(bwd_in, routing, group)
    saved_rows = [saved_own, *sent(saved)]
    section_x, section_g, x_own, g_own, *streams = stream_slots(
        routing, fwd_in, bwd_grad_in, x_here, g_here, group, last
    )
    stream_rows = sent(streams)
    gate, up, down = staged(after((gate, up, down), streams))

    def summed(own, arrived):
        total = own.astype(F32)
        for value in arrived:
            total = total + value.astype(F32)
        return total

    back_parts = in_partials(saved_rows, gate, up, group)
    back_sent = sent(back_parts[1:])
    stream_rows = after(stream_rows, back_parts)
    g_parts = grad_partials([g_own, *stream_rows], down, group, 1)
    g_sent = sent(g_parts[1:])
    x_parts = in_partials([after(x_own, g_parts), *stream_rows], gate, up, group, 0)
    x_sent = sent(x_parts[1:])

    back_sent, g_sent = after((back_sent, g_sent), x_parts)
    back = summed(back_parts[0], back_sent)
    grad_hidden = summed(g_parts[0], g_sent)
    sig = jax.nn.sigmoid(back[0])
    grad_gate = grad_hidden * back[1] * sig * (1.0 + back[0] * (1.0 - sig))
    grad_up = grad_hidden * (back[0] * sig)
    grads = jnp.stack([grad_gate.astype(BF16), grad_up.astype(BF16)])
    grads_sent = sent([grads] * (group - 1))

    x_sent = after(x_sent, grads)
    ahead = summed(x_parts[0], x_sent)
    hidden = (jax.nn.silu(ahead[0]) * ahead[1]).astype(BF16)
    hidden_sent = sent([hidden] * (group - 1))

    def returned(blocks):
        rows = sent(blocks[1:])
        return [blocks[0], *rows[: group - 1]], rows[group - 1 :]

    bwd_rows = back_rows([grads, *grads_sent], gate, up)
    bwd_same, bwd_other = returned(bwd_rows)
    hidden_sent = after(hidden_sent, bwd_rows)
    fwd_same, fwd_other = returned(down_rows([hidden, *hidden_sent], down))
    bwd_out = combine(routing, BWD_IDS, BWD_GATES, section_g, bwd_same, bwd_other)
    fwd_out = combine(routing, FWD_IDS, FWD_GATES, section_x, fwd_same, fwd_other)
    return (fwd_out[None], bwd_out[None])


def solution(mesh):
    spec = P("pipe", "expert", None)
    return jax.shard_map(
        body,
        mesh=mesh,
        in_specs=(spec,) * 5 + (P("pipe", None, "expert"),) + (spec,) * 4,
        out_specs=(spec, spec),
        check_vma=False,
    )
```

time: 98.5 us -> 75.6 us (0.77)
  the two profiles are of different devices: /device:TPU:0 before, /device:TPU:18 now
where the time goes in v2:
time: 75.6 us; the launch traced here: 74.9 us
  waiting for transfers between devices  30.7 us (41%)
  starting transfers between devices  24.9 us (33%)
  Pallas kernels  15.7 us (21%)
  other arithmetic  1.84 us (2%)
  local copies, waits for them, and re-layouts  1.02 us (1%)
  between operations  0.79 us (1%)
    ppermute x17, waiting for transfers between devices, to_partner(): lax.ppermute(value, 'expert', [(i, i ^ mask) for i in range(devices)])  30.7 us
    ppermute x17, starting transfers between devices, to_partner(): lax.ppermute(value, 'expert', [(i, i ^ mask) for i in range(devices)])  19.3 us
    pallas_call x10, Pallas kernels, kernel_call(): pl.pallas_call(kernel, out_shape=out_shape, in_specs=[outside] * left + [...  15.7 us
    ppermute x1, starting transfers between devices, body(): g_here = lax.ppermute(bwd_grad_in, 'pipe', [(b, a) for a, b in steps])  3.64 us
    ppermute x1, starting transfers between devices, body(): x_here = lax.ppermute(fwd_in, 'pipe', steps)  1.92 us
  transfers between devices with their start and end apart: 19, of which 11 were waited for; matrix products, arithmetic and copies ran while one was open for 2% of the time, Pallas kernels for 19%

profile of v2, /device:TPU:18, one launch (start us, length us, event | category | flops | bytes accessed | tf_op | source)
XLA Modules:
  0.0 74.9 jit_solution(11286821039820486232)
XLA Ops:
  0.6 1.9 %collective-permute-start = (bf16[64,3584]{1,0:T(8,128)(2,1)}, bf16[64,3584]{1,0:T(8,128)(2,1)S(1)}, u32[]{:S(2)}, u32[]{:S(2)}) collective-permute-start(bf16[64,3584]{1,0:T(8,128)(2,1)} %bitcast.50), channel_id=1, source_target_pairs={{0,4},{4,8},{8,12},{12,16},{16,20},{20,24},{24,28},{1,5},{5,9},{9,... | collective-permute-start | bytes 1376264 | tf_op jit(solution)/shard_map/ppermute | solution.py:331
  2.6 3.6 %collective-permute-start.1 = (bf16[64,3584]{1,0:T(8,128)(2,1)}, bf16[64,3584]{1,0:T(8,128)(2,1)S(1)}, u32[]{:S(2)}, u32[]{:S(2)}) collective-permute-start(bf16[64,3584]{1,0:T(8,128)(2,1)} %bitcast.52), channel_id=1, source_target_pairs={{4,0},{8,4},{12,8},{16,12},{20,16},{24,20},{28,24},{5,1},{9,5},{13... | collective-permute-start | bytes 1376264 | tf_op jit(solution)/shard_map/ppermute | solution.py:332
  9.6 1.5 %collective-permute-start.6 = (bf16[40,1792]{1,0:T(8,128)(2,1)S(1)}, bf16[40,1792]{1,0:T(8,128)(2,1)S(1)}, u32[]{:S(2)}, u32[]{:S(2)}) collective-permute-start(bf16[40,1792]{1,0:T(8,128)(2,1)S(1)} %get-tuple-element.49), channel_id=1, source_target_pairs={{0,2},{1,3},{2,0},{3,1},{4,6},{5,7},{6,4},{7,5},{8,10},{9,11},{10,... | collective-permute-start | bytes 430088 | tf_op jit(solution)/shard_map/ppermute | solution.py:320
  11.1 1.4 %collective-permute-start.7 = (bf16[40,1792]{1,0:T(8,128)(2,1)S(1)}, bf16[40,1792]{1,0:T(8,128)(2,1)S(1)}, u32[]{:S(2)}, u32[]{:S(2)}) collective-permute-start(bf16[40,1792]{1,0:T(8,128)(2,1)S(1)} %get-tuple-element.50), channel_id=1, source_target_pairs={{0,3},{1,2},{2,1},{3,0},{4,7},{5,6},{6,5},{7,4},{8,11},{9,10},{10,... | collective-permute-start | bytes 430088 | tf_op jit(solution)/shard_map/ppermute | solution.py:320
  13.9 1.5 %collective-permute-start.3 = (bf16[2,40,1792]{2,1,0:T(8,128)(2,1)S(1)}, bf16[2,40,1792]{2,1,0:T(8,128)(2,1)S(1)}, u32[]{:S(2)}, u32[]{:S(2)}) collective-permute-start(bf16[2,40,1792]{2,1,0:T(8,128)(2,1)S(1)} %get-tuple-element.45), channel_id=1, source_target_pairs={{0,2},{1,3},{2,0},{3,1},{4,6},{5,7},{6,4},{7,5},{8,10},{9,11},{10,... | collective-permute-start | bytes 860168 | tf_op jit(solution)/shard_map/ppermute | solution.py:320
  16.8 4.2 %shard_map.115 = (bf16[1792,1024]{1,0:T(8,128)(2,1)S(1)}, bf16[1792,1024]{1,0:T(8,128)(2,1)S(1)}, bf16[1024,1792]{1,0:T(8,128)(2,1)S(1)}) custom-call(bf16[1792,1024]{1,0:T(8,128)(2,1)} %bitcast.55, bf16[1792,1024]{1,0:T(8,128)(2,1)} %bitcast.56, bf16[1024,1792]{1,0:T(8,128)(2,1)} %bitcast.57), custom_call_target="tpu_custom_call" | custom-call | bytes 22020096 | tf_op jit(solution)/shard_map/pallas_call | solution.py:23
  21.1 1.4 %shard_map.116 = (bf16[2,80,1024]{2,1,0:T(8,128)(2,1)S(1)}, bf16[2,80,1024]{2,1,0:T(8,128)(2,1)S(1)}) custom-call(bf16[40,1792]{1,0:T(8,128)(2,1)S(1)} %get-tuple-element.47.refs_0_, bf16[40,1792]{1,0:T(8,128)(2,1)S(1)} %collective-permute-done.5.refs_1_, bf16[40,1792]{1,0:T(8,128)(2,1)S(1)} %collective-permute-done.6.refs_2_, ...), custom_call_target="tpu_custom_call" | custom-call | flops 1174405120 | bytes 8568832 | tf_op jit(solution)/shard_map/pallas_call | solution.py:23
  22.5 1.9 %collective-permute-start.9 = (bf16[2,80,1024]{2,1,0:T(8,128)(2,1)S(1)}, bf16[2,80,1024]{2,1,0:T(8,128)(2,1)S(1)}, u32[]{:S(2)}, u32[]{:S(2)}) collective-permute-start(bf16[2,80,1024]{2,1,0:T(8,128)(2,1)S(1)} %get-tuple-element.57), channel_id=1, source_target_pairs={{0,1},{1,0},{2,3},{3,2},{4,5},{5,4},{6,7},{7,6},{8,9},{9,8},{10,11... | collective-permute-start | bytes 983048 | tf_op jit(solution)/shard_map/ppermute | solution.py:320
  24.9 6.0 %collective-permute-done.4.refs_3_ = bf16[2,40,1792]{2,1,0:T(8,128)(2,1)S(1)} collective-permute-done((bf16[2,40,1792]{2,1,0:T(8,128)(2,1)S(1)}, bf16[2,40,1792]{2,1,0:T(8,128)(2,1)S(1)}, u32[]{:S(2)}, u32[]{:S(2)}) %collective-permute-start.4) | collective-permute-done | bytes 286752 | tf_op jit(solution)/shard_map/ppermute | solution.py:320
  30.9 1.3 %shard_map.117 = (bf16[80,1024]{1,0:T(8,128)(2,1)S(1)}, bf16[80,1024]{1,0:T(8,128)(2,1)S(1)}) custom-call(bf16[40,1792]{1,0:T(8,128)(2,1)S(1)} %get-tuple-element.43.refs_0_, bf16[2,40,1792]{2,1,0:T(8,128)(2,1)S(1)} %collective-permute-done.2.refs_1_, bf16[2,40,1792]{2,1,0:T(8,128)(2,1)S(1)} %collective-permute-done.3.refs_2_, ...), custom_call_target="tpu_custom_call" | custom-call | flops 587202560 | bytes 5001216 | tf_op jit(solution)/shard_map/pallas_call | solution.py:23
  33.0 1.4 %shard_map.118 = (bf16[2,80,1024]{2,1,0:T(8,128)(2,1)S(1)}, bf16[2,80,1024]{2,1,0:T(8,128)(2,1)S(1)}) custom-call(bf16[40,1792]{1,0:T(8,128)(2,1)S(1)} %get-tuple-element.64.refs_0_, bf16[2,40,1792]{2,1,0:T(8,128)(2,1)S(1)} %collective-permute-done.2.refs_1_, bf16[2,40,1792]{2,1,0:T(8,128)(2,1)S(1)} %collective-permute-done.3.refs_2_, ...), custom_call_target="tpu_custom_call" | custom-call | flops 1174405120 | bytes 8998912 | tf_op jit(solution)/shard_map/pallas_call | solution.py:23
  34.4 1.4 %collective-permute-start.8 = (bf16[2,80,1024]{2,1,0:T(8,128)(2,1)S(1)}, bf16[2,80,1024]{2,1,0:T(8,128)(2,1)S(1)}, u32[]{:S(2)}, u32[]{:S(2)}) collective-permute-start(bf16[2,80,1024]{2,1,0:T(8,128)(2,1)S(1)} %get-tuple-element.66), channel_id=1, source_target_pairs={{0,1},{1,0},{2,3},{3,2},{4,5},{5,4},{6,7},{7,6},{8,9},{9,8},{10,11... | collective-permute-start | bytes 983048 | tf_op jit(solution)/shard_map/ppermute | solution.py:320
  37.1 3.5 %collective-permute-done.10 = bf16[80,1024]{1,0:T(8,128)(2,1)S(1)} collective-permute-done((bf16[80,1024]{1,0:T(8,128)(2,1)S(1)}, bf16[80,1024]{1,0:T(8,128)(2,1)S(1)}, u32[]{:S(2)}, u32[]{:S(2)}) %collective-permute-start.10) | collective-permute-done | bytes 163872 | tf_op jit(solution)/shard_map/ppermute | solution.py:320
  41.5 6.1 %collective-permute-done.8 = bf16[2,80,1024]{2,1,0:T(8,128)(2,1)S(1)} collective-permute-done((bf16[2,80,1024]{2,1,0:T(8,128)(2,1)S(1)}, bf16[2,80,1024]{2,1,0:T(8,128)(2,1)S(1)}, u32[]{:S(2)}, u32[]{:S(2)}) %collective-permute-start.8) | collective-permute-done | bytes 327712 | tf_op jit(solution)/shard_map/ppermute | solution.py:320
  48.4 6.2 %collective-permute-done.12.refs_1_ = bf16[2,80,1024]{2,1,0:T(8,128)(2,1)S(1)} collective-permute-done((bf16[2,80,1024]{2,1,0:T(8,128)(2,1)S(1)}, bf16[2,80,1024]{2,1,0:T(8,128)(2,1)S(1)}, u32[]{:S(2)}, u32[]{:S(2)}) %collective-permute-start.12) | collective-permute-done | bytes 327712 | tf_op jit(solution)/shard_map/ppermute | solution.py:320
  54.6 2.5 %shard_map.119 = (bf16[40,1792]{1,0:T(8,128)(2,1)S(1)}, bf16[40,1792]{1,0:T(8,128)(2,1)S(1)}, bf16[40,1792]{1,0:T(8,128)(2,1)S(1)}, bf16[40,1792]{1,0:T(8,128)(2,1)S(1)}) custom-call(bf16[2,80,1024]{2,1,0:T(8,128)(2,1)S(1)} %pad_maximum_fusion.refs_0_, bf16[2,80,1024]{2,1,0:T(8,128)(2,1)S(1)} %collective-permute-done.12.refs_1_, ...), custom_call_target="tpu_custom_call" | custom-call | flops 1174405120 | bytes 8568832 | tf_op jit(solution)/shard_map/pallas_call | solution.py:23
  57.8 1.5 %collective-permute-start.17 = (bf16[40,1792]{1,0:T(8,128)(2,1)S(1)}, bf16[40,1792]{1,0:T(8,128)(2,1)S(1)}, u32[]{:S(2)}, u32[]{:S(2)}) collective-permute-start(bf16[40,1792]{1,0:T(8,128)(2,1)S(1)} %get-tuple-element.72), channel_id=1, source_target_pairs={{0,2},{1,3},{2,0},{3,1},{4,6},{5,7},{6,4},{7,5},{8,10},{9,11},{10,... | collective-permute-start | bytes 430088 | tf_op jit(solution)/shard_map/ppermute | solution.py:320
  59.3 1.4 %collective-permute-start.18 = (bf16[40,1792]{1,0:T(8,128)(2,1)S(1)}, bf16[40,1792]{1,0:T(8,128)(2,1)S(1)}, u32[]{:S(2)}, u32[]{:S(2)}) collective-permute-start(bf16[40,1792]{1,0:T(8,128)(2,1)S(1)} %get-tuple-element.73), channel_id=1, source_target_pairs={{0,3},{1,2},{2,1},{3,0},{4,7},{5,6},{6,5},{7,4},{8,11},{9,10},{10,... | collective-permute-start | bytes 430088 | tf_op jit(solution)/shard_map/ppermute | solution.py:320
  62.1 1.5 %collective-permute-start.14 = (bf16[40,1792]{1,0:T(8,128)(2,1)S(1)}, bf16[40,1792]{1,0:T(8,128)(2,1)S(1)}, u32[]{:S(2)}, u32[]{:S(2)}) collective-permute-start(bf16[40,1792]{1,0:T(8,128)(2,1)S(1)} %get-tuple-element.77), channel_id=1, source_target_pairs={{0,2},{1,3},{2,0},{3,1},{4,6},{5,7},{6,4},{7,5},{8,10},{9,11},{10,... | collective-permute-start | bytes 430088 | tf_op jit(solution)/shard_map/ppermute | solution.py:320
  63.8 1.5 %collective-permute-start.15 = (bf16[40,1792]{1,0:T(8,128)(2,1)S(1)}, bf16[40,1792]{1,0:T(8,128)(2,1)S(1)}, u32[]{:S(2)}, u32[]{:S(2)}) collective-permute-start(bf16[40,1792]{1,0:T(8,128)(2,1)S(1)} %get-tuple-element.78), channel_id=1, source_target_pairs={{0,3},{1,2},{2,1},{3,0},{4,7},{5,6},{6,5},{7,4},{8,11},{9,10},{10,... | collective-permute-start | bytes 430088 | tf_op jit(solution)/shard_map/ppermute | solution.py:320
  65.3 2.4 %collective-permute-done.18.refs_5_ = bf16[40,1792]{1,0:T(8,128)(2,1)S(1)} collective-permute-done((bf16[40,1792]{1,0:T(8,128)(2,1)S(1)}, bf16[40,1792]{1,0:T(8,128)(2,1)S(1)}, u32[]{:S(2)}, u32[]{:S(2)}) %collective-permute-start.18) | collective-permute-done | bytes 143392 | tf_op jit(solution)/shard_map/ppermute | solution.py:320
  67.7 1.5 %shard_map.122 = bf16[64,3584]{1,0:T(8,128)(2,1)} custom-call(f32[4,64]{1,0:T(4,128)S(1)} %pad_maximum_fusion.1.refs_0_.ids, bf16[64,3584]{1,0:T(8,128)(2,1)S(1)} %get-tuple-element.79.refs_1_, bf16[40,1792]{1,0:T(8,128)(2,1)S(1)} %get-tuple-element.70.refs_2_, bf16[40,1792]{1,0:T(8,128)(2,1)S(1)} %collective-permute-done.16.refs_3_, ...), custom_call_target="tpu_custom_call" | custom-call | flops 36700160 | bytes 1491968 | tf_op jit(solution)/shard_map/pallas_call | solution.py:23
  70.0 3.4 %collective-permute-done.15.refs_5_ = bf16[40,1792]{1,0:T(8,128)(2,1)S(1)} collective-permute-done((bf16[40,1792]{1,0:T(8,128)(2,1)S(1)}, bf16[40,1792]{1,0:T(8,128)(2,1)S(1)}, u32[]{:S(2)}, u32[]{:S(2)}) %collective-permute-start.15) | collective-permute-done | bytes 143392 | tf_op jit(solution)/shard_map/ppermute | solution.py:320
  73.4 1.5 %shard_map.121 = bf16[64,3584]{1,0:T(8,128)(2,1)} custom-call(f32[4,64]{1,0:T(4,128)S(1)} %pad_maximum_fusion.1.refs_0_.ids, bf16[64,3584]{1,0:T(8,128)(2,1)S(1)} %get-tuple-element.41.refs_1_, bf16[40,1792]{1,0:T(8,128)(2,1)S(1)} %get-tuple-element.75.refs_2_, bf16[40,1792]{1,0:T(8,128)(2,1)S(1)} %collective-permute-done.13.refs_3_, ...), custom_call_target="tpu_custom_call" | custom-call | flops 36700160 | bytes 1491968 | tf_op jit(solution)/shard_map/pallas_call | solution.py:23
  (37 shorter events, 13.4 us)
Async XLA Ops:
  0.6 11.9 %collective-permute-start = (bf16[64,3584]{1,0:T(8,128)(2,1)}, bf16[64,3584]{1,0:T(8,128)(2,1)S(1)}, u32[]{:S(2)}, u32[]{:S(2)}) collective-permute-start(bf16[64,3584]{1,0:T(8,128)(2,1)} %bitcast.50), channel_id=1, source_target_pairs={{0,4},{4,8},{8,12},{12,16},{16,20},{20,24},{24,28},{1,5},{5,9},{9,... | collective-permute-start | bytes 1376264 | tf_op jit(solution)/shard_map/ppermute | solution.py:331
  2.6 10.0 %collective-permute-start.1 = (bf16[64,3584]{1,0:T(8,128)(2,1)}, bf16[64,3584]{1,0:T(8,128)(2,1)S(1)}, u32[]{:S(2)}, u32[]{:S(2)}) collective-permute-start(bf16[64,3584]{1,0:T(8,128)(2,1)} %bitcast.52), channel_id=1, source_target_pairs={{4,0},{8,4},{12,8},{16,12},{20,16},{24,20},{28,24},{5,1},{9,5},{13... | collective-permute-start | bytes 1376264 | tf_op jit(solution)/shard_map/ppermute | solution.py:332
  7.6 1.0 %copy-start.2 = (bf16[1,64,3584]{2,1,0:T(8,128)(2,1)S(1)}, bf16[1,64,3584]{2,1,0:T(8,128)(2,1)}, u32[]{:S(2)}) copy-start(bf16[1,64,3584]{2,1,0:T(8,128)(2,1)} %param.11) | copy-start | bytes 1376260
  8.6 4.0 %copy-start = (bf16[1,64,3584]{2,1,0:T(8,128)(2,1)S(1)}, bf16[1,64,3584]{2,1,0:T(8,128)(2,1)}, u32[]{:S(2)}) copy-start(bf16[1,64,3584]{2,1,0:T(8,128)(2,1)} %param.10) | copy-start | bytes 1376260
  8.6 4.0 %copy-start.1 = (bf16[1,64,3584]{2,1,0:T(8,128)(2,1)S(1)}, bf16[1,64,3584]{2,1,0:T(8,128)(2,1)}, u32[]{:S(2)}) copy-start(bf16[1,64,3584]{2,1,0:T(8,128)(2,1)} %param.12) | copy-start | bytes 1376260
  9.0 6.7 %collective-permute-start.5 = (bf16[40,1792]{1,0:T(8,128)(2,1)S(1)}, bf16[40,1792]{1,0:T(8,128)(2,1)S(1)}, u32[]{:S(2)}, u32[]{:S(2)}) collective-permute-start(bf16[40,1792]{1,0:T(8,128)(2,1)S(1)} %get-tuple-element.48), channel_id=1, source_target_pairs={{0,1},{1,0},{2,3},{3,2},{4,5},{5,4},{6,7},{7,6},{8,9},{9,8},{10,11... | collective-permute-start | bytes 430088 | tf_op jit(solution)/shard_map/ppermute | solution.py:320
  9.6 11.4 %collective-permute-start.6 = (bf16[40,1792]{1,0:T(8,128)(2,1)S(1)}, bf16[40,1792]{1,0:T(8,128)(2,1)S(1)}, u32[]{:S(2)}, u32[]{:S(2)}) collective-permute-start(bf16[40,1792]{1,0:T(8,128)(2,1)S(1)} %get-tuple-element.49), channel_id=1, source_target_pairs={{0,2},{1,3},{2,0},{3,1},{4,6},{5,7},{6,4},{7,5},{8,10},{9,11},{10,... | collective-permute-start | bytes 430088 | tf_op jit(solution)/shard_map/ppermute | solution.py:320
  11.1 9.9 %collective-permute-start.7 = (bf16[40,1792]{1,0:T(8,128)(2,1)S(1)}, bf16[40,1792]{1,0:T(8,128)(2,1)S(1)}, u32[]{:S(2)}, u32[]{:S(2)}) collective-permute-start(bf16[40,1792]{1,0:T(8,128)(2,1)S(1)} %get-tuple-element.50), channel_id=1, source_target_pairs={{0,3},{1,2},{2,1},{3,0},{4,7},{5,6},{6,5},{7,4},{8,11},{9,10},{10,... | collective-permute-start | bytes 430088 | tf_op jit(solution)/shard_map/ppermute | solution.py:320
  13.3 11.1 %collective-permute-start.2 = (bf16[2,40,1792]{2,1,0:T(8,128)(2,1)S(1)}, bf16[2,40,1792]{2,1,0:T(8,128)(2,1)S(1)}, u32[]{:S(2)}, u32[]{:S(2)}) collective-permute-start(bf16[2,40,1792]{2,1,0:T(8,128)(2,1)S(1)} %get-tuple-element.44), channel_id=1, source_target_pairs={{0,1},{1,0},{2,3},{3,2},{4,5},{5,4},{6,7},{7,6},{8,9},{9,8},{10,11... | collective-permute-start | bytes 860168 | tf_op jit(solution)/shard_map/ppermute | solution.py:320
  13.9 11.0 %collective-permute-start.3 = (bf16[2,40,1792]{2,1,0:T(8,128)(2,1)S(1)}, bf16[2,40,1792]{2,1,0:T(8,128)(2,1)S(1)}, u32[]{:S(2)}, u32[]{:S(2)}) collective-permute-start(bf16[2,40,1792]{2,1,0:T(8,128)(2,1)S(1)} %get-tuple-element.45), channel_id=1, source_target_pairs={{0,2},{1,3},{2,0},{3,1},{4,6},{5,7},{6,4},{7,5},{8,10},{9,11},{10,... | collective-permute-start | bytes 860168 | tf_op jit(solution)/shard_map/ppermute | solution.py:320
  15.7 15.2 %collective-permute-start.4 = (bf16[2,40,1792]{2,1,0:T(8,128)(2,1)S(1)}, bf16[2,40,1792]{2,1,0:T(8,128)(2,1)S(1)}, u32[]{:S(2)}, u32[]{:S(2)}) collective-permute-start(bf16[2,40,1792]{2,1,0:T(8,128)(2,1)S(1)} %get-tuple-element.46), channel_id=1, source_target_pairs={{0,3},{1,2},{2,1},{3,0},{4,7},{5,6},{6,5},{7,4},{8,11},{9,10},{10,... | collective-permute-start | bytes 860168 | tf_op jit(solution)/shard_map/ppermute | solution.py:320
  22.5 14.6 %collective-permute-start.9 = (bf16[2,80,1024]{2,1,0:T(8,128)(2,1)S(1)}, bf16[2,80,1024]{2,1,0:T(8,128)(2,1)S(1)}, u32[]{:S(2)}, u32[]{:S(2)}) collective-permute-start(bf16[2,80,1024]{2,1,0:T(8,128)(2,1)S(1)} %get-tuple-element.57), channel_id=1, source_target_pairs={{0,1},{1,0},{2,3},{3,2},{4,5},{5,4},{6,7},{7,6},{8,9},{9,8},{10,11... | collective-permute-start | bytes 983048 | tf_op jit(solution)/shard_map/ppermute | solution.py:320
  32.2 8.4 %collective-permute-start.10 = (bf16[80,1024]{1,0:T(8,128)(2,1)S(1)}, bf16[80,1024]{1,0:T(8,128)(2,1)S(1)}, u32[]{:S(2)}, u32[]{:S(2)}) collective-permute-start(bf16[80,1024]{1,0:T(8,128)(2,1)S(1)} %get-tuple-element.63), channel_id=1, source_target_pairs={{0,1},{1,0},{2,3},{3,2},{4,5},{5,4},{6,7},{7,6},{8,9},{9,8},{10,11... | collective-permute-start | bytes 491528 | tf_op jit(solution)/shard_map/ppermute | solution.py:320
  34.4 13.2 %collective-permute-start.8 = (bf16[2,80,1024]{2,1,0:T(8,128)(2,1)S(1)}, bf16[2,80,1024]{2,1,0:T(8,128)(2,1)S(1)}, u32[]{:S(2)}, u32[]{:S(2)}) collective-permute-start(bf16[2,80,1024]{2,1,0:T(8,128)(2,1)S(1)} %get-tuple-element.66), channel_id=1, source_target_pairs={{0,1},{1,0},{2,3},{3,2},{4,5},{5,4},{6,7},{7,6},{8,9},{9,8},{10,11... | collective-permute-start | bytes 983048 | tf_op jit(solution)/shard_map/ppermute | solution.py:320
  40.9 13.7 %collective-permute-start.12 = (bf16[2,80,1024]{2,1,0:T(8,128)(2,1)S(1)}, bf16[2,80,1024]{2,1,0:T(8,128)(2,1)S(1)}, u32[]{:S(2)}, u32[]{:S(2)}) collective-permute-start(bf16[2,80,1024]{2,1,0:T(8,128)(2,1)S(1)} %pad_maximum_fusion.refs_0_), channel_id=1, source_target_pairs={{0,1},{1,0},{2,3},{3,2},{4,5},{5,4},{6,7},{7,6},{8,9},{9,8},{10,11... | collective-permute-start | bytes 983048 | tf_op jit(solution)/shard_map/ppermute | solution.py:320
  47.8 12.9 %collective-permute-start.11 = (bf16[80,1024]{1,0:T(8,128)(2,1)S(1)}, bf16[80,1024]{1,0:T(8,128)(2,1)S(1)}, u32[]{:S(2)}, u32[]{:S(2)}) collective-permute-start(bf16[80,1024]{1,0:T(8,128)(2,1)S(1)} %fusion.1.refs_0_), channel_id=1, source_target_pairs={{0,1},{1,0},{2,3},{3,2},{4,5},{5,4},{6,7},{7,6},{8,9},{9,8},{10,11... | collective-permute-start | bytes 491528 | tf_op jit(solution)/shard_map/ppermute | solution.py:320
  57.1 6.6 %collective-permute-start.16 = (bf16[40,1792]{1,0:T(8,128)(2,1)S(1)}, bf16[40,1792]{1,0:T(8,128)(2,1)S(1)}, u32[]{:S(2)}, u32[]{:S(2)}) collective-permute-start(bf16[40,1792]{1,0:T(8,128)(2,1)S(1)} %get-tuple-element.71), channel_id=1, source_target_pairs={{0,1},{1,0},{2,3},{3,2},{4,5},{5,4},{6,7},{7,6},{8,9},{9,8},{10,11... | collective-permute-start | bytes 430088 | tf_op jit(solution)/shard_map/ppermute | solution.py:320
  57.8 7.5 %collective-permute-start.17 = (bf16[40,1792]{1,0:T(8,128)(2,1)S(1)}, bf16[40,1792]{1,0:T(8,128)(2,1)S(1)}, u32[]{:S(2)}, u32[]{:S(2)}) collective-permute-start(bf16[40,1792]{1,0:T(8,128)(2,1)S(1)} %get-tuple-element.72), channel_id=1, source_target_pairs={{0,2},{1,3},{2,0},{3,1},{4,6},{5,7},{6,4},{7,5},{8,10},{9,11},{10,... | collective-permute-start | bytes 430088 | tf_op jit(solution)/shard_map/ppermute | solution.py:320
  59.3 8.5 %collective-permute-start.18 = (bf16[40,1792]{1,0:T(8,128)(2,1)S(1)}, bf16[40,1792]{1,0:T(8,128)(2,1)S(1)}, u32[]{:S(2)}, u32[]{:S(2)}) collective-permute-start(bf16[40,1792]{1,0:T(8,128)(2,1)S(1)} %get-tuple-element.73), channel_id=1, source_target_pairs={{0,3},{1,2},{2,1},{3,0},{4,7},{5,6},{6,5},{7,4},{8,11},{9,10},{10,... | collective-permute-start | bytes 430088 | tf_op jit(solution)/shard_map/ppermute | solution.py:320
  61.5 8.5 %collective-permute-start.13 = (bf16[40,1792]{1,0:T(8,128)(2,1)S(1)}, bf16[40,1792]{1,0:T(8,128)(2,1)S(1)}, u32[]{:S(2)}, u32[]{:S(2)}) collective-permute-start(bf16[40,1792]{1,0:T(8,128)(2,1)S(1)} %get-tuple-element.76), channel_id=1, source_target_pairs={{0,1},{1,0},{2,3},{3,2},{4,5},{5,4},{6,7},{7,6},{8,9},{9,8},{10,11... | collective-permute-start | bytes 430088 | tf_op jit(solution)/shard_map/ppermute | solution.py:320
  62.1 7.9 %collective-permute-start.14 = (bf16[40,1792]{1,0:T(8,128)(2,1)S(1)}, bf16[40,1792]{1,0:T(8,128)(2,1)S(1)}, u32[]{:S(2)}, u32[]{:S(2)}) collective-permute-start(bf16[40,1792]{1,0:T(8,128)(2,1)S(1)} %get-tuple-element.77), channel_id=1, source_target_pairs={{0,2},{1,3},{2,0},{3,1},{4,6},{5,7},{6,4},{7,5},{8,10},{9,11},{10,... | collective-permute-start | bytes 430088 | tf_op jit(solution)/shard_map/ppermute | solution.py:320
  63.8 9.6 %collective-permute-start.15 = (bf16[40,1792]{1,0:T(8,128)(2,1)S(1)}, bf16[40,1792]{1,0:T(8,128)(2,1)S(1)}, u32[]{:S(2)}, u32[]{:S(2)}) collective-permute-start(bf16[40,1792]{1,0:T(8,128)(2,1)S(1)} %get-tuple-element.78), channel_id=1, source_target_pairs={{0,3},{1,2},{2,1},{3,0},{4,7},{5,6},{6,5},{7,4},{8,11},{9,10},{10,... | collective-permute-start | bytes 430088 | tf_op jit(solution)/shard_map/ppermute | solution.py:320

commit v3 on v2

--- a/solution.py
+++ b/solution.py
@@ -12,20 +12,19 @@
 BF16 = jnp.bfloat16
 F32 = jnp.float32
 VMEM_LIMIT = 40 * 1024 * 1024
-FWD_IDS, BWD_IDS, FWD_GATES, BWD_GATES = (slice(i, i + 1) for i in range(4))
-
-
-def kernel_call(kernel, out_shape, inputs, flops, left=0, copies=0):
+APPARENT = 150
+FWD_IDS, BWD_IDS = slice(0, 1), slice(1, 2)
+
+
+def kernel_call(kernel, out_shape, inputs, flops):
     whole = pl.BlockSpec(memory_space=pltpu.VMEM)
-    outside = pl.BlockSpec(memory_space=pltpu.HBM)
     outs = jax.tree.leaves(out_shape)
     moved = sum(v.size * v.dtype.itemsize for v in (*inputs, *outs))
     return pl.pallas_call(
         kernel,
         out_shape=out_shape,
-        in_specs=[outside] * left + [whole] * (len(inputs) - left),
+        in_specs=[whole] * len(inputs),
         out_specs=jax.tree.map(lambda _: whole, out_shape),
-        scratch_shapes=[pltpu.SemaphoreType.DMA((copies,))] * (copies > 0),
         compiler_params=pltpu.CompilerParams(vmem_limit_bytes=VMEM_LIMIT),
         cost_estimate=pl.CostEstimate(flops=flops, bytes_accessed=moved, transcendentals=0),
     )(*inputs)
@@ -55,17 +54,6 @@
     return index // group, lax.rem(index, group)
 
 
-def fetch(sources, targets, sems):
-    copies = [
-        pltpu.make_async_copy(source, target, sems.at[i])
-        for i, (source, target) in enumerate(zip(sources, targets))
-    ]
-    for copy in copies:
-        copy.start()
-    for copy in copies:
-        copy.wait()
-
-
 def home_slots_kernel(group, x, ids, *outs):
     expert, own_slice = position(group)
     table = tables(ids[...][BWD_IDS], expert)
@@ -88,34 +76,21 @@
         functools.partial(home_slots_kernel, group),
         (out,) * (2 * group),
         (x, routing),
-        4 * CAP * tokens * model * 80,
-    )
-
-
-def stage_kernel(count, *refs):
-    fetch(refs[:count], refs[count : 2 * count], refs[-1])
-
-
-def staged(arrays):
-    count = len(arrays)
-    return kernel_call(
-        functools.partial(stage_kernel, count),
-        tuple(like(v.shape) for v in arrays),
-        arrays,
-        0,
-        left=count,
-        copies=count,
+        4 * CAP * tokens * model * APPARENT,
     )
 
 
 def stream_slots_kernel(group, last, *refs):
-    routing, x_kept, g_kept, x_here, g_here, *outs = refs
+    routing, near_sent, near, far, *outs = refs
     section_x, section_g, x_own, g_own, *sent = outs
     section = lax.axis_index("pipe")
     expert, own_slice = position(group)
-    width = x_here.shape[1] // group
-    section_x[...] = jnp.where(section == 0, x_kept[...], x_here[...])
-    section_g[...] = jnp.where(section == last, g_kept[...], g_here[...])
+    width = near.shape[1] // group
+    even = lax.rem(section, 2) == 0
+    edge = (section == 0) | (section == last)
+    from_far = jnp.where(edge, near_sent[...], far[...])
+    section_x[...] = jnp.where(even, from_far, near[...])
+    section_g[...] = jnp.where(even, near[...], from_far)
     small = routing[...]
     streams = (
         (tables(small[FWD_IDS], expert), section_x, x_own),
@@ -137,15 +112,15 @@
                     sent[group - 1 + r][k] = other
 
 
-def stream_slots(routing, x_kept, g_kept, x_here, g_here, group, last):
-    tokens, model = x_here.shape
+def stream_slots(routing, near_sent, near, far, group, last):
+    tokens, model = near.shape
     width = model // group
-    whole, one, two = like(x_here.shape), like((CAP, width)), like((2, CAP, width))
+    whole, one, two = like(near.shape), like((CAP, width)), like((2, CAP, width))
     return kernel_call(
         functools.partial(stream_slots_kernel, group, last),
         (whole, whole, one, one) + (two,) * (2 * group - 1),
-        (routing, x_kept, g_kept, x_here, g_here),
-        8 * CAP * tokens * model,
+        (routing, near_sent, near, far),
+        8 * CAP * tokens * model * APPARENT,
     )
 
 
@@ -161,7 +136,7 @@
 
 
 def tile_of(extent):
-    return next(t for t in (512, 256, extent) if extent % t == 0)
+    return next(t for t in (512, 896, 256, extent) if extent % t == 0)
 
 
 def gathered(refs, stream):
@@ -246,30 +221,46 @@
     )
 
 
-def back_kernel(group, *refs):
-    gs, (gate, up, *outs) = refs[:group], refs[group:]
-    grads_gate = jnp.concatenate([g[0] for g in gs], axis=0)
-    grads_up = jnp.concatenate([g[1] for g in gs], axis=0)
-    width = gate.shape[0]
+def back_kernel(group, first, *refs):
+    gs, (mat, *rest) = refs[:group], refs[group:]
+    outs = rest if first else rest[1:]
+    rows = jnp.concatenate([g[...] for g in gs], axis=0)
+    width = mat.shape[0]
     tile = tile_of(width)
     for at in range(0, width, tile):
-        acc = dot_nt(grads_gate, gate[at : at + tile, :]) + dot_nt(grads_up, up[at : at + tile, :])
-        put_blocks(acc.astype(BF16), group, outs, at, tile)
-
-
-def back_rows(gs, gate, up):
+        acc = dot_nt(mat[at : at + tile, :], rows)
+        if first:
+            outs[0][at : at + tile, :] = acc
+        else:
+            total = (acc + rest[0][at : at + tile, :]).T
+            put_blocks(total.astype(BF16), group, outs, at, tile)
+
+
+def back_half(gs, mat):
     group = len(gs)
-    width, hidden = gate.shape
-    return kernel_call(
-        functools.partial(back_kernel, group),
+    width, hidden = mat.shape
+    rows = gs[0].shape[0] * group
+    return kernel_call(
+        functools.partial(back_kernel, group, True),
+        (jax.ShapeDtypeStruct((width, rows), F32),),
+        (*gs, mat),
+        2 * rows * hidden * width,
+    )[0]
+
+
+def back_rows(gs, mat, half):
+    group = len(gs)
+    width, hidden = mat.shape
+    return kernel_call(
+        functools.partial(back_kernel, group, False),
         (like((CAP, width)),) * (2 * group),
-        (*gs, gate, up),
-        8 * group * CAP * hidden * width,
-    )
-
-
-def combine_kernel(group, ids, gates, *refs):
-    routing, base, *rest = refs
+        (*gs, mat, half),
+        4 * group * CAP * hidden * width,
+    )
+
+
+def combine_kernel(group, ids, *refs):
+    routing, gates, base, *rest = refs
     small = routing[...]
     same, other, out = rest[:group], rest[group : 2 * group], rest[2 * group]
     expert, own_slice = position(group)
@@ -278,7 +269,7 @@
     width = same[0].shape[1]
     row = lax.broadcasted_iota(jnp.int32, (tokens, tokens), 0)
     col = lax.broadcasted_iota(jnp.int32, (tokens, tokens), 1)
-    weight = jnp.sum(jnp.where(row == col, small[gates], 0.0), axis=1, keepdims=True)
+    weight = jnp.sum(jnp.where(row == col, gates[...], 0.0), axis=1, keepdims=True)
     contract = (((0,), (0,)), ((), ()))
     for r in range(group):
         blocks = jnp.concatenate([same[r][...], other[r][...]], axis=0)
@@ -296,9 +287,9 @@
 def combine(routing, ids, gates, base, same, other):
     group = len(same)
     return kernel_call(
-        functools.partial(combine_kernel, group, ids, gates),
+        functools.partial(combine_kernel, group, ids),
         like(base.shape),
-        (routing, base, *same, *other),
+        (routing, gates, base, *same, *other),
         4 * CAP * base.shape[0] * base.shape[1],
     )
 
@@ -319,24 +310,29 @@
     def to_partner(value, mask):
         return lax.ppermute(value, "expert", [(i, i ^ mask) for i in range(devices)])
 
-    first, last = 0, sections - 1
+    last = sections - 1
     fwd_in, bwd_in, bwd_grad_in = fwd_in[0], bwd_in[0], bwd_grad_in[0]
-    small = (fwd_ids, bwd_ids, fwd_gates, bwd_gates)
-    routing = jnp.concatenate([v.reshape(1, tokens).astype(F32) for v in small], axis=0)
+    routing = jnp.concatenate([fwd_ids.reshape(1, tokens), bwd_ids.reshape(1, tokens)], axis=0)
+    fwd_gates, bwd_gates = fwd_gates.reshape(1, tokens), bwd_gates.reshape(1, tokens)
 
     def sent(rows):
         return [to_partner(v, r) for r, v in enumerate(rows, 1)]
 
-    steps = [(p, p + 1) for p in range(last)]
-    x_here = lax.ppermute(fwd_in, "pipe", steps)
-    g_here = lax.ppermute(bwd_grad_in, "pipe", [(b, a) for a, b in steps])
+    even = lax.rem(section, 2) == 0
+    near_sent = jnp.where(even, fwd_in, bwd_grad_in)
+    far_sent = jnp.where(even, bwd_grad_in, fwd_in)
+    bwd_in = jnp.where(section < sections, bwd_in, fwd_in)
+    swaps = [[(p, p + 1) for p in range(start, last, 2)] for start in (0, 1)]
+    near, far = (
+        lax.ppermute(value, "pipe", pairs + [(b, a) for a, b in pairs])
+        for value, pairs in zip((near_sent, far_sent), swaps)
+    )
     saved_own, *saved = home_slots(bwd_in, routing, group)
     saved_rows = [saved_own, *sent(saved)]
     section_x, section_g, x_own, g_own, *streams = stream_slots(
-        routing, fwd_in, bwd_grad_in, x_here, g_here, group, last
+        routing, near_sent, near, far, group, last
     )
     stream_rows = sent(streams)
-    gate, up, down = staged(after((gate, up, down), streams))
 
     def summed(own, arrived):
         total = own.astype(F32)
@@ -357,11 +353,12 @@
     grad_hidden = summed(g_parts[0], g_sent)
     sig = jax.nn.sigmoid(back[0])
     grad_gate = grad_hidden * back[1] * sig * (1.0 + back[0] * (1.0 - sig))
-    grad_up = grad_hidden * (back[0] * sig)
-    grads = jnp.stack([grad_gate.astype(BF16), grad_up.astype(BF16)])
-    grads_sent = sent([grads] * (group - 1))
-
-    x_sent = after(x_sent, grads)
+    grad_up = after(grad_hidden, grad_gate) * (back[0] * sig)
+    grad_gate, grad_up = grad_gate.astype(BF16), grad_up.astype(BF16)
+    gate_sent = sent([grad_gate] * (group - 1))
+    up_sent = sent([grad_up] * (group - 1))
+
+    x_sent = after(x_sent, grad_up)
     ahead = summed(x_parts[0], x_sent)
     hidden = (jax.nn.silu(ahead[0]) * ahead[1]).astype(BF16)
     hidden_sent = sent([hidden] * (group - 1))
@@ -370,12 +367,13 @@
         rows = sent(blocks[1:])
         return [blocks[0], *rows[: group - 1]], rows[group - 1 :]
 
-    bwd_rows = back_rows([grads, *grads_sent], gate, up)
+    half = back_half([grad_gate, *gate_sent], gate)
+    bwd_rows = back_rows([grad_up, *after(up_sent, half)], up, half)
     bwd_same, bwd_other = returned(bwd_rows)
     hidden_sent = after(hidden_sent, bwd_rows)
     fwd_same, fwd_other = returned(down_rows([hidden, *hidden_sent], down))
-    bwd_out = combine(routing, BWD_IDS, BWD_GATES, section_g, bwd_same, bwd_other)
-    fwd_out = combine(routing, FWD_IDS, FWD_GATES, section_x, fwd_same, fwd_other)
+    bwd_out = combine(routing, BWD_IDS, bwd_gates, section_g, bwd_same, bwd_other)
+    fwd_out = combine(routing, FWD_IDS, fwd_gates, section_x, fwd_same, fwd_other)
     return (fwd_out[None], bwd_out[None])
 
 

time: 75.6 us -> 72 us (0.952)
  Pallas kernels: 15.7 us -> 11.4 us
  waiting for transfers between devices: 30.7 us -> 33.9 us
  starting transfers between devices: 24.9 us -> 22.7 us
  local copies, waits for them, and re-layouts: 1.02 us -> 0.02 us
  other arithmetic: 1.84 us -> 2.64 us
    pallas_call x10, Pallas kernels: 15.7 us -> 11.4 us  [kernel_call(): pl.pallas_call(kernel, out_shape=out_shape, in_specs=[whole] * len(inputs...]
    ppermute x2, starting transfers between devices: 5.57 us -> 2.52 us  [body(): lax.ppermute(value, 'pipe', pairs + [(b, a) for a, b in pairs])]
    ppermute x2, waiting for transfers between devices: 0.01 us -> 2.68 us  [body(): lax.ppermute(value, 'pipe', pairs + [(b, a) for a, b in pairs])]
    select_n x0 -> x1, other arithmetic: none -> 1.39 us  [body(): far_sent = jnp.where(even, bwd_grad_in, fwd_in)]
    unnamed x6 -> x10, local copies, waits for them, and re-layouts: 1.02 us -> 0.02 us
    ppermute x17 -> x18, starting transfers between devices: 19.3 us -> 20.2 us  [to_partner(): lax.ppermute(value, 'expert', [(i, i ^ mask) for i in range(devices)])]
    ppermute x17 -> x18, waiting for transfers between devices: 30.7 us -> 31.3 us  [to_partner(): lax.ppermute(value, 'expert', [(i, i ^ mask) for i in range(devices)])]
  transfers between devices with their start and end apart: 19 -> 20, of which waited for: 11 -> 14; matrix products, arithmetic and copies ran while one was open for 2% -> 2% of each run, Pallas kernels for 19% -> 14%
where the time goes in v3:
time: 72 us; the launch traced here: 71.5 us
  waiting for transfers between devices  33.9 us (47%)
  starting transfers between devices  22.7 us (32%)
  Pallas kernels  11.4 us (16%)
  other arithmetic  2.64 us (4%)
  between operations  0.78 us (1%)
    ppermute x18, waiting for transfers between devices, to_partner(): lax.ppermute(value, 'expert', [(i, i ^ mask) for i in range(devices)])  31.3 us
    ppermute x18, starting transfers between devices, to_partner(): lax.ppermute(value, 'expert', [(i, i ^ mask) for i in range(devices)])  20.2 us
    pallas_call x10, Pallas kernels, kernel_call(): pl.pallas_call(kernel, out_shape=out_shape, in_specs=[whole] * len(inputs...  11.4 us
    ppermute x2, waiting for transfers between devices, body(): lax.ppermute(value, 'pipe', pairs + [(b, a) for a, b in pairs])  2.68 us
    ppermute x2, starting transfers between devices, body(): lax.ppermute(value, 'pipe', pairs + [(b, a) for a, b in pairs])  2.52 us
  transfers between devices with their start and end apart: 20, of which 14 were waited for; matrix products, arithmetic and copies ran while one was open for 2% of the time, Pallas kernels for 14%

profile of v3, /device:TPU:18, one launch (start us, length us, event | category | flops | bytes accessed | tf_op | source)
XLA Modules:
  0.0 71.5 jit_solution(8557296714000079984)
XLA Ops:
  0.6 1.4 %select_bitcast_fusion.1 = (bf16[64,3584]{1,0:T(8,128)(2,1)S(1)}, bf16[64,3584]{1,0:T(8,128)(2,1)S(1)}, bf16[64,3584]{1,0:T(8,128)(2,1)S(1)}) fusion(bf16[1,64,3584]{2,1,0:T(8,128)(2,1)} %param.12, bf16[1,64,3584]{2,1,0:T(8,128)(2,1)} %param.10, pred[]{:T(512)S(6)} %eq.3, bf16[1,64,3584]{2,1,0:T(8,128)(2,1)} %param.11, pred[]{:T(512)S(6)} %lt.3), kind=kLoop, calls=%fused_computation.3 | loop fusion | flops 688128 | bytes 2752514 | tf_op jit(solution)/shard_map/jit(_where)/select_n | solution.py:323
  2.1 2.4 %collective-permute-start.1 = (bf16[64,3584]{1,0:T(8,128)(2,1)S(1)}, bf16[64,3584]{1,0:T(8,128)(2,1)S(1)}, u32[]{:S(2)}, u32[]{:S(2)}) collective-permute-start(bf16[64,3584]{1,0:T(8,128)(2,1)S(1)} %get-tuple-element.72), channel_id=1, source_target_pairs={{4,8},{12,16},{20,24},{8,4},{16,12},{24,20},{5,9},{13,17},{21,25},... | collective-permute-start | bytes 1376264 | tf_op jit(solution)/shard_map/ppermute | solution.py:327
  6.3 1.5 %collective-permute-start.6 = (bf16[40,1792]{1,0:T(8,128)(2,1)S(1)}, bf16[40,1792]{1,0:T(8,128)(2,1)S(1)}, u32[]{:S(2)}, u32[]{:S(2)}) collective-permute-start(bf16[40,1792]{1,0:T(8,128)(2,1)S(1)} %get-tuple-element.45), channel_id=1, source_target_pairs={{0,2},{1,3},{2,0},{3,1},{4,6},{5,7},{6,4},{7,5},{8,10},{9,11},{10,... | collective-permute-start | bytes 430088 | tf_op jit(solution)/shard_map/ppermute | solution.py:311
  7.8 1.4 %collective-permute-start.7 = (bf16[40,1792]{1,0:T(8,128)(2,1)S(1)}, bf16[40,1792]{1,0:T(8,128)(2,1)S(1)}, u32[]{:S(2)}, u32[]{:S(2)}) collective-permute-start(bf16[40,1792]{1,0:T(8,128)(2,1)S(1)} %get-tuple-element.46), channel_id=1, source_target_pairs={{0,3},{1,2},{2,1},{3,0},{4,7},{5,6},{6,5},{7,4},{8,11},{9,10},{10,... | collective-permute-start | bytes 430088 | tf_op jit(solution)/shard_map/ppermute | solution.py:311
  9.2 2.7 %collective-permute-done.1.refs_3_ = bf16[64,3584]{1,0:T(8,128)(2,1)S(1)} collective-permute-done((bf16[64,3584]{1,0:T(8,128)(2,1)S(1)}, bf16[64,3584]{1,0:T(8,128)(2,1)S(1)}, u32[]{:S(2)}, u32[]{:S(2)}) %collective-permute-start.1) | collective-permute-done | bytes 458784 | tf_op jit(solution)/shard_map/ppermute | solution.py:327
  13.2 1.5 %collective-permute-start.3 = (bf16[2,40,1792]{2,1,0:T(8,128)(2,1)S(1)}, bf16[2,40,1792]{2,1,0:T(8,128)(2,1)S(1)}, u32[]{:S(2)}, u32[]{:S(2)}) collective-permute-start(bf16[2,40,1792]{2,1,0:T(8,128)(2,1)S(1)} %get-tuple-element.41), channel_id=1, source_target_pairs={{0,2},{1,3},{2,0},{3,1},{4,6},{5,7},{6,4},{7,5},{8,10},{9,11},{10,... | collective-permute-start | bytes 860168 | tf_op jit(solution)/shard_map/ppermute | solution.py:311
  14.7 1.4 %collective-permute-start.4 = (bf16[2,40,1792]{2,1,0:T(8,128)(2,1)S(1)}, bf16[2,40,1792]{2,1,0:T(8,128)(2,1)S(1)}, u32[]{:S(2)}, u32[]{:S(2)}) collective-permute-start(bf16[2,40,1792]{2,1,0:T(8,128)(2,1)S(1)} %get-tuple-element.42), channel_id=1, source_target_pairs={{0,3},{1,2},{2,1},{3,0},{4,7},{5,6},{6,5},{7,4},{8,11},{9,10},{10,... | collective-permute-start | bytes 860168 | tf_op jit(solution)/shard_map/ppermute | solution.py:311
  16.2 1.4 %shard_map.115 = (bf16[2,80,1024]{2,1,0:T(8,128)(2,1)S(1)}, bf16[2,80,1024]{2,1,0:T(8,128)(2,1)S(1)}) custom-call(bf16[40,1792]{1,0:T(8,128)(2,1)S(1)} %get-tuple-element.43.refs_0_, bf16[40,1792]{1,0:T(8,128)(2,1)S(1)} %collective-permute-done.5.refs_1_, bf16[40,1792]{1,0:T(8,128)(2,1)S(1)} %collective-permute-done.6.refs_2_, ...), custom_call_target="tpu_custom_call" | custom-call | flops 1174405120 | bytes 8568832 | tf_op jit(solution)/shard_map/pallas_call | solution.py:23
  18.9 3.5 %collective-permute-done.2.refs_1_ = bf16[2,40,1792]{2,1,0:T(8,128)(2,1)S(1)} collective-permute-done((bf16[2,40,1792]{2,1,0:T(8,128)(2,1)S(1)}, bf16[2,40,1792]{2,1,0:T(8,128)(2,1)S(1)}, u32[]{:S(2)}, u32[]{:S(2)}) %collective-permute-start.2) | collective-permute-done | bytes 286752 | tf_op jit(solution)/shard_map/ppermute | solution.py:311
  22.4 5.2 %collective-permute-done.3.refs_2_ = bf16[2,40,1792]{2,1,0:T(8,128)(2,1)S(1)} collective-permute-done((bf16[2,40,1792]{2,1,0:T(8,128)(2,1)S(1)}, bf16[2,40,1792]{2,1,0:T(8,128)(2,1)S(1)}, u32[]{:S(2)}, u32[]{:S(2)}) %collective-permute-start.3) | collective-permute-done | bytes 286752 | tf_op jit(solution)/shard_map/ppermute | solution.py:311
  27.6 1.9 %collective-permute-done.4.refs_3_ = bf16[2,40,1792]{2,1,0:T(8,128)(2,1)S(1)} collective-permute-done((bf16[2,40,1792]{2,1,0:T(8,128)(2,1)S(1)}, bf16[2,40,1792]{2,1,0:T(8,128)(2,1)S(1)}, u32[]{:S(2)}, u32[]{:S(2)}) %collective-permute-start.4) | collective-permute-done | bytes 286752 | tf_op jit(solution)/shard_map/ppermute | solution.py:311
  32.9 1.5 %collective-permute-start.8 = (bf16[2,80,1024]{2,1,0:T(8,128)(2,1)S(1)}, bf16[2,80,1024]{2,1,0:T(8,128)(2,1)S(1)}, u32[]{:S(2)}, u32[]{:S(2)}) collective-permute-start(bf16[2,80,1024]{2,1,0:T(8,128)(2,1)S(1)} %get-tuple-element.56), channel_id=1, source_target_pairs={{0,1},{1,0},{2,3},{3,2},{4,5},{5,4},{6,7},{7,6},{8,9},{9,8},{10,11... | collective-permute-start | bytes 983048 | tf_op jit(solution)/shard_map/ppermute | solution.py:311
  35.6 3.5 %collective-permute-done.10 = bf16[80,1024]{1,0:T(8,128)(2,1)S(1)} collective-permute-done((bf16[80,1024]{1,0:T(8,128)(2,1)S(1)}, bf16[80,1024]{1,0:T(8,128)(2,1)S(1)}, u32[]{:S(2)}, u32[]{:S(2)}) %collective-permute-start.10) | collective-permute-done | bytes 163872 | tf_op jit(solution)/shard_map/ppermute | solution.py:311
  40.1 1.6 %collective-permute-start.12 = (bf16[80,1024]{1,0:T(8,128)(2,1)S(1)}, bf16[80,1024]{1,0:T(8,128)(2,1)S(1)}, u32[]{:S(2)}, u32[]{:S(2)}) collective-permute-start(bf16[80,1024]{1,0:T(8,128)(2,1)S(1)} %multiply_convert_fusion.refs_0_), channel_id=1, source_target_pairs={{0,1},{1,0},{2,3},{3,2},{4,5},{5,4},{6,7},{7,6},{8,9},{9,8},{10,11... | collective-permute-start | bytes 491528 | tf_op jit(solution)/shard_map/ppermute | solution.py:311
  41.7 4.5 %collective-permute-done.8 = bf16[2,80,1024]{2,1,0:T(8,128)(2,1)S(1)} collective-permute-done((bf16[2,80,1024]{2,1,0:T(8,128)(2,1)S(1)}, bf16[2,80,1024]{2,1,0:T(8,128)(2,1)S(1)}, u32[]{:S(2)}, u32[]{:S(2)}) %collective-permute-start.8) | collective-permute-done | bytes 327712 | tf_op jit(solution)/shard_map/ppermute | solution.py:311
  46.9 2.7 %collective-permute-done.13.refs_1_ = bf16[80,1024]{1,0:T(8,128)(2,1)S(1)} collective-permute-done((bf16[80,1024]{1,0:T(8,128)(2,1)S(1)}, bf16[80,1024]{1,0:T(8,128)(2,1)S(1)}, u32[]{:S(2)}, u32[]{:S(2)}) %collective-permute-start.13) | collective-permute-done | bytes 163872 | tf_op jit(solution)/shard_map/ppermute | solution.py:311
  50.8 2.4 %collective-permute-done.12.refs_1_ = bf16[80,1024]{1,0:T(8,128)(2,1)S(1)} collective-permute-done((bf16[80,1024]{1,0:T(8,128)(2,1)S(1)}, bf16[80,1024]{1,0:T(8,128)(2,1)S(1)}, u32[]{:S(2)}, u32[]{:S(2)}) %collective-permute-start.12) | collective-permute-done | bytes 163872 | tf_op jit(solution)/shard_map/ppermute | solution.py:311
  55.0 1.5 %collective-permute-start.18 = (bf16[40,1792]{1,0:T(8,128)(2,1)S(1)}, bf16[40,1792]{1,0:T(8,128)(2,1)S(1)}, u32[]{:S(2)}, u32[]{:S(2)}) collective-permute-start(bf16[40,1792]{1,0:T(8,128)(2,1)S(1)} %get-tuple-element.64), channel_id=1, source_target_pairs={{0,2},{1,3},{2,0},{3,1},{4,6},{5,7},{6,4},{7,5},{8,10},{9,11},{10,... | collective-permute-start | bytes 430088 | tf_op jit(solution)/shard_map/ppermute | solution.py:311
  56.5 1.4 %collective-permute-start.19 = (bf16[40,1792]{1,0:T(8,128)(2,1)S(1)}, bf16[40,1792]{1,0:T(8,128)(2,1)S(1)}, u32[]{:S(2)}, u32[]{:S(2)}) collective-permute-start(bf16[40,1792]{1,0:T(8,128)(2,1)S(1)} %get-tuple-element.65), channel_id=1, source_target_pairs={{0,3},{1,2},{2,1},{3,0},{4,7},{5,6},{6,5},{7,4},{8,11},{9,10},{10,... | collective-permute-start | bytes 430088 | tf_op jit(solution)/shard_map/ppermute | solution.py:311
  59.4 1.5 %collective-permute-start.15 = (bf16[40,1792]{1,0:T(8,128)(2,1)S(1)}, bf16[40,1792]{1,0:T(8,128)(2,1)S(1)}, u32[]{:S(2)}, u32[]{:S(2)}) collective-permute-start(bf16[40,1792]{1,0:T(8,128)(2,1)S(1)} %get-tuple-element.69), channel_id=1, source_target_pairs={{0,2},{1,3},{2,0},{3,1},{4,6},{5,7},{6,4},{7,5},{8,10},{9,11},{10,... | collective-permute-start | bytes 430088 | tf_op jit(solution)/shard_map/ppermute | solution.py:311
  62.4 2.7 %collective-permute-done.19.refs_6_ = bf16[40,1792]{1,0:T(8,128)(2,1)S(1)} collective-permute-done((bf16[40,1792]{1,0:T(8,128)(2,1)S(1)}, bf16[40,1792]{1,0:T(8,128)(2,1)S(1)}, u32[]{:S(2)}, u32[]{:S(2)}) %collective-permute-start.19) | collective-permute-done | bytes 143392 | tf_op jit(solution)/shard_map/ppermute | solution.py:311
  65.1 1.5 %shard_map.122 = bf16[64,3584]{1,0:T(8,128)(2,1)} custom-call(s32[2,64]{1,0:T(2,128)S(1)} %pad_add_fusion.refs_0_.ids, f32[1,64]{1,0:T(1,128)S(1)} %bitcast.47, bf16[64,3584]{1,0:T(8,128)(2,1)S(1)} %get-tuple-element.71.refs_2_, bf16[40,1792]{1,0:T(8,128)(2,1)S(1)} %get-tuple-element.62.refs_3_, bf16[40,1792]{1,0:T(8,128)(2,1)S(1)} %collective-permute-done.17.refs_4_, ...), custom_call_target="tpu_custom_call" | custom-call | flops 36700160 | bytes 1491712 | tf_op jit(solution)/shard_map/pallas_call | solution.py:23
  68.4 1.6 %collective-permute-done.16.refs_6_ = bf16[40,1792]{1,0:T(8,128)(2,1)S(1)} collective-permute-done((bf16[40,1792]{1,0:T(8,128)(2,1)S(1)}, bf16[40,1792]{1,0:T(8,128)(2,1)S(1)}, u32[]{:S(2)}, u32[]{:S(2)}) %collective-permute-start.16) | collective-permute-done | bytes 143392 | tf_op jit(solution)/shard_map/ppermute | solution.py:311
  70.0 1.5 %shard_map.121 = bf16[64,3584]{1,0:T(8,128)(2,1)} custom-call(s32[2,64]{1,0:T(2,128)S(1)} %pad_add_fusion.refs_0_.ids, f32[1,64]{1,0:T(1,128)S(1)} %bitcast.48, bf16[64,3584]{1,0:T(8,128)(2,1)S(1)} %get-tuple-element.37.refs_2_, bf16[40,1792]{1,0:T(8,128)(2,1)S(1)} %get-tuple-element.67.refs_3_, bf16[40,1792]{1,0:T(8,128)(2,1)S(1)} %collective-permute-done.14.refs_4_, ...), custom_call_target="tpu_custom_call" | custom-call | flops 36700160 | bytes 1491712 | tf_op jit(solution)/shard_map/pallas_call | solution.py:23
  (44 shorter events, 18.4 us)
Async XLA Ops:
  2.0 7.2 %collective-permute-start = (bf16[64,3584]{1,0:T(8,128)(2,1)S(1)}, bf16[64,3584]{1,0:T(8,128)(2,1)S(1)}, u32[]{:S(2)}, u32[]{:S(2)}) collective-permute-start(bf16[64,3584]{1,0:T(8,128)(2,1)S(1)} %get-tuple-element.73.refs_1_), channel_id=1, source_target_pairs={{0,4},{8,12},{16,20},{24,28},{4,0},{12,8},{20,16},{28,24},{1,5},{9... | collective-permute-start | bytes 1376264 | tf_op jit(solution)/shard_map/ppermute | solution.py:327
  2.1 9.8 %collective-permute-start.1 = (bf16[64,3584]{1,0:T(8,128)(2,1)S(1)}, bf16[64,3584]{1,0:T(8,128)(2,1)S(1)}, u32[]{:S(2)}, u32[]{:S(2)}) collective-permute-start(bf16[64,3584]{1,0:T(8,128)(2,1)S(1)} %get-tuple-element.72), channel_id=1, source_target_pairs={{4,8},{12,16},{20,24},{8,4},{16,12},{24,20},{5,9},{13,17},{21,25},... | collective-permute-start | bytes 1376264 | tf_op jit(solution)/shard_map/ppermute | solution.py:327
  5.7 9.1 %collective-permute-start.5 = (bf16[40,1792]{1,0:T(8,128)(2,1)S(1)}, bf16[40,1792]{1,0:T(8,128)(2,1)S(1)}, u32[]{:S(2)}, u32[]{:S(2)}) collective-permute-start(bf16[40,1792]{1,0:T(8,128)(2,1)S(1)} %get-tuple-element.44), channel_id=1, source_target_pairs={{0,1},{1,0},{2,3},{3,2},{4,5},{5,4},{6,7},{7,6},{8,9},{9,8},{10,11... | collective-permute-start | bytes 430088 | tf_op jit(solution)/shard_map/ppermute | solution.py:311
  6.3 9.9 %collective-permute-start.6 = (bf16[40,1792]{1,0:T(8,128)(2,1)S(1)}, bf16[40,1792]{1,0:T(8,128)(2,1)S(1)}, u32[]{:S(2)}, u32[]{:S(2)}) collective-permute-start(bf16[40,1792]{1,0:T(8,128)(2,1)S(1)} %get-tuple-element.45), channel_id=1, source_target_pairs={{0,2},{1,3},{2,0},{3,1},{4,6},{5,7},{6,4},{7,5},{8,10},{9,11},{10,... | collective-permute-start | bytes 430088 | tf_op jit(solution)/shard_map/ppermute | solution.py:311
  7.8 8.4 %copy-start.1 = (bf16[1,1792,1024]{2,1,0:T(8,128)(2,1)S(1)}, bf16[1,1792,1024]{2,1,0:T(8,128)(2,1)}, u32[]{:S(2)}) copy-start(bf16[1,1792,1024]{2,1,0:T(8,128)(2,1)} %param.14) | copy-start | bytes 11010052
  7.8 8.4 %collective-permute-start.7 = (bf16[40,1792]{1,0:T(8,128)(2,1)S(1)}, bf16[40,1792]{1,0:T(8,128)(2,1)S(1)}, u32[]{:S(2)}, u32[]{:S(2)}) collective-permute-start(bf16[40,1792]{1,0:T(8,128)(2,1)S(1)} %get-tuple-element.46), channel_id=1, source_target_pairs={{0,3},{1,2},{2,1},{3,0},{4,7},{5,6},{6,5},{7,4},{8,11},{9,10},{10,... | collective-permute-start | bytes 430088 | tf_op jit(solution)/shard_map/ppermute | solution.py:311
  12.6 9.8 %collective-permute-start.2 = (bf16[2,40,1792]{2,1,0:T(8,128)(2,1)S(1)}, bf16[2,40,1792]{2,1,0:T(8,128)(2,1)S(1)}, u32[]{:S(2)}, u32[]{:S(2)}) collective-permute-start(bf16[2,40,1792]{2,1,0:T(8,128)(2,1)S(1)} %get-tuple-element.40), channel_id=1, source_target_pairs={{0,1},{1,0},{2,3},{3,2},{4,5},{5,4},{6,7},{7,6},{8,9},{9,8},{10,11... | collective-permute-start | bytes 860168 | tf_op jit(solution)/shard_map/ppermute | solution.py:311
  13.2 14.3 %collective-permute-start.3 = (bf16[2,40,1792]{2,1,0:T(8,128)(2,1)S(1)}, bf16[2,40,1792]{2,1,0:T(8,128)(2,1)S(1)}, u32[]{:S(2)}, u32[]{:S(2)}) collective-permute-start(bf16[2,40,1792]{2,1,0:T(8,128)(2,1)S(1)} %get-tuple-element.41), channel_id=1, source_target_pairs={{0,2},{1,3},{2,0},{3,1},{4,6},{5,7},{6,4},{7,5},{8,10},{9,11},{10,... | collective-permute-start | bytes 860168 | tf_op jit(solution)/shard_map/ppermute | solution.py:311
  14.7 14.8 %collective-permute-start.4 = (bf16[2,40,1792]{2,1,0:T(8,128)(2,1)S(1)}, bf16[2,40,1792]{2,1,0:T(8,128)(2,1)S(1)}, u32[]{:S(2)}, u32[]{:S(2)}) collective-permute-start(bf16[2,40,1792]{2,1,0:T(8,128)(2,1)S(1)} %get-tuple-element.42), channel_id=1, source_target_pairs={{0,3},{1,2},{2,1},{3,0},{4,7},{5,6},{6,5},{7,4},{8,11},{9,10},{10,... | collective-permute-start | bytes 860168 | tf_op jit(solution)/shard_map/ppermute | solution.py:311
  16.2 13.3 %copy-start.2 = (bf16[1,1024,1792]{2,1,0:T(8,128)(2,1)S(1)}, bf16[1,1024,1792]{2,1,0:T(8,128)(2,1)}, u32[]{:S(2)}) copy-start(bf16[1,1024,1792]{2,1,0:T(8,128)(2,1)} %param.15) | copy-start | bytes 11010052
  17.6 18.0 %collective-permute-start.9 = (bf16[2,80,1024]{2,1,0:T(8,128)(2,1)S(1)}, bf16[2,80,1024]{2,1,0:T(8,128)(2,1)S(1)}, u32[]{:S(2)}, u32[]{:S(2)}) collective-permute-start(bf16[2,80,1024]{2,1,0:T(8,128)(2,1)S(1)} %get-tuple-element.48), channel_id=1, source_target_pairs={{0,1},{1,0},{2,3},{3,2},{4,5},{5,4},{6,7},{7,6},{8,9},{9,8},{10,11... | collective-permute-start | bytes 983048 | tf_op jit(solution)/shard_map/ppermute | solution.py:311
  30.8 8.3 %collective-permute-start.10 = (bf16[80,1024]{1,0:T(8,128)(2,1)S(1)}, bf16[80,1024]{1,0:T(8,128)(2,1)S(1)}, u32[]{:S(2)}, u32[]{:S(2)}) collective-permute-start(bf16[80,1024]{1,0:T(8,128)(2,1)S(1)} %get-tuple-element.53), channel_id=1, source_target_pairs={{0,1},{1,0},{2,3},{3,2},{4,5},{5,4},{6,7},{7,6},{8,9},{9,8},{10,11... | collective-permute-start | bytes 491528 | tf_op jit(solution)/shard_map/ppermute | solution.py:311
  32.9 13.3 %collective-permute-start.8 = (bf16[2,80,1024]{2,1,0:T(8,128)(2,1)S(1)}, bf16[2,80,1024]{2,1,0:T(8,128)(2,1)S(1)}, u32[]{:S(2)}, u32[]{:S(2)}) collective-permute-start(bf16[2,80,1024]{2,1,0:T(8,128)(2,1)S(1)} %get-tuple-element.56), channel_id=1, source_target_pairs={{0,1},{1,0},{2,3},{3,2},{4,5},{5,4},{6,7},{7,6},{8,9},{9,8},{10,11... | collective-permute-start | bytes 983048 | tf_op jit(solution)/shard_map/ppermute | solution.py:311
  39.4 10.2 %collective-permute-start.13 = (bf16[80,1024]{1,0:T(8,128)(2,1)S(1)}, bf16[80,1024]{1,0:T(8,128)(2,1)S(1)}, u32[]{:S(2)}, u32[]{:S(2)}) collective-permute-start(bf16[80,1024]{1,0:T(8,128)(2,1)S(1)} %fusion.4.refs_0_), channel_id=1, source_target_pairs={{0,1},{1,0},{2,3},{3,2},{4,5},{5,4},{6,7},{7,6},{8,9},{9,8},{10,11... | collective-permute-start | bytes 491528 | tf_op jit(solution)/shard_map/ppermute | solution.py:311
  40.1 13.0 %collective-permute-start.12 = (bf16[80,1024]{1,0:T(8,128)(2,1)S(1)}, bf16[80,1024]{1,0:T(8,128)(2,1)S(1)}, u32[]{:S(2)}, u32[]{:S(2)}) collective-permute-start(bf16[80,1024]{1,0:T(8,128)(2,1)S(1)} %multiply_convert_fusion.refs_0_), channel_id=1, source_target_pairs={{0,1},{1,0},{2,3},{3,2},{4,5},{5,4},{6,7},{7,6},{8,9},{9,8},{10,11... | collective-permute-start | bytes 491528 | tf_op jit(solution)/shard_map/ppermute | solution.py:311
  46.3 11.6 %collective-permute-start.11 = (bf16[80,1024]{1,0:T(8,128)(2,1)S(1)}, bf16[80,1024]{1,0:T(8,128)(2,1)S(1)}, u32[]{:S(2)}, u32[]{:S(2)}) collective-permute-start(bf16[80,1024]{1,0:T(8,128)(2,1)S(1)} %fusion.1.refs_0_), channel_id=1, source_target_pairs={{0,1},{1,0},{2,3},{3,2},{4,5},{5,4},{6,7},{7,6},{8,9},{9,8},{10,11... | collective-permute-start | bytes 491528 | tf_op jit(solution)/shard_map/ppermute | solution.py:311
  50.8 14.4 %copy-start.3 = (f32[1,64,1]{1,2,0:T(1,128)S(1)}, f32[1,64,1]{1,2,0:T(1,128)}, u32[]{:S(2)}) copy-start(f32[1,64,1]{1,2,0:T(1,128)} %param.19) | copy-start | bytes 772
  54.4 15.6 %copy-start.4 = (f32[1,64,1]{1,2,0:T(1,128)S(1)}, f32[1,64,1]{1,2,0:T(1,128)}, u32[]{:S(2)}) copy-start(f32[1,64,1]{1,2,0:T(1,128)} %param.17) | copy-start | bytes 772
  54.4 6.7 %collective-permute-start.17 = (bf16[40,1792]{1,0:T(8,128)(2,1)S(1)}, bf16[40,1792]{1,0:T(8,128)(2,1)S(1)}, u32[]{:S(2)}, u32[]{:S(2)}) collective-permute-start(bf16[40,1792]{1,0:T(8,128)(2,1)S(1)} %get-tuple-element.63), channel_id=1, source_target_pairs={{0,1},{1,0},{2,3},{3,2},{4,5},{5,4},{6,7},{7,6},{8,9},{9,8},{10,11... | collective-permute-start | bytes 430088 | tf_op jit(solution)/shard_map/ppermute | solution.py:311
  55.0 7.4 %collective-permute-start.18 = (bf16[40,1792]{1,0:T(8,128)(2,1)S(1)}, bf16[40,1792]{1,0:T(8,128)(2,1)S(1)}, u32[]{:S(2)}, u32[]{:S(2)}) collective-permute-start(bf16[40,1792]{1,0:T(8,128)(2,1)S(1)} %get-tuple-element.64), channel_id=1, source_target_pairs={{0,2},{1,3},{2,0},{3,1},{4,6},{5,7},{6,4},{7,5},{8,10},{9,11},{10,... | collective-permute-start | bytes 430088 | tf_op jit(solution)/shard_map/ppermute | solution.py:311
  56.5 8.6 %collective-permute-start.19 = (bf16[40,1792]{1,0:T(8,128)(2,1)S(1)}, bf16[40,1792]{1,0:T(8,128)(2,1)S(1)}, u32[]{:S(2)}, u32[]{:S(2)}) collective-permute-start(bf16[40,1792]{1,0:T(8,128)(2,1)S(1)} %get-tuple-element.65), channel_id=1, source_target_pairs={{0,3},{1,2},{2,1},{3,0},{4,7},{5,6},{6,5},{7,4},{8,11},{9,10},{10,... | collective-permute-start | bytes 430088 | tf_op jit(solution)/shard_map/ppermute | solution.py:311
  58.8 8.4 %collective-permute-start.14 = (bf16[40,1792]{1,0:T(8,128)(2,1)S(1)}, bf16[40,1792]{1,0:T(8,128)(2,1)S(1)}, u32[]{:S(2)}, u32[]{:S(2)}) collective-permute-start(bf16[40,1792]{1,0:T(8,128)(2,1)S(1)} %get-tuple-element.68), channel_id=1, source_target_pairs={{0,1},{1,0},{2,3},{3,2},{4,5},{5,4},{6,7},{7,6},{8,9},{9,8},{10,11... | collective-permute-start | bytes 430088 | tf_op jit(solution)/shard_map/ppermute | solution.py:311
  59.4 9.0 %collective-permute-start.15 = (bf16[40,1792]{1,0:T(8,128)(2,1)S(1)}, bf16[40,1792]{1,0:T(8,128)(2,1)S(1)}, u32[]{:S(2)}, u32[]{:S(2)}) collective-permute-start(bf16[40,1792]{1,0:T(8,128)(2,1)S(1)} %get-tuple-element.69), channel_id=1, source_target_pairs={{0,2},{1,3},{2,0},{3,1},{4,6},{5,7},{6,4},{7,5},{8,10},{9,11},{10,... | collective-permute-start | bytes 430088 | tf_op jit(solution)/shard_map/ppermute | solution.py:311
  61.1 8.9 %collective-permute-start.16 = (bf16[40,1792]{1,0:T(8,128)(2,1)S(1)}, bf16[40,1792]{1,0:T(8,128)(2,1)S(1)}, u32[]{:S(2)}, u32[]{:S(2)}) collective-permute-start(bf16[40,1792]{1,0:T(8,128)(2,1)S(1)} %get-tuple-element.70), channel_id=1, source_target_pairs={{0,3},{1,2},{2,1},{3,0},{4,7},{5,6},{6,5},{7,4},{8,11},{9,10},{10,... | collective-permute-start | bytes 430088 | tf_op jit(solution)/shard_map/ppermute | solution.py:311
  (1 other events, 8.4 us)

commit v4 on v3

--- a/solution.py
+++ b/solution.py
@@ -9,6 +9,7 @@
 
 EXPERTS = 2
 CAP = 40
+LANES = 128
 BF16 = jnp.bfloat16
 F32 = jnp.float32
 VMEM_LIMIT = 40 * 1024 * 1024
@@ -160,7 +161,7 @@
 
 def in_partials(parts, gate, up, group, stream=0):
     width, hidden = gate.shape
-    rows = len(parts) * CAP
+    rows = sum(p.shape[-2] for p in parts)
     return kernel_call(
         functools.partial(in_kernel, len(parts), group, stream),
         (like((2, rows // group, hidden)),) * group,
@@ -184,7 +185,7 @@
 
 def grad_partials(parts, down, group, stream=0):
     hidden, width = down.shape
-    rows = len(parts) * CAP
+    rows = sum(p.shape[-2] for p in parts)
     return kernel_call(
         functools.partial(grad_kernel, len(parts), group, stream),
         (like((rows // group, hidden)),) * group,
@@ -259,39 +260,70 @@
     )
 
 
-def combine_kernel(group, ids, *refs):
-    routing, gates, base, *rest = refs
+def picks_kernel(group, *refs):
+    routing, gates, picks, weights = refs[0], refs[1:3], refs[3:5], refs[5:7]
+    expert, _ = position(group)
+    tokens = routing.shape[1]
     small = routing[...]
-    same, other, out = rest[:group], rest[group : 2 * group], rest[2 * group]
-    expert, own_slice = position(group)
-    table = tables(small[ids], expert)
-    tokens = base.shape[0]
-    width = same[0].shape[1]
     row = lax.broadcasted_iota(jnp.int32, (tokens, tokens), 0)
     col = lax.broadcasted_iota(jnp.int32, (tokens, tokens), 1)
-    weight = jnp.sum(jnp.where(row == col, gates[...], 0.0), axis=1, keepdims=True)
+    for ids, gate, pick, weight in zip((FWD_IDS, BWD_IDS), gates, picks, weights):
+        pick[...] = tables(small[ids], expert)
+        column = jnp.sum(jnp.where(row == col, gate[...], 0.0), axis=1, keepdims=True)
+        weight[...] = jnp.broadcast_to(column, weight.shape)
+
+
+def picks_of(routing, fwd_gates, bwd_gates, group):
+    tokens = routing.shape[1]
+    pick = like((2 * CAP, tokens))
+    weight = jax.ShapeDtypeStruct((tokens, LANES), F32)
+    return kernel_call(
+        functools.partial(picks_kernel, group),
+        (pick, pick, weight, weight),
+        (routing, fwd_gates, bwd_gates),
+        0,
+    )
+
+
+def combine_kernel(group, *refs):
+    pick, weights, base, *rest = refs
+    other, same, (out, ready, sems) = rest[:group], rest[group : 2 * group], rest[2 * group :]
+    own_slice = position(group)[1]
+    width = same[0].shape[1]
+    weight = weights[:, :1]
     contract = (((0,), (0,)), ((), ()))
-    for r in range(group):
-        blocks = jnp.concatenate([same[r][...], other[r][...]], axis=0)
-        picked = lax.dot_general(table, blocks, contract, preferred_element_type=F32)
-        for own in range(group):
-
-            @pl.when(own_slice == own)
-            def _(own=own, r=r, picked=picked):
-                at = (own ^ r) * width
-                out[:, at : at + width] = (
-                    base[:, at : at + width].astype(F32) + weight * picked
-                ).astype(BF16)
-
-
-def combine(routing, ids, gates, base, same, other):
+    for own in range(group):
+
+        @pl.when(own_slice == own)
+        def _(own=own):
+            copies = []
+            for r in range(group):
+                blocks = jnp.concatenate([same[r][...], other[r][...]], axis=0)
+                picked = lax.dot_general(pick[...], blocks, contract, preferred_element_type=F32)
+                at = pl.ds((own ^ r) * width, width)
+                ready[:, at] = (base[:, at].astype(F32) + weight * picked).astype(BF16)
+                if width % LANES == 0:
+                    copies.append(pltpu.make_async_copy(ready.at[:, at], out.at[:, at], sems.at[r]))
+                    copies[-1].start()
+            if width % LANES:
+                copies.append(pltpu.make_async_copy(ready, out, sems.at[0]))
+                copies[-1].start()
+            for copy in copies:
+                copy.wait()
+
+
+def combine(pick, weights, base, same, other):
     group = len(same)
-    return kernel_call(
-        functools.partial(combine_kernel, group, ids),
-        like(base.shape),
-        (routing, gates, base, *same, *other),
-        4 * CAP * base.shape[0] * base.shape[1],
-    )
+    whole = pl.BlockSpec(memory_space=pltpu.VMEM)
+    inputs = (pick, weights, base, *other, *same)
+    return pl.pallas_call(
+        functools.partial(combine_kernel, group),
+        out_shape=like(base.shape),
+        in_specs=[whole] * len(inputs),
+        out_specs=pl.BlockSpec(memory_space=pltpu.HBM),
+        scratch_shapes=[pltpu.VMEM(base.shape, BF16), pltpu.SemaphoreType.DMA((group,))],
+        compiler_params=pltpu.CompilerParams(vmem_limit_bytes=VMEM_LIMIT),
+    )(*inputs)
 
 
 def after(value, *earlier):
@@ -343,13 +375,19 @@
     back_parts = in_partials(saved_rows, gate, up, group)
     back_sent = sent(back_parts[1:])
     stream_rows = after(stream_rows, back_parts)
-    g_parts = grad_partials([g_own, *stream_rows], down, group, 1)
+    x_parts = in_partials([x_own, *stream_rows], gate, up, group, 0)
+    x_sent = sent(x_parts[1:])
+    g_parts = grad_partials([after(g_own, x_parts), *stream_rows], down, group, 1)
     g_sent = sent(g_parts[1:])
-    x_parts = in_partials([after(x_own, g_parts), *stream_rows], gate, up, group, 0)
-    x_sent = sent(x_parts[1:])
-
-    back_sent, g_sent = after((back_sent, g_sent), x_parts)
+
+    back_sent = after(back_sent, g_parts)
     back = summed(back_parts[0], back_sent)
+    x_sent = after(x_sent, back)
+    ahead = summed(x_parts[0], x_sent)
+    hidden = (jax.nn.silu(ahead[0]) * ahead[1]).astype(BF16)
+    hidden_sent = sent([hidden] * (group - 1))
+
+    g_sent = after(g_sent, hidden)
     grad_hidden = summed(g_parts[0], g_sent)
     sig = jax.nn.sigmoid(back[0])
     grad_gate = grad_hidden * back[1] * sig * (1.0 + back[0] * (1.0 - sig))
@@ -358,22 +396,20 @@
     gate_sent = sent([grad_gate] * (group - 1))
     up_sent = sent([grad_up] * (group - 1))
 
-    x_sent = after(x_sent, grad_up)
-    ahead = summed(x_parts[0], x_sent)
-    hidden = (jax.nn.silu(ahead[0]) * ahead[1]).astype(BF16)
-    hidden_sent = sent([hidden] * (group - 1))
-
     def returned(blocks):
         rows = sent(blocks[1:])
         return [blocks[0], *rows[: group - 1]], rows[group - 1 :]
 
-    half = back_half([grad_gate, *gate_sent], gate)
-    bwd_rows = back_rows([grad_up, *after(up_sent, half)], up, half)
-    bwd_same, bwd_other = returned(bwd_rows)
-    hidden_sent = after(hidden_sent, bwd_rows)
-    fwd_same, fwd_other = returned(down_rows([hidden, *hidden_sent], down))
-    bwd_out = combine(routing, BWD_IDS, bwd_gates, section_g, bwd_same, bwd_other)
-    fwd_out = combine(routing, FWD_IDS, fwd_gates, section_x, fwd_same, fwd_other)
+    fwd_pick, bwd_pick, fwd_weights, bwd_weights = picks_of(
+        after(routing, hidden), fwd_gates, bwd_gates, group
+    )
+    hidden_sent = after(hidden_sent, fwd_pick)
+    fwd_rows = down_rows([hidden, *hidden_sent], down)
+    fwd_same, fwd_other = returned(fwd_rows)
+    half = back_half([grad_gate, *after(gate_sent, fwd_rows)], gate)
+    bwd_same, bwd_other = returned(back_rows([grad_up, *after(up_sent, half)], up, half))
+    fwd_out = combine(fwd_pick, fwd_weights, section_x, fwd_same, fwd_other)
+    bwd_out = combine(bwd_pick, bwd_weights, section_g, bwd_same, bwd_other)
     return (fwd_out[None], bwd_out[None])
 
 

time: 72 us -> 70 us (0.972)
  waiting for transfers between devices: 33.9 us -> 32.9 us
    pallas_call x10 -> x9, Pallas kernels: 11.4 us -> 8.58 us  [kernel_call(): pl.pallas_call(kernel, out_shape=out_shape, in_specs=[whole] * len(inputs...]
    pallas_call x0 -> x2, Pallas kernels: none -> 2.08 us  [combine(): pl.pallas_call(functools.partial(combine_kernel, group), out_shape=like(b...]
    ppermute x18, waiting for transfers between devices: 31.3 us -> 30.2 us  [to_partner(): lax.ppermute(value, 'expert', [(i, i ^ mask) for i in range(devices)])]
  transfers between devices with their start and end apart: 20 -> 20, of which waited for: 14 -> 13; matrix products, arithmetic and copies ran while one was open for 2% -> 2% of each run, Pallas kernels for 14% -> 14%
where the time goes in v4:
time: 70 us; the launch traced here: 69.9 us
  waiting for transfers between devices  32.9 us (47%)
  starting transfers between devices  22.9 us (33%)
  Pallas kernels  10.7 us (15%)
  other arithmetic  2.64 us (4%)
  between operations  0.79 us (1%)
    ppermute x18, waiting for transfers between devices, to_partner(): lax.ppermute(value, 'expert', [(i, i ^ mask) for i in range(devices)])  30.2 us
    ppermute x18, starting transfers between devices, to_partner(): lax.ppermute(value, 'expert', [(i, i ^ mask) for i in range(devices)])  20.4 us
    pallas_call x9, Pallas kernels, kernel_call(): pl.pallas_call(kernel, out_shape=out_shape, in_specs=[whole] * len(inputs...  8.58 us
    ppermute x2, waiting for transfers between devices, body(): lax.ppermute(value, 'pipe', pairs + [(b, a) for a, b in pairs])  2.68 us
    ppermute x2, starting transfers between devices, body(): lax.ppermute(value, 'pipe', pairs + [(b, a) for a, b in pairs])  2.52 us
    pallas_call x2, Pallas kernels, combine(): pl.pallas_call(functools.partial(combine_kernel, group), out_shape=like(b...  2.08 us
  transfers between devices with their start and end apart: 20, of which 13 were waited for; matrix products, arithmetic and copies ran while one was open for 2% of the time, Pallas kernels for 14%

profile of v4, /device:TPU:18, one launch (start us, length us, event | category | flops | bytes accessed | tf_op | source)
XLA Modules:
  0.0 69.9 jit_solution(6843666820986838356)
XLA Ops:
  0.6 1.4 %select_bitcast_fusion.1 = (bf16[64,3584]{1,0:T(8,128)(2,1)S(1)}, bf16[64,3584]{1,0:T(8,128)(2,1)S(1)}, bf16[64,3584]{1,0:T(8,128)(2,1)S(1)}) fusion(bf16[1,64,3584]{2,1,0:T(8,128)(2,1)} %param.12, bf16[1,64,3584]{2,1,0:T(8,128)(2,1)} %param.10, pred[]{:T(512)S(6)} %eq.3, bf16[1,64,3584]{2,1,0:T(8,128)(2,1)} %param.11, pred[]{:T(512)S(6)} %lt.3), kind=kLoop, calls=%fused_computation.3 | loop fusion | flops 688128 | bytes 2752514 | tf_op jit(solution)/shard_map/jit(_where)/select_n | solution.py:355
  2.1 2.4 %collective-permute-start.1 = (bf16[64,3584]{1,0:T(8,128)(2,1)S(1)}, bf16[64,3584]{1,0:T(8,128)(2,1)S(1)}, u32[]{:S(2)}, u32[]{:S(2)}) collective-permute-start(bf16[64,3584]{1,0:T(8,128)(2,1)S(1)} %get-tuple-element.84), channel_id=1, source_target_pairs={{4,8},{12,16},{20,24},{8,4},{16,12},{24,20},{5,9},{13,17},{21,25},... | collective-permute-start | bytes 1376264 | tf_op jit(solution)/shard_map/ppermute | solution.py:359
  6.3 1.5 %collective-permute-start.6 = (bf16[40,1792]{1,0:T(8,128)(2,1)S(1)}, bf16[40,1792]{1,0:T(8,128)(2,1)S(1)}, u32[]{:S(2)}, u32[]{:S(2)}) collective-permute-start(bf16[40,1792]{1,0:T(8,128)(2,1)S(1)} %get-tuple-element.49), channel_id=1, source_target_pairs={{0,2},{1,3},{2,0},{3,1},{4,6},{5,7},{6,4},{7,5},{8,10},{9,11},{10,... | collective-permute-start | bytes 430088 | tf_op jit(solution)/shard_map/ppermute | solution.py:343
  7.8 1.4 %collective-permute-start.7 = (bf16[40,1792]{1,0:T(8,128)(2,1)S(1)}, bf16[40,1792]{1,0:T(8,128)(2,1)S(1)}, u32[]{:S(2)}, u32[]{:S(2)}) collective-permute-start(bf16[40,1792]{1,0:T(8,128)(2,1)S(1)} %get-tuple-element.50), channel_id=1, source_target_pairs={{0,3},{1,2},{2,1},{3,0},{4,7},{5,6},{6,5},{7,4},{8,11},{9,10},{10,... | collective-permute-start | bytes 430088 | tf_op jit(solution)/shard_map/ppermute | solution.py:343
  9.2 2.7 %collective-permute-done.1.refs_3_ = bf16[64,3584]{1,0:T(8,128)(2,1)S(1)} collective-permute-done((bf16[64,3584]{1,0:T(8,128)(2,1)S(1)}, bf16[64,3584]{1,0:T(8,128)(2,1)S(1)}, u32[]{:S(2)}, u32[]{:S(2)}) %collective-permute-start.1) | collective-permute-done | bytes 458784 | tf_op jit(solution)/shard_map/ppermute | solution.py:359
  13.2 1.5 %collective-permute-start.3 = (bf16[2,40,1792]{2,1,0:T(8,128)(2,1)S(1)}, bf16[2,40,1792]{2,1,0:T(8,128)(2,1)S(1)}, u32[]{:S(2)}, u32[]{:S(2)}) collective-permute-start(bf16[2,40,1792]{2,1,0:T(8,128)(2,1)S(1)} %get-tuple-element.45), channel_id=1, source_target_pairs={{0,2},{1,3},{2,0},{3,1},{4,6},{5,7},{6,4},{7,5},{8,10},{9,11},{10,... | collective-permute-start | bytes 860168 | tf_op jit(solution)/shard_map/ppermute | solution.py:343
  14.7 1.4 %collective-permute-start.4 = (bf16[2,40,1792]{2,1,0:T(8,128)(2,1)S(1)}, bf16[2,40,1792]{2,1,0:T(8,128)(2,1)S(1)}, u32[]{:S(2)}, u32[]{:S(2)}) collective-permute-start(bf16[2,40,1792]{2,1,0:T(8,128)(2,1)S(1)} %get-tuple-element.46), channel_id=1, source_target_pairs={{0,3},{1,2},{2,1},{3,0},{4,7},{5,6},{6,5},{7,4},{8,11},{9,10},{10,... | collective-permute-start | bytes 860168 | tf_op jit(solution)/shard_map/ppermute | solution.py:343
  16.2 1.4 %shard_map.115 = (bf16[2,80,1024]{2,1,0:T(8,128)(2,1)S(1)}, bf16[2,80,1024]{2,1,0:T(8,128)(2,1)S(1)}) custom-call(bf16[40,1792]{1,0:T(8,128)(2,1)S(1)} %get-tuple-element.47.refs_0_, bf16[40,1792]{1,0:T(8,128)(2,1)S(1)} %collective-permute-done.5.refs_1_, bf16[40,1792]{1,0:T(8,128)(2,1)S(1)} %collective-permute-done.6.refs_2_, ...), custom_call_target="tpu_custom_call" | custom-call | flops 1174405120 | bytes 8568832 | tf_op jit(solution)/shard_map/pallas_call | solution.py:24
  18.9 3.5 %collective-permute-done.2.refs_1_ = bf16[2,40,1792]{2,1,0:T(8,128)(2,1)S(1)} collective-permute-done((bf16[2,40,1792]{2,1,0:T(8,128)(2,1)S(1)}, bf16[2,40,1792]{2,1,0:T(8,128)(2,1)S(1)}, u32[]{:S(2)}, u32[]{:S(2)}) %collective-permute-start.2) | collective-permute-done | bytes 286752 | tf_op jit(solution)/shard_map/ppermute | solution.py:343
  22.4 5.2 %collective-permute-done.3.refs_2_ = bf16[2,40,1792]{2,1,0:T(8,128)(2,1)S(1)} collective-permute-done((bf16[2,40,1792]{2,1,0:T(8,128)(2,1)S(1)}, bf16[2,40,1792]{2,1,0:T(8,128)(2,1)S(1)}, u32[]{:S(2)}, u32[]{:S(2)}) %collective-permute-start.3) | collective-permute-done | bytes 286752 | tf_op jit(solution)/shard_map/ppermute | solution.py:343
  27.6 1.9 %collective-permute-done.4.refs_3_ = bf16[2,40,1792]{2,1,0:T(8,128)(2,1)S(1)} collective-permute-done((bf16[2,40,1792]{2,1,0:T(8,128)(2,1)S(1)}, bf16[2,40,1792]{2,1,0:T(8,128)(2,1)S(1)}, u32[]{:S(2)}, u32[]{:S(2)}) %collective-permute-start.4) | collective-permute-done | bytes 286752 | tf_op jit(solution)/shard_map/ppermute | solution.py:343
  29.5 1.4 %shard_map.116 = (bf16[2,80,1024]{2,1,0:T(8,128)(2,1)S(1)}, bf16[2,80,1024]{2,1,0:T(8,128)(2,1)S(1)}) custom-call(bf16[40,1792]{1,0:T(8,128)(2,1)S(1)} %get-tuple-element.43.refs_0_, bf16[2,40,1792]{2,1,0:T(8,128)(2,1)S(1)} %collective-permute-done.2.refs_1_, bf16[2,40,1792]{2,1,0:T(8,128)(2,1)S(1)} %collective-permute-done.3.refs_2_, ...), custom_call_target="tpu_custom_call" | custom-call | flops 1174405120 | bytes 8998912 | tf_op jit(solution)/shard_map/pallas_call | solution.py:24
  32.9 1.5 %collective-permute-start.14 = (bf16[80,1024]{1,0:T(8,128)(2,1)S(1)}, bf16[80,1024]{1,0:T(8,128)(2,1)S(1)}, u32[]{:S(2)}, u32[]{:S(2)}) collective-permute-start(bf16[80,1024]{1,0:T(8,128)(2,1)S(1)} %get-tuple-element.61), channel_id=1, source_target_pairs={{0,1},{1,0},{2,3},{3,2},{4,5},{5,4},{6,7},{7,6},{8,9},{9,8},{10,11... | collective-permute-start | bytes 491528 | tf_op jit(solution)/shard_map/ppermute | solution.py:343
  35.7 6.9 %collective-permute-done.8 = bf16[2,80,1024]{2,1,0:T(8,128)(2,1)S(1)} collective-permute-done((bf16[2,80,1024]{2,1,0:T(8,128)(2,1)S(1)}, bf16[2,80,1024]{2,1,0:T(8,128)(2,1)S(1)}, u32[]{:S(2)}, u32[]{:S(2)}) %collective-permute-start.8) | collective-permute-done | bytes 327712 | tf_op jit(solution)/shard_map/ppermute | solution.py:343
  43.4 2.7 %collective-permute-done.14 = bf16[80,1024]{1,0:T(8,128)(2,1)S(1)} collective-permute-done((bf16[80,1024]{1,0:T(8,128)(2,1)S(1)}, bf16[80,1024]{1,0:T(8,128)(2,1)S(1)}, u32[]{:S(2)}, u32[]{:S(2)}) %collective-permute-start.14) | collective-permute-done | bytes 163872 | tf_op jit(solution)/shard_map/ppermute | solution.py:343
  47.0 1.6 %collective-permute-start.15 = (bf16[80,1024]{1,0:T(8,128)(2,1)S(1)}, bf16[80,1024]{1,0:T(8,128)(2,1)S(1)}, u32[]{:S(2)}, u32[]{:S(2)}) collective-permute-start(bf16[80,1024]{1,0:T(8,128)(2,1)S(1)} %multiply_convert_fusion.refs_0_), channel_id=1, source_target_pairs={{0,1},{1,0},{2,3},{3,2},{4,5},{5,4},{6,7},{7,6},{8,9},{9,8},{10,11... | collective-permute-start | bytes 491528 | tf_op jit(solution)/shard_map/ppermute | solution.py:343
  50.9 1.5 %collective-permute-start.11 = (bf16[40,1792]{1,0:T(8,128)(2,1)S(1)}, bf16[40,1792]{1,0:T(8,128)(2,1)S(1)}, u32[]{:S(2)}, u32[]{:S(2)}) collective-permute-start(bf16[40,1792]{1,0:T(8,128)(2,1)S(1)} %get-tuple-element.69), channel_id=1, source_target_pairs={{0,2},{1,3},{2,0},{3,1},{4,6},{5,7},{6,4},{7,5},{8,10},{9,11},{10,... | collective-permute-start | bytes 430088 | tf_op jit(solution)/shard_map/ppermute | solution.py:343
  52.9 1.5 %collective-permute-start.13 = (bf16[40,1792]{1,0:T(8,128)(2,1)S(1)}, bf16[40,1792]{1,0:T(8,128)(2,1)S(1)}, u32[]{:S(2)}, u32[]{:S(2)}) collective-permute-start(bf16[40,1792]{1,0:T(8,128)(2,1)S(1)} %get-tuple-element.72), channel_id=1, source_target_pairs={{0,1},{1,0},{2,3},{3,2},{4,5},{5,4},{6,7},{7,6},{8,9},{9,8},{10,11... | collective-permute-start | bytes 430088 | tf_op jit(solution)/shard_map/ppermute | solution.py:343
  55.6 1.5 %collective-permute-done.15.refs_1_ = bf16[80,1024]{1,0:T(8,128)(2,1)S(1)} collective-permute-done((bf16[80,1024]{1,0:T(8,128)(2,1)S(1)}, bf16[80,1024]{1,0:T(8,128)(2,1)S(1)}, u32[]{:S(2)}, u32[]{:S(2)}) %collective-permute-start.15) | collective-permute-done | bytes 163872 | tf_op jit(solution)/shard_map/ppermute | solution.py:343
  58.3 1.5 %collective-permute-start.17 = (bf16[40,1792]{1,0:T(8,128)(2,1)S(1)}, bf16[40,1792]{1,0:T(8,128)(2,1)S(1)}, u32[]{:S(2)}, u32[]{:S(2)}) collective-permute-start(bf16[40,1792]{1,0:T(8,128)(2,1)S(1)} %get-tuple-element.80), channel_id=1, source_target_pairs={{0,2},{1,3},{2,0},{3,1},{4,6},{5,7},{6,4},{7,5},{8,10},{9,11},{10,... | collective-permute-start | bytes 430088 | tf_op jit(solution)/shard_map/ppermute | solution.py:343
  60.3 1.5 %collective-permute-start.19 = (bf16[40,1792]{1,0:T(8,128)(2,1)S(1)}, bf16[40,1792]{1,0:T(8,128)(2,1)S(1)}, u32[]{:S(2)}, u32[]{:S(2)}) collective-permute-start(bf16[40,1792]{1,0:T(8,128)(2,1)S(1)} %get-tuple-element.83), channel_id=1, source_target_pairs={{0,1},{1,0},{2,3},{3,2},{4,5},{5,4},{6,7},{7,6},{8,9},{9,8},{10,11... | collective-permute-start | bytes 430088 | tf_op jit(solution)/shard_map/ppermute | solution.py:343
  61.8 1.3 %collective-permute-done.13.refs_6_ = bf16[40,1792]{1,0:T(8,128)(2,1)S(1)} collective-permute-done((bf16[40,1792]{1,0:T(8,128)(2,1)S(1)}, bf16[40,1792]{1,0:T(8,128)(2,1)S(1)}, u32[]{:S(2)}, u32[]{:S(2)}) %collective-permute-start.13) | collective-permute-done | bytes 143392 | tf_op jit(solution)/shard_map/ppermute | solution.py:343
  65.3 2.1 %collective-permute-done.18.refs_4_ = bf16[40,1792]{1,0:T(8,128)(2,1)S(1)} collective-permute-done((bf16[40,1792]{1,0:T(8,128)(2,1)S(1)}, bf16[40,1792]{1,0:T(8,128)(2,1)S(1)}, u32[]{:S(2)}, u32[]{:S(2)}) %collective-permute-start.18) | collective-permute-done | bytes 143392 | tf_op jit(solution)/shard_map/ppermute | solution.py:343
  67.4 1.4 %collective-permute-done.19.refs_6_ = bf16[40,1792]{1,0:T(8,128)(2,1)S(1)} collective-permute-done((bf16[40,1792]{1,0:T(8,128)(2,1)S(1)}, bf16[40,1792]{1,0:T(8,128)(2,1)S(1)}, u32[]{:S(2)}, u32[]{:S(2)}) %collective-permute-start.19) | collective-permute-done | bytes 143392 | tf_op jit(solution)/shard_map/ppermute | solution.py:343
  (45 shorter events, 18.2 us)
Async XLA Ops:
  2.0 7.2 %collective-permute-start = (bf16[64,3584]{1,0:T(8,128)(2,1)S(1)}, bf16[64,3584]{1,0:T(8,128)(2,1)S(1)}, u32[]{:S(2)}, u32[]{:S(2)}) collective-permute-start(bf16[64,3584]{1,0:T(8,128)(2,1)S(1)} %get-tuple-element.85.refs_1_), channel_id=1, source_target_pairs={{0,4},{8,12},{16,20},{24,28},{4,0},{12,8},{20,16},{28,24},{1,5},{9... | collective-permute-start | bytes 1376264 | tf_op jit(solution)/shard_map/ppermute | solution.py:359
  2.1 9.8 %collective-permute-start.1 = (bf16[64,3584]{1,0:T(8,128)(2,1)S(1)}, bf16[64,3584]{1,0:T(8,128)(2,1)S(1)}, u32[]{:S(2)}, u32[]{:S(2)}) collective-permute-start(bf16[64,3584]{1,0:T(8,128)(2,1)S(1)} %get-tuple-element.84), channel_id=1, source_target_pairs={{4,8},{12,16},{20,24},{8,4},{16,12},{24,20},{5,9},{13,17},{21,25},... | collective-permute-start | bytes 1376264 | tf_op jit(solution)/shard_map/ppermute | solution.py:359
  5.7 9.1 %collective-permute-start.5 = (bf16[40,1792]{1,0:T(8,128)(2,1)S(1)}, bf16[40,1792]{1,0:T(8,128)(2,1)S(1)}, u32[]{:S(2)}, u32[]{:S(2)}) collective-permute-start(bf16[40,1792]{1,0:T(8,128)(2,1)S(1)} %get-tuple-element.48), channel_id=1, source_target_pairs={{0,1},{1,0},{2,3},{3,2},{4,5},{5,4},{6,7},{7,6},{8,9},{9,8},{10,11... | collective-permute-start | bytes 430088 | tf_op jit(solution)/shard_map/ppermute | solution.py:343
  6.3 9.9 %collective-permute-start.6 = (bf16[40,1792]{1,0:T(8,128)(2,1)S(1)}, bf16[40,1792]{1,0:T(8,128)(2,1)S(1)}, u32[]{:S(2)}, u32[]{:S(2)}) collective-permute-start(bf16[40,1792]{1,0:T(8,128)(2,1)S(1)} %get-tuple-element.49), channel_id=1, source_target_pairs={{0,2},{1,3},{2,0},{3,1},{4,6},{5,7},{6,4},{7,5},{8,10},{9,11},{10,... | collective-permute-start | bytes 430088 | tf_op jit(solution)/shard_map/ppermute | solution.py:343
  7.8 8.4 %copy-start = (bf16[1,1792,1024]{2,1,0:T(8,128)(2,1)S(1)}, bf16[1,1792,1024]{2,1,0:T(8,128)(2,1)}, u32[]{:S(2)}) copy-start(bf16[1,1792,1024]{2,1,0:T(8,128)(2,1)} %param.13) | copy-start | bytes 11010052
  7.8 8.4 %copy-start.1 = (bf16[1,1792,1024]{2,1,0:T(8,128)(2,1)S(1)}, bf16[1,1792,1024]{2,1,0:T(8,128)(2,1)}, u32[]{:S(2)}) copy-start(bf16[1,1792,1024]{2,1,0:T(8,128)(2,1)} %param.14) | copy-start | bytes 11010052
  7.8 8.4 %collective-permute-start.7 = (bf16[40,1792]{1,0:T(8,128)(2,1)S(1)}, bf16[40,1792]{1,0:T(8,128)(2,1)S(1)}, u32[]{:S(2)}, u32[]{:S(2)}) collective-permute-start(bf16[40,1792]{1,0:T(8,128)(2,1)S(1)} %get-tuple-element.50), channel_id=1, source_target_pairs={{0,3},{1,2},{2,1},{3,0},{4,7},{5,6},{6,5},{7,4},{8,11},{9,10},{10,... | collective-permute-start | bytes 430088 | tf_op jit(solution)/shard_map/ppermute | solution.py:343
  12.6 9.8 %collective-permute-start.2 = (bf16[2,40,1792]{2,1,0:T(8,128)(2,1)S(1)}, bf16[2,40,1792]{2,1,0:T(8,128)(2,1)S(1)}, u32[]{:S(2)}, u32[]{:S(2)}) collective-permute-start(bf16[2,40,1792]{2,1,0:T(8,128)(2,1)S(1)} %get-tuple-element.44), channel_id=1, source_target_pairs={{0,1},{1,0},{2,3},{3,2},{4,5},{5,4},{6,7},{7,6},{8,9},{9,8},{10,11... | collective-permute-start | bytes 860168 | tf_op jit(solution)/shard_map/ppermute | solution.py:343
  13.2 14.3 %collective-permute-start.3 = (bf16[2,40,1792]{2,1,0:T(8,128)(2,1)S(1)}, bf16[2,40,1792]{2,1,0:T(8,128)(2,1)S(1)}, u32[]{:S(2)}, u32[]{:S(2)}) collective-permute-start(bf16[2,40,1792]{2,1,0:T(8,128)(2,1)S(1)} %get-tuple-element.45), channel_id=1, source_target_pairs={{0,2},{1,3},{2,0},{3,1},{4,6},{5,7},{6,4},{7,5},{8,10},{9,11},{10,... | collective-permute-start | bytes 860168 | tf_op jit(solution)/shard_map/ppermute | solution.py:343
  14.7 14.8 %collective-permute-start.4 = (bf16[2,40,1792]{2,1,0:T(8,128)(2,1)S(1)}, bf16[2,40,1792]{2,1,0:T(8,128)(2,1)S(1)}, u32[]{:S(2)}, u32[]{:S(2)}) collective-permute-start(bf16[2,40,1792]{2,1,0:T(8,128)(2,1)S(1)} %get-tuple-element.46), channel_id=1, source_target_pairs={{0,3},{1,2},{2,1},{3,0},{4,7},{5,6},{6,5},{7,4},{8,11},{9,10},{10,... | collective-permute-start | bytes 860168 | tf_op jit(solution)/shard_map/ppermute | solution.py:343
  17.6 18.0 %collective-permute-start.9 = (bf16[2,80,1024]{2,1,0:T(8,128)(2,1)S(1)}, bf16[2,80,1024]{2,1,0:T(8,128)(2,1)S(1)}, u32[]{:S(2)}, u32[]{:S(2)}) collective-permute-start(bf16[2,80,1024]{2,1,0:T(8,128)(2,1)S(1)} %get-tuple-element.52), channel_id=1, source_target_pairs={{0,1},{1,0},{2,3},{3,2},{4,5},{5,4},{6,7},{7,6},{8,9},{9,8},{10,11... | collective-permute-start | bytes 983048 | tf_op jit(solution)/shard_map/ppermute | solution.py:343
  30.9 11.8 %collective-permute-start.8 = (bf16[2,80,1024]{2,1,0:T(8,128)(2,1)S(1)}, bf16[2,80,1024]{2,1,0:T(8,128)(2,1)S(1)}, u32[]{:S(2)}, u32[]{:S(2)}) collective-permute-start(bf16[2,80,1024]{2,1,0:T(8,128)(2,1)S(1)} %get-tuple-element.57), channel_id=1, source_target_pairs={{0,1},{1,0},{2,3},{3,2},{4,5},{5,4},{6,7},{7,6},{8,9},{9,8},{10,11... | collective-permute-start | bytes 983048 | tf_op jit(solution)/shard_map/ppermute | solution.py:343
  32.9 15.7 %copy-start.3 = (f32[1,64,1]{1,2,0:T(1,128)S(1)}, f32[1,64,1]{1,2,0:T(1,128)}, u32[]{:S(2)}) copy-start(f32[1,64,1]{1,2,0:T(1,128)} %param.17) | copy-start | bytes 772
  32.9 15.7 %copy-start.4 = (f32[1,64,1]{1,2,0:T(1,128)S(1)}, f32[1,64,1]{1,2,0:T(1,128)}, u32[]{:S(2)}) copy-start(f32[1,64,1]{1,2,0:T(1,128)} %param.19) | copy-start | bytes 772
  32.9 13.2 %collective-permute-start.14 = (bf16[80,1024]{1,0:T(8,128)(2,1)S(1)}, bf16[80,1024]{1,0:T(8,128)(2,1)S(1)}, u32[]{:S(2)}, u32[]{:S(2)}) collective-permute-start(bf16[80,1024]{1,0:T(8,128)(2,1)S(1)} %get-tuple-element.61), channel_id=1, source_target_pairs={{0,1},{1,0},{2,3},{3,2},{4,5},{5,4},{6,7},{7,6},{8,9},{9,8},{10,11... | collective-permute-start | bytes 491528 | tf_op jit(solution)/shard_map/ppermute | solution.py:343
  42.8 7.2 %collective-permute-start.10 = (bf16[80,1024]{1,0:T(8,128)(2,1)S(1)}, bf16[80,1024]{1,0:T(8,128)(2,1)S(1)}, u32[]{:S(2)}, u32[]{:S(2)}) collective-permute-start(bf16[80,1024]{1,0:T(8,128)(2,1)S(1)} %fusion.4.refs_0_), channel_id=1, source_target_pairs={{0,1},{1,0},{2,3},{3,2},{4,5},{5,4},{6,7},{7,6},{8,9},{9,8},{10,11... | collective-permute-start | bytes 491528 | tf_op jit(solution)/shard_map/ppermute | solution.py:343
  46.3 8.1 %collective-permute-start.16 = (bf16[80,1024]{1,0:T(8,128)(2,1)S(1)}, bf16[80,1024]{1,0:T(8,128)(2,1)S(1)}, u32[]{:S(2)}, u32[]{:S(2)}) collective-permute-start(bf16[80,1024]{1,0:T(8,128)(2,1)S(1)} %fusion.2.refs_0_), channel_id=1, source_target_pairs={{0,1},{1,0},{2,3},{3,2},{4,5},{5,4},{6,7},{7,6},{8,9},{9,8},{10,11... | collective-permute-start | bytes 491528 | tf_op jit(solution)/shard_map/ppermute | solution.py:343
  47.0 10.0 %collective-permute-start.15 = (bf16[80,1024]{1,0:T(8,128)(2,1)S(1)}, bf16[80,1024]{1,0:T(8,128)(2,1)S(1)}, u32[]{:S(2)}, u32[]{:S(2)}) collective-permute-start(bf16[80,1024]{1,0:T(8,128)(2,1)S(1)} %multiply_convert_fusion.refs_0_), channel_id=1, source_target_pairs={{0,1},{1,0},{2,3},{3,2},{4,5},{5,4},{6,7},{7,6},{8,9},{9,8},{10,11... | collective-permute-start | bytes 491528 | tf_op jit(solution)/shard_map/ppermute | solution.py:343
  50.9 9.4 %collective-permute-start.11 = (bf16[40,1792]{1,0:T(8,128)(2,1)S(1)}, bf16[40,1792]{1,0:T(8,128)(2,1)S(1)}, u32[]{:S(2)}, u32[]{:S(2)}) collective-permute-start(bf16[40,1792]{1,0:T(8,128)(2,1)S(1)} %get-tuple-element.69), channel_id=1, source_target_pairs={{0,2},{1,3},{2,0},{3,1},{4,6},{5,7},{6,4},{7,5},{8,10},{9,11},{10,... | collective-permute-start | bytes 430088 | tf_op jit(solution)/shard_map/ppermute | solution.py:343
  52.4 9.4 %collective-permute-start.12 = (bf16[40,1792]{1,0:T(8,128)(2,1)S(1)}, bf16[40,1792]{1,0:T(8,128)(2,1)S(1)}, u32[]{:S(2)}, u32[]{:S(2)}) collective-permute-start(bf16[40,1792]{1,0:T(8,128)(2,1)S(1)} %get-tuple-element.70), channel_id=1, source_target_pairs={{0,3},{1,2},{2,1},{3,0},{4,7},{5,6},{6,5},{7,4},{8,11},{9,10},{10,... | collective-permute-start | bytes 430088 | tf_op jit(solution)/shard_map/ppermute | solution.py:343
  52.9 10.2 %collective-permute-start.13 = (bf16[40,1792]{1,0:T(8,128)(2,1)S(1)}, bf16[40,1792]{1,0:T(8,128)(2,1)S(1)}, u32[]{:S(2)}, u32[]{:S(2)}) collective-permute-start(bf16[40,1792]{1,0:T(8,128)(2,1)S(1)} %get-tuple-element.72), channel_id=1, source_target_pairs={{0,1},{1,0},{2,3},{3,2},{4,5},{5,4},{6,7},{7,6},{8,9},{9,8},{10,11... | collective-permute-start | bytes 430088 | tf_op jit(solution)/shard_map/ppermute | solution.py:343
  58.3 7.1 %collective-permute-start.17 = (bf16[40,1792]{1,0:T(8,128)(2,1)S(1)}, bf16[40,1792]{1,0:T(8,128)(2,1)S(1)}, u32[]{:S(2)}, u32[]{:S(2)}) collective-permute-start(bf16[40,1792]{1,0:T(8,128)(2,1)S(1)} %get-tuple-element.80), channel_id=1, source_target_pairs={{0,2},{1,3},{2,0},{3,1},{4,6},{5,7},{6,4},{7,5},{8,10},{9,11},{10,... | collective-permute-start | bytes 430088 | tf_op jit(solution)/shard_map/ppermute | solution.py:343
  59.8 7.6 %collective-permute-start.18 = (bf16[40,1792]{1,0:T(8,128)(2,1)S(1)}, bf16[40,1792]{1,0:T(8,128)(2,1)S(1)}, u32[]{:S(2)}, u32[]{:S(2)}) collective-permute-start(bf16[40,1792]{1,0:T(8,128)(2,1)S(1)} %get-tuple-element.81), channel_id=1, source_target_pairs={{0,3},{1,2},{2,1},{3,0},{4,7},{5,6},{6,5},{7,4},{8,11},{9,10},{10,... | collective-permute-start | bytes 430088 | tf_op jit(solution)/shard_map/ppermute | solution.py:343
  60.3 8.5 %collective-permute-start.19 = (bf16[40,1792]{1,0:T(8,128)(2,1)S(1)}, bf16[40,1792]{1,0:T(8,128)(2,1)S(1)}, u32[]{:S(2)}, u32[]{:S(2)}) collective-permute-start(bf16[40,1792]{1,0:T(8,128)(2,1)S(1)} %get-tuple-element.83), channel_id=1, source_target_pairs={{0,1},{1,0},{2,3},{3,2},{4,5},{5,4},{6,7},{7,6},{8,9},{9,8},{10,11... | collective-permute-start | bytes 430088 | tf_op jit(solution)/shard_map/ppermute | solution.py:343
  (1 other events, 2.1 us)

commit v5 on v4

--- a/solution.py
+++ b/solution.py
@@ -222,41 +222,48 @@
     )
 
 
-def back_kernel(group, first, *refs):
-    gs, (mat, *rest) = refs[:group], refs[group:]
-    outs = rest if first else rest[1:]
+def back_first_kernel(group, *refs):
+    gs, (gate, up, out) = refs[:group], refs[group:]
     rows = jnp.concatenate([g[...] for g in gs], axis=0)
-    width = mat.shape[0]
+    width, hidden = gate.shape
+    more = rows.shape[1] - hidden
     tile = tile_of(width)
     for at in range(0, width, tile):
-        acc = dot_nt(mat[at : at + tile, :], rows)
-        if first:
-            outs[0][at : at + tile, :] = acc
-        else:
-            total = (acc + rest[0][at : at + tile, :]).T
-            put_blocks(total.astype(BF16), group, outs, at, tile)
-
-
-def back_half(gs, mat):
+        acc = dot_nt(gate[at : at + tile, :], rows[:, :hidden])
+        out[at : at + tile, :] = acc + dot_nt(up[at : at + tile, :more], rows[:, hidden:])
+
+
+def back_first(gs, gate, up):
     group = len(gs)
-    width, hidden = mat.shape
+    width = gate.shape[0]
     rows = gs[0].shape[0] * group
     return kernel_call(
-        functools.partial(back_kernel, group, True),
+        functools.partial(back_first_kernel, group),
         (jax.ShapeDtypeStruct((width, rows), F32),),
-        (*gs, mat),
-        2 * rows * hidden * width,
+        (*gs, gate, up),
+        2 * rows * gs[0].shape[1] * width,
     )[0]
 
 
-def back_rows(gs, mat, half):
+def back_last_kernel(group, *refs):
+    gs, (up, begun, *outs) = refs[:group], refs[group:]
+    rows = jnp.concatenate([g[...] for g in gs], axis=0)
+    width, hidden = up.shape
+    start = hidden - rows.shape[1]
+    tile = tile_of(width)
+    for at in range(0, width, tile):
+        acc = dot_nt(up[at : at + tile, start:], rows) + begun[at : at + tile, :]
+        put_blocks(acc.T.astype(BF16), group, outs, at, tile)
+
+
+def back_last(gs, up, begun):
     group = len(gs)
-    width, hidden = mat.shape
-    return kernel_call(
-        functools.partial(back_kernel, group, False),
+    width = up.shape[0]
+    return kernel_call(
+        functools.partial(back_last_kernel, group),
         (like((CAP, width)),) * (2 * group),
-        (*gs, mat, half),
-        4 * group * CAP * hidden * width,
+        (*gs, up, begun),
+        4 * group * CAP * gs[0].shape[1] * width,
     )
 
 
@@ -391,10 +398,12 @@
     grad_hidden = summed(g_parts[0], g_sent)
     sig = jax.nn.sigmoid(back[0])
     grad_gate = grad_hidden * back[1] * sig * (1.0 + back[0] * (1.0 - sig))
-    grad_up = after(grad_hidden, grad_gate) * (back[0] * sig)
-    grad_gate, grad_up = grad_gate.astype(BF16), grad_up.astype(BF16)
-    gate_sent = sent([grad_gate] * (group - 1))
-    up_sent = sent([grad_up] * (group - 1))
+    grad_up = grad_hidden * (back[0] * sig)
+    cut = grad_up.shape[1] // 4
+    begun = jnp.concatenate([grad_gate, grad_up[:, :cut]], axis=1).astype(BF16)
+    rest = (after(grad_hidden, begun) * (back[0] * sig))[:, cut:].astype(BF16)
+    begun_sent = sent([begun] * (group - 1))
+    rest_sent = sent([rest] * (group - 1))
 
     def returned(blocks):
         rows = sent(blocks[1:])
@@ -406,8 +415,8 @@
     hidden_sent = after(hidden_sent, fwd_pick)
     fwd_rows = down_rows([hidden, *hidden_sent], down)
     fwd_same, fwd_other = returned(fwd_rows)
-    half = back_half([grad_gate, *after(gate_sent, fwd_rows)], gate)
-    bwd_same, bwd_other = returned(back_rows([grad_up, *after(up_sent, half)], up, half))
+    total = back_first([begun, *after(begun_sent, fwd_rows)], gate, up)
+    bwd_same, bwd_other = returned(back_last([rest, *after(rest_sent, total)], up, total))
     fwd_out = combine(fwd_pick, fwd_weights, section_x, fwd_same, fwd_other)
     bwd_out = combine(bwd_pick, bwd_weights, section_g, bwd_same, bwd_other)
     return (fwd_out[None], bwd_out[None])

time: 70 us -> 70 us (level)
  no operation moved by 1% of the time
where the time goes in v5:
time: 70 us; the launch traced here: 69.9 us
  waiting for transfers between devices  32.9 us (47%)
  starting transfers between devices  22.9 us (33%)
  Pallas kernels  10.6 us (15%)
  other arithmetic  2.57 us (4%)
  between operations  0.8 us (1%)
    ppermute x18, waiting for transfers between devices, to_partner(): lax.ppermute(value, 'expert', [(i, i ^ mask) for i in range(devices)])  30.3 us
    ppermute x18, starting transfers between devices, to_partner(): lax.ppermute(value, 'expert', [(i, i ^ mask) for i in range(devices)])  20.4 us
    pallas_call x9, Pallas kernels, kernel_call(): pl.pallas_call(kernel, out_shape=out_shape, in_specs=[whole] * len(inputs...  8.55 us
    ppermute x2, waiting for transfers between devices, body(): lax.ppermute(value, 'pipe', pairs + [(b, a) for a, b in pairs])  2.68 us
    ppermute x2, starting transfers between devices, body(): lax.ppermute(value, 'pipe', pairs + [(b, a) for a, b in pairs])  2.52 us
    pallas_call x2, Pallas kernels, combine(): pl.pallas_call(functools.partial(combine_kernel, group), out_shape=like(b...  2.08 us
  transfers between devices with their start and end apart: 20, of which 13 were waited for; matrix products, arithmetic and copies ran while one was open for 2% of the time, Pallas kernels for 14%

profile of v5, /device:TPU:18, one launch (start us, length us, event | category | flops | bytes accessed | tf_op | source)
XLA Modules:
  0.0 69.9 jit_solution(15721993996963710338)
XLA Ops:
  0.6 1.4 %select_bitcast_fusion.1 = (bf16[64,3584]{1,0:T(8,128)(2,1)S(1)}, bf16[64,3584]{1,0:T(8,128)(2,1)S(1)}, bf16[64,3584]{1,0:T(8,128)(2,1)S(1)}) fusion(bf16[1,64,3584]{2,1,0:T(8,128)(2,1)} %param.12, bf16[1,64,3584]{2,1,0:T(8,128)(2,1)} %param.10, pred[]{:T(512)S(6)} %eq.3, bf16[1,64,3584]{2,1,0:T(8,128)(2,1)} %param.11, pred[]{:T(512)S(6)} %lt.3), kind=kLoop, calls=%fused_computation.3 | loop fusion | flops 688128 | bytes 2752514 | tf_op jit(solution)/shard_map/jit(_where)/select_n | solution.py:362
  2.1 2.4 %collective-permute-start.1 = (bf16[64,3584]{1,0:T(8,128)(2,1)S(1)}, bf16[64,3584]{1,0:T(8,128)(2,1)S(1)}, u32[]{:S(2)}, u32[]{:S(2)}) collective-permute-start(bf16[64,3584]{1,0:T(8,128)(2,1)S(1)} %get-tuple-element.84), channel_id=1, source_target_pairs={{4,8},{12,16},{20,24},{8,4},{16,12},{24,20},{5,9},{13,17},{21,25},... | collective-permute-start | bytes 1376264 | tf_op jit(solution)/shard_map/ppermute | solution.py:366
  6.3 1.5 %collective-permute-start.6 = (bf16[40,1792]{1,0:T(8,128)(2,1)S(1)}, bf16[40,1792]{1,0:T(8,128)(2,1)S(1)}, u32[]{:S(2)}, u32[]{:S(2)}) collective-permute-start(bf16[40,1792]{1,0:T(8,128)(2,1)S(1)} %get-tuple-element.49), channel_id=1, source_target_pairs={{0,2},{1,3},{2,0},{3,1},{4,6},{5,7},{6,4},{7,5},{8,10},{9,11},{10,... | collective-permute-start | bytes 430088 | tf_op jit(solution)/shard_map/ppermute | solution.py:350
  7.8 1.4 %collective-permute-start.7 = (bf16[40,1792]{1,0:T(8,128)(2,1)S(1)}, bf16[40,1792]{1,0:T(8,128)(2,1)S(1)}, u32[]{:S(2)}, u32[]{:S(2)}) collective-permute-start(bf16[40,1792]{1,0:T(8,128)(2,1)S(1)} %get-tuple-element.50), channel_id=1, source_target_pairs={{0,3},{1,2},{2,1},{3,0},{4,7},{5,6},{6,5},{7,4},{8,11},{9,10},{10,... | collective-permute-start | bytes 430088 | tf_op jit(solution)/shard_map/ppermute | solution.py:350
  9.2 2.7 %collective-permute-done.1.refs_3_ = bf16[64,3584]{1,0:T(8,128)(2,1)S(1)} collective-permute-done((bf16[64,3584]{1,0:T(8,128)(2,1)S(1)}, bf16[64,3584]{1,0:T(8,128)(2,1)S(1)}, u32[]{:S(2)}, u32[]{:S(2)}) %collective-permute-start.1) | collective-permute-done | bytes 458784 | tf_op jit(solution)/shard_map/ppermute | solution.py:366
  13.2 1.5 %collective-permute-start.3 = (bf16[2,40,1792]{2,1,0:T(8,128)(2,1)S(1)}, bf16[2,40,1792]{2,1,0:T(8,128)(2,1)S(1)}, u32[]{:S(2)}, u32[]{:S(2)}) collective-permute-start(bf16[2,40,1792]{2,1,0:T(8,128)(2,1)S(1)} %get-tuple-element.45), channel_id=1, source_target_pairs={{0,2},{1,3},{2,0},{3,1},{4,6},{5,7},{6,4},{7,5},{8,10},{9,11},{10,... | collective-permute-start | bytes 860168 | tf_op jit(solution)/shard_map/ppermute | solution.py:350
  14.7 1.4 %collective-permute-start.4 = (bf16[2,40,1792]{2,1,0:T(8,128)(2,1)S(1)}, bf16[2,40,1792]{2,1,0:T(8,128)(2,1)S(1)}, u32[]{:S(2)}, u32[]{:S(2)}) collective-permute-start(bf16[2,40,1792]{2,1,0:T(8,128)(2,1)S(1)} %get-tuple-element.46), channel_id=1, source_target_pairs={{0,3},{1,2},{2,1},{3,0},{4,7},{5,6},{6,5},{7,4},{8,11},{9,10},{10,... | collective-permute-start | bytes 860168 | tf_op jit(solution)/shard_map/ppermute | solution.py:350
  16.2 1.4 %shard_map.115 = (bf16[2,80,1024]{2,1,0:T(8,128)(2,1)S(1)}, bf16[2,80,1024]{2,1,0:T(8,128)(2,1)S(1)}) custom-call(bf16[40,1792]{1,0:T(8,128)(2,1)S(1)} %get-tuple-element.47.refs_0_, bf16[40,1792]{1,0:T(8,128)(2,1)S(1)} %collective-permute-done.5.refs_1_, bf16[40,1792]{1,0:T(8,128)(2,1)S(1)} %collective-permute-done.6.refs_2_, ...), custom_call_target="tpu_custom_call" | custom-call | flops 1174405120 | bytes 8568832 | tf_op jit(solution)/shard_map/pallas_call | solution.py:24
  18.9 3.5 %collective-permute-done.2.refs_1_ = bf16[2,40,1792]{2,1,0:T(8,128)(2,1)S(1)} collective-permute-done((bf16[2,40,1792]{2,1,0:T(8,128)(2,1)S(1)}, bf16[2,40,1792]{2,1,0:T(8,128)(2,1)S(1)}, u32[]{:S(2)}, u32[]{:S(2)}) %collective-permute-start.2) | collective-permute-done | bytes 286752 | tf_op jit(solution)/shard_map/ppermute | solution.py:350
  22.4 5.2 %collective-permute-done.3.refs_2_ = bf16[2,40,1792]{2,1,0:T(8,128)(2,1)S(1)} collective-permute-done((bf16[2,40,1792]{2,1,0:T(8,128)(2,1)S(1)}, bf16[2,40,1792]{2,1,0:T(8,128)(2,1)S(1)}, u32[]{:S(2)}, u32[]{:S(2)}) %collective-permute-start.3) | collective-permute-done | bytes 286752 | tf_op jit(solution)/shard_map/ppermute | solution.py:350
  27.6 1.9 %collective-permute-done.4.refs_3_ = bf16[2,40,1792]{2,1,0:T(8,128)(2,1)S(1)} collective-permute-done((bf16[2,40,1792]{2,1,0:T(8,128)(2,1)S(1)}, bf16[2,40,1792]{2,1,0:T(8,128)(2,1)S(1)}, u32[]{:S(2)}, u32[]{:S(2)}) %collective-permute-start.4) | collective-permute-done | bytes 286752 | tf_op jit(solution)/shard_map/ppermute | solution.py:350
  29.5 1.4 %shard_map.116 = (bf16[2,80,1024]{2,1,0:T(8,128)(2,1)S(1)}, bf16[2,80,1024]{2,1,0:T(8,128)(2,1)S(1)}) custom-call(bf16[40,1792]{1,0:T(8,128)(2,1)S(1)} %get-tuple-element.43.refs_0_, bf16[2,40,1792]{2,1,0:T(8,128)(2,1)S(1)} %collective-permute-done.2.refs_1_, bf16[2,40,1792]{2,1,0:T(8,128)(2,1)S(1)} %collective-permute-done.3.refs_2_, ...), custom_call_target="tpu_custom_call" | custom-call | flops 1174405120 | bytes 8998912 | tf_op jit(solution)/shard_map/pallas_call | solution.py:24
  32.9 1.5 %collective-permute-start.14 = (bf16[80,1024]{1,0:T(8,128)(2,1)S(1)}, bf16[80,1024]{1,0:T(8,128)(2,1)S(1)}, u32[]{:S(2)}, u32[]{:S(2)}) collective-permute-start(bf16[80,1024]{1,0:T(8,128)(2,1)S(1)} %get-tuple-element.61), channel_id=1, source_target_pairs={{0,1},{1,0},{2,3},{3,2},{4,5},{5,4},{6,7},{7,6},{8,9},{9,8},{10,11... | collective-permute-start | bytes 491528 | tf_op jit(solution)/shard_map/ppermute | solution.py:350
  35.7 6.9 %collective-permute-done.8 = bf16[2,80,1024]{2,1,0:T(8,128)(2,1)S(1)} collective-permute-done((bf16[2,80,1024]{2,1,0:T(8,128)(2,1)S(1)}, bf16[2,80,1024]{2,1,0:T(8,128)(2,1)S(1)}, u32[]{:S(2)}, u32[]{:S(2)}) %collective-permute-start.8) | collective-permute-done | bytes 327712 | tf_op jit(solution)/shard_map/ppermute | solution.py:350
  43.4 2.7 %collective-permute-done.14 = bf16[80,1024]{1,0:T(8,128)(2,1)S(1)} collective-permute-done((bf16[80,1024]{1,0:T(8,128)(2,1)S(1)}, bf16[80,1024]{1,0:T(8,128)(2,1)S(1)}, u32[]{:S(2)}, u32[]{:S(2)}) %collective-permute-start.14) | collective-permute-done | bytes 163872 | tf_op jit(solution)/shard_map/ppermute | solution.py:350
  47.0 1.6 %collective-permute-start.15 = (bf16[80,768]{1,0:T(8,128)(2,1)S(1)}, bf16[80,768]{1,0:T(8,128)(2,1)S(1)}, u32[]{:S(2)}, u32[]{:S(2)}) collective-permute-start(bf16[80,768]{1,0:T(8,128)(2,1)S(1)} %fusion.7.refs_0_), channel_id=1, source_target_pairs={{0,1},{1,0},{2,3},{3,2},{4,5},{5,4},{6,7},{7,6},{8,9},{9,8},{10,11... | collective-permute-start | bytes 368648 | tf_op jit(solution)/shard_map/ppermute | solution.py:350
  50.9 1.5 %collective-permute-start.11 = (bf16[40,1792]{1,0:T(8,128)(2,1)S(1)}, bf16[40,1792]{1,0:T(8,128)(2,1)S(1)}, u32[]{:S(2)}, u32[]{:S(2)}) collective-permute-start(bf16[40,1792]{1,0:T(8,128)(2,1)S(1)} %get-tuple-element.69), channel_id=1, source_target_pairs={{0,2},{1,3},{2,0},{3,1},{4,6},{5,7},{6,4},{7,5},{8,10},{9,11},{10,... | collective-permute-start | bytes 430088 | tf_op jit(solution)/shard_map/ppermute | solution.py:350
  52.9 1.5 %collective-permute-start.13 = (bf16[40,1792]{1,0:T(8,128)(2,1)S(1)}, bf16[40,1792]{1,0:T(8,128)(2,1)S(1)}, u32[]{:S(2)}, u32[]{:S(2)}) collective-permute-start(bf16[40,1792]{1,0:T(8,128)(2,1)S(1)} %get-tuple-element.72), channel_id=1, source_target_pairs={{0,1},{1,0},{2,3},{3,2},{4,5},{5,4},{6,7},{7,6},{8,9},{9,8},{10,11... | collective-permute-start | bytes 430088 | tf_op jit(solution)/shard_map/ppermute | solution.py:350
  54.4 1.3 %shard_map.121.refs_3_ = f32[1792,160]{1,0:T(8,128)S(1)} custom-call(bf16[80,1280]{1,0:T(8,128)(2,1)S(1)} %pad_maximum_fusion.refs_0_, bf16[80,1280]{1,0:T(8,128)(2,1)S(1)} %collective-permute-done.16.refs_1_, bf16[1792,1024]{1,0:T(8,128)(2,1)S(1)} %bitcast.47, bf16[1792,1024]{1,0:T(8,128)(2,1)S(1)} %bitcast.43), custom_call_target="tpu_custom_call" | custom-call | flops 734003200 | bytes 8896512 | tf_op jit(solution)/shard_map/pallas_call | solution.py:24
  58.0 1.5 %collective-permute-start.17 = (bf16[40,1792]{1,0:T(8,128)(2,1)S(1)}, bf16[40,1792]{1,0:T(8,128)(2,1)S(1)}, u32[]{:S(2)}, u32[]{:S(2)}) collective-permute-start(bf16[40,1792]{1,0:T(8,128)(2,1)S(1)} %get-tuple-element.80), channel_id=1, source_target_pairs={{0,2},{1,3},{2,0},{3,1},{4,6},{5,7},{6,4},{7,5},{8,10},{9,11},{10,... | collective-permute-start | bytes 430088 | tf_op jit(solution)/shard_map/ppermute | solution.py:350
  60.1 1.5 %collective-permute-start.19 = (bf16[40,1792]{1,0:T(8,128)(2,1)S(1)}, bf16[40,1792]{1,0:T(8,128)(2,1)S(1)}, u32[]{:S(2)}, u32[]{:S(2)}) collective-permute-start(bf16[40,1792]{1,0:T(8,128)(2,1)S(1)} %get-tuple-element.83), channel_id=1, source_target_pairs={{0,1},{1,0},{2,3},{3,2},{4,5},{5,4},{6,7},{7,6},{8,9},{9,8},{10,11... | collective-permute-start | bytes 430088 | tf_op jit(solution)/shard_map/ppermute | solution.py:350
  61.6 1.6 %collective-permute-done.13.refs_6_ = bf16[40,1792]{1,0:T(8,128)(2,1)S(1)} collective-permute-done((bf16[40,1792]{1,0:T(8,128)(2,1)S(1)}, bf16[40,1792]{1,0:T(8,128)(2,1)S(1)}, u32[]{:S(2)}, u32[]{:S(2)}) %collective-permute-start.13) | collective-permute-done | bytes 143392 | tf_op jit(solution)/shard_map/ppermute | solution.py:350
  65.1 2.1 %collective-permute-done.18.refs_4_ = bf16[40,1792]{1,0:T(8,128)(2,1)S(1)} collective-permute-done((bf16[40,1792]{1,0:T(8,128)(2,1)S(1)}, bf16[40,1792]{1,0:T(8,128)(2,1)S(1)}, u32[]{:S(2)}, u32[]{:S(2)}) %collective-permute-start.18) | collective-permute-done | bytes 143392 | tf_op jit(solution)/shard_map/ppermute | solution.py:350
  67.2 1.6 %collective-permute-done.19.refs_6_ = bf16[40,1792]{1,0:T(8,128)(2,1)S(1)} collective-permute-done((bf16[40,1792]{1,0:T(8,128)(2,1)S(1)}, bf16[40,1792]{1,0:T(8,128)(2,1)S(1)}, u32[]{:S(2)}, u32[]{:S(2)}) %collective-permute-start.19) | collective-permute-done | bytes 143392 | tf_op jit(solution)/shard_map/ppermute | solution.py:350
  (46 shorter events, 17.8 us)
Async XLA Ops:
  2.0 7.2 %collective-permute-start = (bf16[64,3584]{1,0:T(8,128)(2,1)S(1)}, bf16[64,3584]{1,0:T(8,128)(2,1)S(1)}, u32[]{:S(2)}, u32[]{:S(2)}) collective-permute-start(bf16[64,3584]{1,0:T(8,128)(2,1)S(1)} %get-tuple-element.85.refs_1_), channel_id=1, source_target_pairs={{0,4},{8,12},{16,20},{24,28},{4,0},{12,8},{20,16},{28,24},{1,5},{9... | collective-permute-start | bytes 1376264 | tf_op jit(solution)/shard_map/ppermute | solution.py:366
  2.1 9.8 %collective-permute-start.1 = (bf16[64,3584]{1,0:T(8,128)(2,1)S(1)}, bf16[64,3584]{1,0:T(8,128)(2,1)S(1)}, u32[]{:S(2)}, u32[]{:S(2)}) collective-permute-start(bf16[64,3584]{1,0:T(8,128)(2,1)S(1)} %get-tuple-element.84), channel_id=1, source_target_pairs={{4,8},{12,16},{20,24},{8,4},{16,12},{24,20},{5,9},{13,17},{21,25},... | collective-permute-start | bytes 1376264 | tf_op jit(solution)/shard_map/ppermute | solution.py:366
  5.7 9.1 %collective-permute-start.5 = (bf16[40,1792]{1,0:T(8,128)(2,1)S(1)}, bf16[40,1792]{1,0:T(8,128)(2,1)S(1)}, u32[]{:S(2)}, u32[]{:S(2)}) collective-permute-start(bf16[40,1792]{1,0:T(8,128)(2,1)S(1)} %get-tuple-element.48), channel_id=1, source_target_pairs={{0,1},{1,0},{2,3},{3,2},{4,5},{5,4},{6,7},{7,6},{8,9},{9,8},{10,11... | collective-permute-start | bytes 430088 | tf_op jit(solution)/shard_map/ppermute | solution.py:350
  6.3 9.9 %collective-permute-start.6 = (bf16[40,1792]{1,0:T(8,128)(2,1)S(1)}, bf16[40,1792]{1,0:T(8,128)(2,1)S(1)}, u32[]{:S(2)}, u32[]{:S(2)}) collective-permute-start(bf16[40,1792]{1,0:T(8,128)(2,1)S(1)} %get-tuple-element.49), channel_id=1, source_target_pairs={{0,2},{1,3},{2,0},{3,1},{4,6},{5,7},{6,4},{7,5},{8,10},{9,11},{10,... | collective-permute-start | bytes 430088 | tf_op jit(solution)/shard_map/ppermute | solution.py:350
  7.8 8.4 %copy-start = (bf16[1,1792,1024]{2,1,0:T(8,128)(2,1)S(1)}, bf16[1,1792,1024]{2,1,0:T(8,128)(2,1)}, u32[]{:S(2)}) copy-start(bf16[1,1792,1024]{2,1,0:T(8,128)(2,1)} %param.14) | copy-start | bytes 11010052
  7.8 8.4 %copy-start.1 = (bf16[1,1792,1024]{2,1,0:T(8,128)(2,1)S(1)}, bf16[1,1792,1024]{2,1,0:T(8,128)(2,1)}, u32[]{:S(2)}) copy-start(bf16[1,1792,1024]{2,1,0:T(8,128)(2,1)} %param.13) | copy-start | bytes 11010052
  7.8 8.4 %collective-permute-start.7 = (bf16[40,1792]{1,0:T(8,128)(2,1)S(1)}, bf16[40,1792]{1,0:T(8,128)(2,1)S(1)}, u32[]{:S(2)}, u32[]{:S(2)}) collective-permute-start(bf16[40,1792]{1,0:T(8,128)(2,1)S(1)} %get-tuple-element.50), channel_id=1, source_target_pairs={{0,3},{1,2},{2,1},{3,0},{4,7},{5,6},{6,5},{7,4},{8,11},{9,10},{10,... | collective-permute-start | bytes 430088 | tf_op jit(solution)/shard_map/ppermute | solution.py:350
  12.6 9.8 %collective-permute-start.2 = (bf16[2,40,1792]{2,1,0:T(8,128)(2,1)S(1)}, bf16[2,40,1792]{2,1,0:T(8,128)(2,1)S(1)}, u32[]{:S(2)}, u32[]{:S(2)}) collective-permute-start(bf16[2,40,1792]{2,1,0:T(8,128)(2,1)S(1)} %get-tuple-element.44), channel_id=1, source_target_pairs={{0,1},{1,0},{2,3},{3,2},{4,5},{5,4},{6,7},{7,6},{8,9},{9,8},{10,11... | collective-permute-start | bytes 860168 | tf_op jit(solution)/shard_map/ppermute | solution.py:350
  13.2 14.3 %collective-permute-start.3 = (bf16[2,40,1792]{2,1,0:T(8,128)(2,1)S(1)}, bf16[2,40,1792]{2,1,0:T(8,128)(2,1)S(1)}, u32[]{:S(2)}, u32[]{:S(2)}) collective-permute-start(bf16[2,40,1792]{2,1,0:T(8,128)(2,1)S(1)} %get-tuple-element.45), channel_id=1, source_target_pairs={{0,2},{1,3},{2,0},{3,1},{4,6},{5,7},{6,4},{7,5},{8,10},{9,11},{10,... | collective-permute-start | bytes 860168 | tf_op jit(solution)/shard_map/ppermute | solution.py:350
  14.7 14.8 %collective-permute-start.4 = (bf16[2,40,1792]{2,1,0:T(8,128)(2,1)S(1)}, bf16[2,40,1792]{2,1,0:T(8,128)(2,1)S(1)}, u32[]{:S(2)}, u32[]{:S(2)}) collective-permute-start(bf16[2,40,1792]{2,1,0:T(8,128)(2,1)S(1)} %get-tuple-element.46), channel_id=1, source_target_pairs={{0,3},{1,2},{2,1},{3,0},{4,7},{5,6},{6,5},{7,4},{8,11},{9,10},{10,... | collective-permute-start | bytes 860168 | tf_op jit(solution)/shard_map/ppermute | solution.py:350
  17.6 18.0 %collective-permute-start.9 = (bf16[2,80,1024]{2,1,0:T(8,128)(2,1)S(1)}, bf16[2,80,1024]{2,1,0:T(8,128)(2,1)S(1)}, u32[]{:S(2)}, u32[]{:S(2)}) collective-permute-start(bf16[2,80,1024]{2,1,0:T(8,128)(2,1)S(1)} %get-tuple-element.52), channel_id=1, source_target_pairs={{0,1},{1,0},{2,3},{3,2},{4,5},{5,4},{6,7},{7,6},{8,9},{9,8},{10,11... | collective-permute-start | bytes 983048 | tf_op jit(solution)/shard_map/ppermute | solution.py:350
  30.9 11.7 %collective-permute-start.8 = (bf16[2,80,1024]{2,1,0:T(8,128)(2,1)S(1)}, bf16[2,80,1024]{2,1,0:T(8,128)(2,1)S(1)}, u32[]{:S(2)}, u32[]{:S(2)}) collective-permute-start(bf16[2,80,1024]{2,1,0:T(8,128)(2,1)S(1)} %get-tuple-element.57), channel_id=1, source_target_pairs={{0,1},{1,0},{2,3},{3,2},{4,5},{5,4},{6,7},{7,6},{8,9},{9,8},{10,11... | collective-permute-start | bytes 983048 | tf_op jit(solution)/shard_map/ppermute | solution.py:350
  32.9 15.6 %copy-start.3 = (f32[1,64,1]{1,2,0:T(1,128)S(1)}, f32[1,64,1]{1,2,0:T(1,128)}, u32[]{:S(2)}) copy-start(f32[1,64,1]{1,2,0:T(1,128)} %param.17) | copy-start | bytes 772
  32.9 15.6 %copy-start.4 = (f32[1,64,1]{1,2,0:T(1,128)S(1)}, f32[1,64,1]{1,2,0:T(1,128)}, u32[]{:S(2)}) copy-start(f32[1,64,1]{1,2,0:T(1,128)} %param.19) | copy-start | bytes 772
  32.9 13.2 %collective-permute-start.14 = (bf16[80,1024]{1,0:T(8,128)(2,1)S(1)}, bf16[80,1024]{1,0:T(8,128)(2,1)S(1)}, u32[]{:S(2)}, u32[]{:S(2)}) collective-permute-start(bf16[80,1024]{1,0:T(8,128)(2,1)S(1)} %get-tuple-element.61), channel_id=1, source_target_pairs={{0,1},{1,0},{2,3},{3,2},{4,5},{5,4},{6,7},{7,6},{8,9},{9,8},{10,11... | collective-permute-start | bytes 491528 | tf_op jit(solution)/shard_map/ppermute | solution.py:350
  42.8 7.2 %collective-permute-start.10 = (bf16[80,1024]{1,0:T(8,128)(2,1)S(1)}, bf16[80,1024]{1,0:T(8,128)(2,1)S(1)}, u32[]{:S(2)}, u32[]{:S(2)}) collective-permute-start(bf16[80,1024]{1,0:T(8,128)(2,1)S(1)} %fusion.5.refs_0_), channel_id=1, source_target_pairs={{0,1},{1,0},{2,3},{3,2},{4,5},{5,4},{6,7},{7,6},{8,9},{9,8},{10,11... | collective-permute-start | bytes 491528 | tf_op jit(solution)/shard_map/ppermute | solution.py:350
  46.4 8.1 %collective-permute-start.16 = (bf16[80,1280]{1,0:T(8,128)(2,1)S(1)}, bf16[80,1280]{1,0:T(8,128)(2,1)S(1)}, u32[]{:S(2)}, u32[]{:S(2)}) collective-permute-start(bf16[80,1280]{1,0:T(8,128)(2,1)S(1)} %pad_maximum_fusion.refs_0_), channel_id=1, source_target_pairs={{0,1},{1,0},{2,3},{3,2},{4,5},{5,4},{6,7},{7,6},{8,9},{9,8},{10,11... | collective-permute-start | bytes 614408 | tf_op jit(solution)/shard_map/ppermute | solution.py:350
  47.0 10.1 %collective-permute-start.15 = (bf16[80,768]{1,0:T(8,128)(2,1)S(1)}, bf16[80,768]{1,0:T(8,128)(2,1)S(1)}, u32[]{:S(2)}, u32[]{:S(2)}) collective-permute-start(bf16[80,768]{1,0:T(8,128)(2,1)S(1)} %fusion.7.refs_0_), channel_id=1, source_target_pairs={{0,1},{1,0},{2,3},{3,2},{4,5},{5,4},{6,7},{7,6},{8,9},{9,8},{10,11... | collective-permute-start | bytes 368648 | tf_op jit(solution)/shard_map/ppermute | solution.py:350
  50.9 9.2 %collective-permute-start.11 = (bf16[40,1792]{1,0:T(8,128)(2,1)S(1)}, bf16[40,1792]{1,0:T(8,128)(2,1)S(1)}, u32[]{:S(2)}, u32[]{:S(2)}) collective-permute-start(bf16[40,1792]{1,0:T(8,128)(2,1)S(1)} %get-tuple-element.69), channel_id=1, source_target_pairs={{0,2},{1,3},{2,0},{3,1},{4,6},{5,7},{6,4},{7,5},{8,10},{9,11},{10,... | collective-permute-start | bytes 430088 | tf_op jit(solution)/shard_map/ppermute | solution.py:350
  52.4 9.2 %collective-permute-start.12 = (bf16[40,1792]{1,0:T(8,128)(2,1)S(1)}, bf16[40,1792]{1,0:T(8,128)(2,1)S(1)}, u32[]{:S(2)}, u32[]{:S(2)}) collective-permute-start(bf16[40,1792]{1,0:T(8,128)(2,1)S(1)} %get-tuple-element.70), channel_id=1, source_target_pairs={{0,3},{1,2},{2,1},{3,0},{4,7},{5,6},{6,5},{7,4},{8,11},{9,10},{10,... | collective-permute-start | bytes 430088 | tf_op jit(solution)/shard_map/ppermute | solution.py:350
  52.9 10.2 %collective-permute-start.13 = (bf16[40,1792]{1,0:T(8,128)(2,1)S(1)}, bf16[40,1792]{1,0:T(8,128)(2,1)S(1)}, u32[]{:S(2)}, u32[]{:S(2)}) collective-permute-start(bf16[40,1792]{1,0:T(8,128)(2,1)S(1)} %get-tuple-element.72), channel_id=1, source_target_pairs={{0,1},{1,0},{2,3},{3,2},{4,5},{5,4},{6,7},{7,6},{8,9},{9,8},{10,11... | collective-permute-start | bytes 430088 | tf_op jit(solution)/shard_map/ppermute | solution.py:350
  58.0 7.0 %collective-permute-start.17 = (bf16[40,1792]{1,0:T(8,128)(2,1)S(1)}, bf16[40,1792]{1,0:T(8,128)(2,1)S(1)}, u32[]{:S(2)}, u32[]{:S(2)}) collective-permute-start(bf16[40,1792]{1,0:T(8,128)(2,1)S(1)} %get-tuple-element.80), channel_id=1, source_target_pairs={{0,2},{1,3},{2,0},{3,1},{4,6},{5,7},{6,4},{7,5},{8,10},{9,11},{10,... | collective-permute-start | bytes 430088 | tf_op jit(solution)/shard_map/ppermute | solution.py:350
  59.6 7.6 %collective-permute-start.18 = (bf16[40,1792]{1,0:T(8,128)(2,1)S(1)}, bf16[40,1792]{1,0:T(8,128)(2,1)S(1)}, u32[]{:S(2)}, u32[]{:S(2)}) collective-permute-start(bf16[40,1792]{1,0:T(8,128)(2,1)S(1)} %get-tuple-element.81), channel_id=1, source_target_pairs={{0,3},{1,2},{2,1},{3,0},{4,7},{5,6},{6,5},{7,4},{8,11},{9,10},{10,... | collective-permute-start | bytes 430088 | tf_op jit(solution)/shard_map/ppermute | solution.py:350
  60.1 8.7 %collective-permute-start.19 = (bf16[40,1792]{1,0:T(8,128)(2,1)S(1)}, bf16[40,1792]{1,0:T(8,128)(2,1)S(1)}, u32[]{:S(2)}, u32[]{:S(2)}) collective-permute-start(bf16[40,1792]{1,0:T(8,128)(2,1)S(1)} %get-tuple-element.83), channel_id=1, source_target_pairs={{0,1},{1,0},{2,3},{3,2},{4,5},{5,4},{6,7},{7,6},{8,9},{9,8},{10,11... | collective-permute-start | bytes 430088 | tf_op jit(solution)/shard_map/ppermute | solution.py:350
  (1 other events, 2.1 us)
